TPU v7x, 32 devices: a whole 2x2x4 slice. The times are simulated.
32 devices in a mesh: gx: 8 (over z, x), gy: 4 (over y, core).
Axes of the slice: x: 2, y: 2, z: 4, core: 2. Of those that a mesh axis runs over, the one named last changes fastest.
Arguments:
- velocity: float32 [3, 2048, 4, 2048], P(None, 'gx', None, 'gy'), may hold values from -6 to 6
- cut_flags: int32 [2048, 4, 2048], P('gx', None, 'gy'), may hold values 0 or 1
- redirect: int32 [2048, 4, 2048], P('gx', None, 'gy'), may hold values from 0 to 3
- share_weight: float32 [2048, 4, 2048], P('gx', None, 'gy'), may hold values from 0.2 to 0.8
- inverse_dx: float32 [2048], replicated, may hold values from 0.5 to 4.8
- inverse_dy: float32 [2048], replicated, may hold values from 0.5 to 4.8
- basis_x: bfloat16 [2048, 2048], replicated, may hold values from -0.125 to 0.125
- basis_y: bfloat16 [2048, 2048], replicated, may hold values from -0.125 to 0.125
- basis_z: float32 [4, 4], replicated, may hold values from -3 to 3
- eigen_x: float32 [2048], replicated, may hold values from 0.05 to 4
- eigen_y: float32 [2048], replicated, may hold values from 0.05 to 4
- eigen_z: float32 [4], replicated, may hold values from 0.05 to 4
Outputs:
- corrected: float32 [3, 2048, 4, 2048], P(None, 'gx', None, 'gy')
- pressure: float32 [2048, 4, 2048], P('gx', None, 'gy')
Inputs may be any that keep to these rules, and one draw needn't show every extreme that they name: `redirect`: 0 sends to the next cell along the first dimension, 1 to the previous one, 2 to the next along the second dimension, 3 to the previous one; read only where cut_flags is 1.
All inputs are finite; a program needn't handle non-finite values. No bound on the sum of `cut_flags` on one device may be relied on, other than what follows from the above.
Results may differ from a plain program's by a relative error of at most 0.0003.
Values sent between devices are 32-bit elements; how exact they have to be, the bound alone decides.
No kernel may reach another device: no remote copies, remote signals or barrier semaphores. Data moves between devices by JAX's collectives and lax.ppermute only.
A program may use at most 192 MiB of HBM per device.

v0:
```python
import jax
import jax.numpy as jnp
from jax import lax
from jax.sharding import PartitionSpec as P

ITERS = 4


time_step = 0.25
cell_shift = 0.05
cut_shift = 0.45


def extended_2(value, sides, width, wrap):
    for axis, dim in sides:
        size, length = (lax.axis_size(axis), value.shape[dim])
        up = [(i, (i + 1) % size) for i in range(size if wrap else size - 1)]
        down = [(j, i) for i, j in up]
        last = lax.slice_in_dim(value, length - width, length, axis=dim)
        leading = lax.slice_in_dim(value, 0, width, axis=dim)
        before = lax.ppermute(last, axis, up)
        after = lax.ppermute(leading, axis, down)
        value = jnp.concatenate([before, value, after], axis=dim)
    return value


def x_slope(extended, inverse):
    return 0.5 * inverse[:, None, None] * (extended[..., 2:, :, 1:-1] - extended[..., :-2, :, 1:-1])


def y_slope(extended, inverse):
    return 0.5 * inverse * (extended[..., 1:-1, :, 2:] - extended[..., 1:-1, :, :-2])


def z_slope(values):
    return 0.5 * (jnp.roll(values, -1, axis=-2) - jnp.roll(values, 1, axis=-2))


def combine_terms(values, extended, diagonal_term, face_x, face_y):
    flux_x = face_x[:, None, None] * (extended[1:, :, 1:-1] - extended[:-1, :, 1:-1])
    flux_y = face_y * (extended[1:-1, :, 1:] - extended[1:-1, :, :-1])
    plane_term = 2.0 * values - jnp.roll(values, 1, axis=1) - jnp.roll(values, -1, axis=1)
    return (
        diagonal_term * values
        + (flux_x[:-1] - flux_x[1:])
        + (flux_y[..., :-1] - flux_y[..., 1:])
        + plane_term
    )


def operate_lines(values, diagonal_term, face_x, face_y, first_block, last_block):
    beside = extended_2(values, (("gx", 2),), 1, True)
    left_edge = beside[:, :, 0]
    right_edge = beside[:, :, -1]
    edges = jnp.stack([right_edge, left_edge])
    across = extended_2(edges, (("gy", 0),), 1, False)
    left_edge = jnp.where(first_block, across[0], left_edge)
    right_edge = jnp.where(last_block, across[3], right_edge)
    widened = jnp.concatenate([left_edge[:, :, None], values, right_edge[:, :, None]], axis=2)
    extended = jnp.pad(widened, ((1, 1), (0, 0), (0, 0)))
    return combine_terms(values, extended, diagonal_term, face_x, face_y)


def to_x_lines(tile_form):
    return lax.all_to_all(tile_form, "gx", split_axis=2, concat_axis=0, tiled=True)


def precondition(x_lines, basis_x, rows_basis, basis_z, eigen_slice, eigen_z, rows_eigen):
    highest = lax.Precision.HIGHEST
    full_x, planes, columns = x_lines.shape
    spread = lax.dot_general(
        basis_x,
        x_lines.reshape(full_x, planes * columns),
        (((0,), (0,)), ((), ())),
        precision=highest,
        preferred_element_type=jnp.float32,
    )
    spread = spread.reshape(full_x, planes, columns)
    tile_form = lax.all_to_all(spread, "gx", split_axis=0, concat_axis=2, tiled=True)
    y_lines = lax.all_to_all(tile_form, "gy", split_axis=0, concat_axis=2, tiled=True)
    x_rows, planes, full_y = y_lines.shape
    along_y = jnp.dot(
        y_lines.reshape(x_rows * planes, full_y),
        rows_basis,
        precision=highest,
        preferred_element_type=jnp.float32,
    ).reshape(x_rows, planes, full_y)
    spectral = jnp.einsum("xzy,zw->xwy", along_y, basis_z, precision=highest)
    spectral = spectral / (
        eigen_slice[:, None, None] + eigen_z[None, :, None] + rows_eigen[None, None, :]
    )
    back_z = jnp.einsum("xwy,zw->xzy", spectral, basis_z, precision=highest)
    back_z = back_z.reshape(x_rows * planes, full_y)
    back_y = lax.dot_general(
        back_z,
        rows_basis,
        (((1,), (1,)), ((), ())),
        precision=highest,
        preferred_element_type=jnp.float32,
    )
    back_y = back_y.reshape(x_rows, planes, full_y)
    tile_form = lax.all_to_all(back_y, "gy", split_axis=2, concat_axis=0, tiled=True)
    x_lines = to_x_lines(tile_form)
    result = jnp.dot(
        basis_x,
        x_lines.reshape(full_x, planes * columns),
        precision=highest,
        preferred_element_type=jnp.float32,
    )
    return result.reshape(full_x, planes, columns)


def residual_inner(residual, lifted):
    return lax.psum(jnp.sum(residual * lifted), ("gx", "gy"))


def per_device(
    velocity,
    cut_flags,
    redirect,
    share_weight,
    inverse_dx,
    inverse_dy,
    basis_x,
    basis_y,
    basis_z,
    eigen_x,
    eigen_y,
    eigen_z,
):
    x_parts = lax.axis_size("gx")
    y_parts = lax.axis_size("gy")
    x_index = lax.axis_index("gx")
    y_index = lax.axis_index("gy")
    x_count = velocity.shape[1]
    y_count = velocity.shape[3]
    columns = y_count // x_parts
    inverse_x = lax.dynamic_slice_in_dim(inverse_dx, x_index * x_count, x_count)
    inverse_y = lax.dynamic_slice_in_dim(inverse_dy, y_index * y_count, y_count)
    x_rows = x_count // y_parts
    eigen_slice = lax.dynamic_slice_in_dim(eigen_x, (x_index * y_parts + y_index) * x_rows, x_rows)
    wide_x = basis_x.astype(jnp.float32)
    wide_y = basis_y.astype(jnp.float32)
    extended = extended_2(velocity, (("gx", 1), ("gy", 3)), 1, False)
    advect = (
        x_slope(extended[0][None] * extended, inverse_x)
        + y_slope(extended[1][None] * extended, inverse_y)
        + z_slope(velocity[2][None] * velocity)
    )
    flags_float = cut_flags.astype(jnp.float32)
    code = (cut_flags * (redirect + 1)).astype(jnp.float32)
    moved_part = share_weight * flags_float * advect
    stacked = jnp.concatenate([moved_part, code[None]], axis=0)
    beside_all = extended_2(stacked, (("gx", 1), ("gy", 3)), 1, False)
    shares = beside_all[:3]
    code_moved = beside_all[3]
    received = jnp.where(code_moved[:-2, :, 1:-1] == 1.0, shares[:, :-2, :, 1:-1], 0.0)
    received = received + jnp.where(code_moved[2:, :, 1:-1] == 2.0, shares[:, 2:, :, 1:-1], 0.0)
    received = received + jnp.where(code_moved[1:-1, :, :-2] == 3.0, shares[:, 1:-1, :, :-2], 0.0)
    received = received + jnp.where(code_moved[1:-1, :, 2:] == 4.0, shares[:, 1:-1, :, 2:], 0.0)
    settled = advect - moved_part + received
    predicted = velocity - time_step * settled
    predicted_ext = extended_2(predicted, (("gx", 1), ("gy", 3)), 1, False)
    source = -(
        x_slope(predicted_ext[0], inverse_x)
        + y_slope(predicted_ext[1], inverse_y)
        + z_slope(predicted[2])
    )
    diagonal_term = cell_shift + cut_shift * flags_float
    source_work, diagonal_work = (
        lax.all_to_all(source, "gx", split_axis=2, concat_axis=0, tiled=True),
        lax.all_to_all(diagonal_term, "gx", split_axis=2, concat_axis=0, tiled=True),
    )
    whole_x = jnp.pad(inverse_dx, 1)
    face_whole = whole_x[:-1] * whole_x[1:]
    column_start = y_index * y_count + x_index * columns
    column_y = lax.dynamic_slice_in_dim(jnp.pad(inverse_dy, 1), column_start, columns + 2)
    face_columns = column_y[:-1] * column_y[1:]
    first_block = x_index == 0
    last_block = x_index == x_parts - 1

    def lift(residual):
        return precondition(residual, wide_x, wide_y, basis_z, eigen_slice, eigen_z, eigen_y)

    pressure = jnp.zeros_like(source_work)
    residual = source_work
    lifted = lift(residual)
    direction = lifted
    product = residual_inner(residual, lifted)
    for iteration in range(ITERS):
        mapped = operate_lines(
            direction, diagonal_work, face_whole, face_columns, first_block, last_block
        )
        step_length = product / lax.psum(jnp.sum(direction * mapped), ("gx", "gy"))
        pressure = pressure + step_length * direction
        residual = residual - step_length * mapped
        if iteration + 1 < ITERS:
            lifted = lift(residual)
            renewed = residual_inner(residual, lifted)
            direction = lifted + renewed / product * direction
            product = renewed
    pressure = lax.all_to_all(pressure, "gx", split_axis=0, concat_axis=2, tiled=True)
    pressure_ext = extended_2(pressure, (("gx", 0), ("gy", 2)), 1, False)
    gradient = jnp.stack(
        [x_slope(pressure_ext, inverse_x), y_slope(pressure_ext, inverse_y), z_slope(pressure)]
    )
    return (predicted - gradient, pressure)


def solution(mesh):
    in_specs = (
        P(None, "gx", None, "gy"),
        P("gx", None, "gy"),
        P("gx", None, "gy"),
        P("gx", None, "gy"),
        P(),
        P(),
        P(),
        P(),
        P(),
        P(),
        P(),
        P(),
    )
    out_specs = (P(None, "gx", None, "gy"), P("gx", None, "gy"))
    return jax.shard_map(
        per_device, mesh=mesh, in_specs=in_specs, out_specs=out_specs, check_vma=False
    )
```

profile of v0, /device:TPU:9, one launch (start us, length us, event | category | flops | bytes accessed | tf_op | source)
XLA Modules:
  0.0 1937.4 jit_solution(8082093264147567119)
XLA Ops:
  200.9 51.3 %all_to_all.318 = f32[256,4,512]{0,1,2:T(4,128)S(1)} all-to-all(f32[256,4,512]{0,1,2:T(4,128)S(1)} %copy.369), channel_id=1, replica_groups=mesh['gx'=8,'gy'=4] {'gx'}, dimensions={2} | all-to-all | bytes 4194304 | tf_op jit(solution)/shard_map/all_to_all | solution.py:171
  271.9 50.6 %all_to_all.319 = f32[8,1,65536]{2,1,0:T(1,128)} all-to-all(f32[8,1,65536]{2,1,0:T(1,128)S(1)} %reshape.229), channel_id=1, replica_groups=mesh['gx'=8,'gy'=4] {'gx'}, dimensions={0} | all-to-all | bytes 4194304 | tf_op jit(solution)/shard_map/all_to_all | solution.py:79
  462.9 28.6 %all-to-all-done.5 = f32[256,4,512]{0,1,2:T(4,128)} async-done(((f32[256,4,512]{0,1,2:T(4,128)}), f32[256,4,512]{0,1,2:T(4,128)}, u32[]{:S(2)}, u32[]{:S(2)}) %all-to-all-start.5) | async-done | bytes 2097184 | tf_op jit(solution)/shard_map/all_to_all | solution.py:172
  501.2 42.6 %all-to-all-done.4 = f32[256,4,512]{0,1,2:T(4,128)S(1)} async-done(((f32[256,4,512]{0,1,2:T(4,128)}), f32[256,4,512]{0,1,2:T(4,128)S(1)}, u32[]{:S(2)}, u32[]{:S(2)}) %all-to-all-start.4) | async-done | bytes 2097184 | tf_op jit(solution)/shard_map/all_to_all | solution.py:65
  578.4 39.2 %all-reduce.6 = (f32[]{:T(128)}, f32[]{:T(128)}) all-reduce(f32[]{:T(128)} %fusion.80, f32[]{:T(128)} %multiply_reduce_fusion.5), channel_id=1, replica_groups=mesh['gx'=8,'gy'=4] {'gx','gy'}, use_global_device_ids=true, to_apply=%region_1.2 | all-reduce | flops 2 | bytes 16 | tf_op jit(solution)/shard_map/psum | solution.py:114
  645.0 51.9 %all_to_all.320 = f32[8,1,65536]{2,1,0:T(1,128)} all-to-all(f32[8,1,65536]{2,1,0:T(1,128)} %reshape.233), channel_id=1, replica_groups=mesh['gx'=8,'gy'=4] {'gx'}, dimensions={0} | all-to-all | bytes 4194304 | tf_op jit(solution)/shard_map/all_to_all | solution.py:79
  719.8 30.6 %all_to_all.321 = f32[256,4,512]{2,1,0:T(4,128)S(1)} all-to-all(f32[256,4,512]{2,1,0:T(4,128)} %copy.395), channel_id=1, replica_groups=mesh['gx'=8,'gy'=4] {'gy'}, dimensions={0} | all-to-all | bytes 4194304 | tf_op jit(solution)/shard_map/all_to_all | solution.py:80
  790.7 30.5 %all_to_all.322 = f32[4,1,131072]{2,1,0:T(1,128)} all-to-all(f32[4,1,131072]{2,1,0:T(1,128)} %reshape.235), channel_id=1, replica_groups=mesh['gx'=8,'gy'=4] {'gy'}, dimensions={0} | all-to-all | bytes 4194304 | tf_op jit(solution)/shard_map/all_to_all | solution.py:102
  844.5 50.6 %all_to_all.323 = f32[256,4,512]{0,1,2:T(4,128)S(1)} all-to-all(f32[256,4,512]{0,1,2:T(4,128)} %copy.404), channel_id=1, replica_groups=mesh['gx'=8,'gy'=4] {'gx'}, dimensions={2} | all-to-all | bytes 4194304 | tf_op jit(solution)/shard_map/all_to_all | solution.py:65
  909.5 39.8 %psum.58 = f32[]{:T(128)} all-reduce(f32[]{:T(128)} %multiply_reduce_fusion.4), channel_id=1, replica_groups=mesh['gx'=8,'gy'=4] {'gx','gy'}, use_global_device_ids=true, to_apply=%region_5.6 | all-reduce | flops 1 | bytes 8 | tf_op jit(solution)/shard_map/psum | solution.py:114
  974.4 38.2 %psum.59 = f32[]{:T(128)} all-reduce(f32[]{:T(128)} %get-tuple-element.18), channel_id=1, replica_groups=mesh['gx'=8,'gy'=4] {'gx','gy'}, use_global_device_ids=true, to_apply=%region_7.8 | all-reduce | flops 1 | bytes 8 | tf_op jit(solution)/shard_map/psum | solution.py:194
  1039.9 51.5 %all_to_all.324 = f32[8,1,65536]{2,1,0:T(1,128)} all-to-all(f32[8,1,65536]{2,1,0:T(1,128)} %reshape.237), channel_id=1, replica_groups=mesh['gx'=8,'gy'=4] {'gx'}, dimensions={0} | all-to-all | bytes 4194304 | tf_op jit(solution)/shard_map/all_to_all | solution.py:79
  1114.1 30.9 %all_to_all.325 = f32[256,4,512]{2,1,0:T(4,128)S(1)} all-to-all(f32[256,4,512]{2,1,0:T(4,128)} %copy.410), channel_id=1, replica_groups=mesh['gx'=8,'gy'=4] {'gy'}, dimensions={0} | all-to-all | bytes 4194304 | tf_op jit(solution)/shard_map/all_to_all | solution.py:80
  1185.1 30.4 %all_to_all.326 = f32[4,1,131072]{2,1,0:T(1,128)} all-to-all(f32[4,1,131072]{2,1,0:T(1,128)} %reshape.239), channel_id=1, replica_groups=mesh['gx'=8,'gy'=4] {'gy'}, dimensions={0} | all-to-all | bytes 4194304 | tf_op jit(solution)/shard_map/all_to_all | solution.py:102
  1238.6 50.8 %all_to_all.327 = f32[256,4,512]{0,1,2:T(4,128)S(1)} all-to-all(f32[256,4,512]{0,1,2:T(4,128)} %copy.419), channel_id=1, replica_groups=mesh['gx'=8,'gy'=4] {'gx'}, dimensions={2} | all-to-all | bytes 4194304 | tf_op jit(solution)/shard_map/all_to_all | solution.py:65
  1303.8 39.8 %psum.60 = f32[]{:T(128)} all-reduce(f32[]{:T(128)} %multiply_reduce_fusion.2), channel_id=1, replica_groups=mesh['gx'=8,'gy'=4] {'gx','gy'}, use_global_device_ids=true, to_apply=%region_9.10 | all-reduce | flops 1 | bytes 8 | tf_op jit(solution)/shard_map/psum | solution.py:114
  1369.5 38.2 %psum.61 = f32[]{:T(128)} all-reduce(f32[]{:T(128)} %get-tuple-element.16), channel_id=1, replica_groups=mesh['gx'=8,'gy'=4] {'gx','gy'}, use_global_device_ids=true, to_apply=%region_11.12 | all-reduce | flops 1 | bytes 8 | tf_op jit(solution)/shard_map/psum | solution.py:194
  1435.1 51.5 %all_to_all.328 = f32[8,1,65536]{2,1,0:T(1,128)} all-to-all(f32[8,1,65536]{2,1,0:T(1,128)} %reshape.241), channel_id=1, replica_groups=mesh['gx'=8,'gy'=4] {'gx'}, dimensions={0} | all-to-all | bytes 4194304 | tf_op jit(solution)/shard_map/all_to_all | solution.py:79
  1509.5 30.7 %all_to_all.329 = f32[256,4,512]{2,1,0:T(4,128)S(1)} all-to-all(f32[256,4,512]{2,1,0:T(4,128)} %copy.425), channel_id=1, replica_groups=mesh['gx'=8,'gy'=4] {'gy'}, dimensions={0} | all-to-all | bytes 4194304 | tf_op jit(solution)/shard_map/all_to_all | solution.py:80
  1580.6 30.3 %all_to_all.330 = f32[4,1,131072]{2,1,0:T(1,128)} all-to-all(f32[4,1,131072]{2,1,0:T(1,128)} %reshape.243), channel_id=1, replica_groups=mesh['gx'=8,'gy'=4] {'gy'}, dimensions={0} | all-to-all | bytes 4194304 | tf_op jit(solution)/shard_map/all_to_all | solution.py:102
  1634.2 50.6 %all_to_all.331 = f32[256,4,512]{0,1,2:T(4,128)S(1)} all-to-all(f32[256,4,512]{0,1,2:T(4,128)} %copy.434), channel_id=1, replica_groups=mesh['gx'=8,'gy'=4] {'gx'}, dimensions={2} | all-to-all | bytes 4194304 | tf_op jit(solution)/shard_map/all_to_all | solution.py:65
  1699.3 39.9 %psum.62 = f32[]{:T(128)} all-reduce(f32[]{:T(128)} %multiply_reduce_fusion), channel_id=1, replica_groups=mesh['gx'=8,'gy'=4] {'gx','gy'}, use_global_device_ids=true, to_apply=%region_13.14 | all-reduce | flops 1 | bytes 8 | tf_op jit(solution)/shard_map/psum | solution.py:114
  1765.1 38.3 %psum.63 = f32[]{:T(128)} all-reduce(f32[]{:T(128)} %fusion.52), channel_id=1, replica_groups=mesh['gx'=8,'gy'=4] {'gx','gy'}, use_global_device_ids=true, to_apply=%region_15.16 | all-reduce | flops 1 | bytes 8 | tf_op jit(solution)/shard_map/psum | solution.py:194
  1821.6 51.3 %all_to_all.332 = f32[8,1,65536]{2,1,0:T(1,128)} all-to-all(f32[8,1,65536]{2,1,0:T(1,128)S(1)} %reshape.245), channel_id=1, replica_groups=mesh['gx'=8,'gy'=4] {'gx'}, dimensions={0} | all-to-all | bytes 4194304 | tf_op jit(solution)/shard_map/all_to_all | solution.py:202
  (399 shorter events, 938.5 us)
Async XLA Ops:
  1.4 42.7 %collective-permute-start = (f32[3,1,4,512]{3,2,1,0:T(4,128)S(1)}, f32[3,1,4,512]{3,2,1,0:T(4,128)S(1)}, u32[]{:S(2)}, u32[]{:S(2)}) collective-permute-start(f32[3,1,4,512]{3,2,1,0:T(4,128)S(1)} %get-tuple-element.38), channel_id=1, source_target_pairs={{0,4},{4,8},{8,12},{12,16},{16,20},{20,24},{24,28},{1,5},{5,9},{9,... | collective-permute-start | bytes 73736 | tf_op jit(solution)/shard_map/ppermute | solution.py:21
  4.5 41.8 %collective-permute-start.1 = (f32[3,1,4,512]{3,2,1,0:T(4,128)S(1)}, f32[3,1,4,512]{3,2,1,0:T(4,128)S(1)}, u32[]{:S(2)}, u32[]{:S(2)}) collective-permute-start(f32[3,1,4,512]{3,2,1,0:T(4,128)S(1)} %get-tuple-element.39), channel_id=1, source_target_pairs={{4,0},{8,4},{12,8},{16,12},{20,16},{24,20},{28,24},{5,1},{9,5},{13... | collective-permute-start | bytes 73736 | tf_op jit(solution)/shard_map/ppermute | solution.py:22
  49.7 9.6 collective-permute-start.2
  109.5 9.0 collective-permute-start.4
  114.6 6.7 collective-permute-start.5
  125.4 7.1 collective-permute-start.6
  168.9 10.6 collective-permute-start.8
  175.1 6.5 collective-permute-start.9
  340.9 30.8 %all-to-all-start.2 = ((f32[256,4,512]{2,1,0:T(4,128)}), f32[256,4,512]{2,1,0:T(4,128)S(1)}, u32[]{:S(2)}, u32[]{:S(2)}) async-start(f32[256,4,512]{2,1,0:T(4,128)} %copy.375), calls=%async_computation.2 | async-start | bytes 4194304 | tf_op jit(solution)/shard_map/all_to_all | solution.py:80
  409.4 29.3 %all-to-all-start.3 = ((f32[4,1,131072]{2,1,0:T(1,128)}), f32[4,1,131072]{2,1,0:T(1,128)S(1)}, u32[]{:S(2)}, u32[]{:S(2)}) async-start(f32[4,1,131072]{2,1,0:T(1,128)} %reshape.231), calls=%async_computation.3 | async-start | bytes 4194304 | tf_op jit(solution)/shard_map/all_to_all | solution.py:102
  440.0 51.5 %all-to-all-start.5 = ((f32[256,4,512]{0,1,2:T(4,128)}), f32[256,4,512]{0,1,2:T(4,128)}, u32[]{:S(2)}, u32[]{:S(2)}) async-start(f32[256,4,512]{0,1,2:T(4,128)} %copy.388), calls=%async_computation.5 | async-start | bytes 4194304 | tf_op jit(solution)/shard_map/all_to_all | solution.py:172
  491.5 52.3 %all-to-all-start.4 = ((f32[256,4,512]{0,1,2:T(4,128)}), f32[256,4,512]{0,1,2:T(4,128)S(1)}, u32[]{:S(2)}, u32[]{:S(2)}) async-start(f32[256,4,512]{0,1,2:T(4,128)} %copy.384), calls=%async_computation.4 | async-start | bytes 4194304 | tf_op jit(solution)/shard_map/all_to_all | solution.py:65
  556.5 8.8 collective-permute-start.14
  559.7 7.5 collective-permute-start.13
  954.9 8.0 collective-permute-start.18
  956.3 8.5 collective-permute-start.17
  1350.0 8.0 collective-permute-start.22
  1351.5 8.5 collective-permute-start.21
  1746.6 8.0 collective-permute-start.26
  1748.1 8.5 collective-permute-start.25
  1897.1 9.4 collective-permute-start.28
  1901.3 5.5 collective-permute-start.29
  1909.2 10.7 collective-permute-start.30
  1914.3 5.6 collective-permute-start.31
  (65 other events, 1185.6 us)
where the time goes:
time: 1950 us; the launch traced here: 1940 us
  blocking collectives  917 us (47%)
  local copies, waits for them, and re-layouts  346 us (18%)
  other arithmetic  225 us (12%)
  matrix products  188 us (10%)
  waiting for transfers between devices  139 us (7%)
  starting transfers between devices  112 us (6%)
    all_to_all x4, blocking collectives, precondition(): lax.all_to_all(spread, 'gx', split_axis=0, concat_axis=2, tiled=True)  206 us
    psum x4, blocking collectives, residual_inner(): return lax.psum(jnp.sum(residual * lifted), ('gx', 'gy'))  159 us
    unnamed x135, local copies, waits for them, and re-layouts  156 us
    all_to_all x3, blocking collectives, to_x_lines(): lax.all_to_all(tile_form, 'gx', split_axis=2, concat_axis=0, tiled=True)  152 us
    psum x3, blocking collectives, per_device(): step_length = product / lax.psum(jnp.sum(direction * mapped), ('gx', 'gy'))  115 us
    all_to_all x3, blocking collectives, precondition(): lax.all_to_all(tile_form, 'gy', split_axis=0, concat_axis=2, tiled=True)  92.1 us
    all_to_all x3, blocking collectives, precondition(): lax.all_to_all(back_y, 'gy', split_axis=2, concat_axis=0, tiled=True)  91.2 us
    ppermute x16, starting transfers between devices, extended_2(): before = lax.ppermute(last, axis, up)  54.2 us
  transfers between devices with their start and end apart: 36, of which 14 were waited for; matrix products, arithmetic and copies ran while one was open for 5% of the time, Pallas kernels for 0%

commit v1 on v0

v1 whole, which is shorter than its diff:
```python
import functools

import jax
import jax.numpy as jnp
from jax import lax
from jax.experimental import pallas as pl
from jax.experimental.pallas import tpu as pltpu
from jax.sharding import PartitionSpec as P

ITERS = 4


time_step = 0.25
cell_shift = 0.05
cut_shift = 0.45
both = ("gx", "gy")
spare = 8
vmem_bytes = 56 * 1024 * 1024


def extended_2(value, sides, width, wrap):
    for axis, dim in sides:
        size, length = (lax.axis_size(axis), value.shape[dim])
        up = [(i, (i + 1) % size) for i in range(size if wrap else size - 1)]
        down = [(j, i) for i, j in up]
        last = lax.slice_in_dim(value, length - width, length, axis=dim)
        leading = lax.slice_in_dim(value, 0, width, axis=dim)
        before = lax.ppermute(last, axis, up)
        after = lax.ppermute(leading, axis, down)
        value = jnp.concatenate([before, value, after], axis=dim)
    return value


def x_slope(extended, inverse):
    return 0.5 * inverse[:, None, None] * (extended[..., 2:, :, 1:-1] - extended[..., :-2, :, 1:-1])


def y_slope(extended, inverse):
    return 0.5 * inverse * (extended[..., 1:-1, :, 2:] - extended[..., 1:-1, :, :-2])


def z_slope(values):
    return 0.5 * (jnp.roll(values, -1, axis=-2) - jnp.roll(values, 1, axis=-2))


def halves(value):
    high = value.astype(jnp.bfloat16)
    low = (value - high.astype(jnp.float32)).astype(jnp.bfloat16)
    return high, low


def params(steps=True):
    return pltpu.CompilerParams(
        dimension_semantics=("arbitrary",) if steps else None, vmem_limit_bytes=vmem_bytes
    )


def whole(shape):
    return pl.BlockSpec(shape, lambda n: (0,) * len(shape))


def mix_planes(read, mix_ref, lines, rows):
    planes = mix_ref.shape[0]
    width = lines.shape[1]
    lane = 512 if width % 512 == 0 else width
    half = planes * rows

    def strip(index, carry):
        start = pl.multiple_of(index * 16, 16)
        for left in range(0, width, lane):
            fields = [read(k, pl.ds(start, 16), pl.ds(left, lane)) for k in range(planes)]
            for m in range(planes):
                total = fields[0] * mix_ref[0, m]
                for k in range(1, planes):
                    total = total + fields[k] * mix_ref[k, m]
                high, low = halves(total)
                lines[pl.ds(m * rows + start, 16), pl.ds(left, lane)] = high
                lines[pl.ds(half + m * rows + start, 16), pl.ds(left, lane)] = low
        return carry

    lax.fori_loop(0, rows // 16, strip, 0)


def send_lines(lines, basis_ref, out_ref, rows):
    planes, parts, _, columns = out_ref.shape
    half = planes * rows
    result = jnp.dot(lines[...], basis_ref[...], preferred_element_type=jnp.float32)
    result = result[:half] + result[half:]
    for m in range(planes):
        for part in range(parts):
            out_ref[m, part] = result[m * rows : (m + 1) * rows, part * columns : (part + 1) * columns]


def start_kernel(rows, mix_ref, field_ref, basis_ref, kept_ref, out_ref, lines):
    @pl.when(pl.program_id(0) == 0)
    def _():
        pieces, planes, _, span = field_ref.shape
        for piece in range(pieces):
            kept_ref[:, :, piece * span : (piece + 1) * span] = field_ref[piece]
        mix_planes(lambda k, i, j: kept_ref[k, i, j], mix_ref, lines, rows)

    send_lines(lines, basis_ref, out_ref, rows)


def start_lines(field, basis_z, basis_y, columns):
    pieces, planes, rows, span = field.shape
    full = pieces * span
    width = min(256, full)
    parts = width // columns
    return pl.pallas_call(
        functools.partial(start_kernel, rows),
        grid=(full // width,),
        in_specs=[
            pl.BlockSpec(memory_space=pltpu.SMEM),
            whole(field.shape),
            pl.BlockSpec((full, width), lambda n: (0, n)),
        ],
        out_specs=[
            whole((planes, rows, full)),
            pl.BlockSpec((planes, parts, rows, columns), lambda n: (0, n, 0, 0)),
        ],
        out_shape=[
            jax.ShapeDtypeStruct((planes, rows, full), jnp.float32),
            jax.ShapeDtypeStruct((planes, full // columns, rows, columns), jnp.float32),
        ],
        scratch_shapes=[pltpu.VMEM((2 * planes * rows, full), jnp.bfloat16)],
        compiler_params=params(),
    )(basis_z, field, basis_y)


def column_kernel(rows, blocks, field_ref, aux_ref, ahead_ref, back_ref, along_ref, other_ref, out_ref, lines, spectral):
    step = pl.program_id(0)
    full, columns = field_ref.shape
    block = full // blocks

    @pl.when(step == 0)
    def _():
        def strip(index, carry):
            start = pl.multiple_of(index * 64, 64)
            high, low = halves(field_ref[pl.ds(start, 64), :])
            lines[pl.ds(start, 64), :columns] = high
            lines[pl.ds(start, 64), columns:] = low
            return carry

        lax.fori_loop(0, full // 64, strip, 0)

    @pl.when(step < blocks)
    def _():
        result = jnp.dot(ahead_ref[...], lines[...], preferred_element_type=jnp.float32)
        result = result[:, :columns] + result[:, columns:]
        result = result / (along_ref[...] + other_ref[...])
        high, low = halves(result)
        start = pl.multiple_of(step * block, block)
        spectral[pl.ds(start, block), :columns] = high
        spectral[pl.ds(start, block), columns:] = low

    @pl.when(step >= blocks)
    def _():
        result = jnp.dot(back_ref[...], spectral[...], preferred_element_type=jnp.float32)
        result = result[:, :columns] + result[:, columns:]
        group = block // rows
        first = (step - blocks) * group
        for part in range(group):
            out_ref[first + part, :rows, :] = result[part * rows : (part + 1) * rows]

    @pl.when(step == 2 * blocks - 1)
    def _():
        devices = full // rows
        edge = jnp.zeros((1, columns), jnp.float32)
        rest = aux_ref[2:, :]
        for part in range(devices):
            above = out_ref[part - 1, rows - 1 : rows, :] if part > 0 else edge
            below = out_ref[part + 1, 0:1, :] if part + 1 < devices else edge
            out_ref[part, rows:, :] = jnp.concatenate([above, below, rest], axis=0)


def column_lines(field, aux, basis_xt, basis_x, along, other, rows):
    full, columns = field.shape
    block = min(512, full)
    blocks = full // block
    devices = full // rows
    return pl.pallas_call(
        functools.partial(column_kernel, rows, blocks),
        grid=(2 * blocks,),
        in_specs=[
            whole(field.shape),
            whole(aux.shape),
            pl.BlockSpec((block, full), lambda n: (jnp.minimum(n, blocks - 1), 0)),
            pl.BlockSpec((block, full), lambda n: (jnp.maximum(n - blocks, 0), 0)),
            pl.BlockSpec((block, 1), lambda n: (jnp.minimum(n, blocks - 1), 0)),
            whole(other.shape),
        ],
        out_specs=whole((devices, rows + spare, columns)),
        out_shape=jax.ShapeDtypeStruct((devices, rows + spare, columns), jnp.float32),
        scratch_shapes=[
            pltpu.VMEM((full, 2 * columns), jnp.bfloat16),
            pltpu.VMEM((full, 2 * columns), jnp.bfloat16),
        ],
        compiler_params=params(),
    )(field, aux, basis_xt, basis_x, along, other)


def turn_kernel(stage, last, blocks, rows, *refs):
    refs = list(refs)
    take = lambda: refs.pop(0)
    mix_ref, got_ref, rows_ref = take(), take(), take()
    ahead_ref = None if last else take()
    diagonal_ref, low_x, high_x, low_y, high_y = take(), take(), take(), take(), take()
    if stage >= 1:
        old_z, old_edge_z = take(), take()
    if stage >= 2:
        old_v, old_edge_v, old_scalars = take(), take(), take()
    z_ref, edge_z_ref, y_ref = take(), take(), take()
    if stage >= 1:
        v_ref, edge_v_ref, scalars_ref = take(), take(), take()
    out_ref = None if last else take()
    lines, around = take(), take()
    ahead_lines = None if last else take()
    step = pl.program_id(0)
    planes, _, full = y_ref.shape
    devices, _, columns = got_ref.shape
    parts = devices // planes
    half = planes * (rows + spare)
    main = planes * rows
    width = rows_ref.shape[0]

    @pl.when(step == 0)
    def _():
        edge_rows = lax.broadcasted_iota(jnp.int32, (spare, columns), 0) < 2
        for part in range(parts):
            lanes = slice(part * columns, (part + 1) * columns)
            edges = []
            for m in range(planes):
                high, low = halves(got_ref[m * parts + part, :rows, :])
                lines[m * rows : (m + 1) * rows, lanes] = high
                lines[half + m * rows : half + (m + 1) * rows, lanes] = low
                edges.append(jnp.where(edge_rows, got_ref[m * parts + part, rows:, :], 0.0))
            high, low = halves(jnp.concatenate(edges, axis=0))
            lines[main:half, lanes] = high
            lines[half + main :, lanes] = low
        if stage >= 1:
            product = jnp.sum(jnp.sum(got_ref[:, rows + 2, :], axis=0, keepdims=True), axis=1, keepdims=True)
            image = jnp.sum(jnp.sum(got_ref[:, rows + 3, :], axis=0, keepdims=True), axis=1, keepdims=True)
            if stage >= 2:
                turn = product / old_scalars[0:1, 0:1]
                image = image - turn * turn * old_scalars[1:2, 0:1]
            else:
                turn = jnp.zeros_like(product)
            length = product / image
            kept = [product, image, length, turn]
            kept = [jnp.broadcast_to(value, (1, 128)) for value in kept]
            scalars_ref[...] = jnp.concatenate(kept + [jnp.zeros((4, 128), jnp.float32)], axis=0)

    @pl.when(step < blocks)
    def _():
        result = lax.dot_general(
            lines[...], rows_ref[...], (((1,), (1,)), ((), ())), preferred_element_type=jnp.float32
        )
        result = result[:half] + result[half:]
        lanes = pl.ds(pl.multiple_of(step * width, width), width)
        if stage >= 1:
            length = scalars_ref[2:3, 0:1]
            turn = scalars_ref[3:4, 0:1]
        for k in range(planes):
            value = result[:rows] * mix_ref[k, 0]
            edge = result[main : main + spare] * mix_ref[k, 0]
            for m in range(1, planes):
                value = value + result[m * rows : (m + 1) * rows] * mix_ref[k, m]
                edge = edge + result[main + m * spare : main + (m + 1) * spare] * mix_ref[k, m]
            if stage >= 1:
                if stage >= 2:
                    value = value + turn * old_v[k]
                    edge = edge + turn * old_edge_v[k]
                v_ref[k] = value
                edge_v_ref[k] = edge
                value = old_z[k] - length * value
                edge = old_edge_z[k] - length * edge
            z_ref[k] = value
            edge_z_ref[k] = edge
            around[k, spare : spare + rows, lanes] = value
            around[k, spare - 1 : spare, lanes] = edge[0:1]
            around[k, spare + rows : spare + rows + 1, lanes] = edge[1:2]

    @pl.when(step == blocks - 1 if last else step == blocks)
    def _():
        for k in range(planes):
            for start in range(0, rows, 8):
                value = around[k, spare + start : spare + start + 8, :]
                above = around[k, spare + start - 1 : spare + start + 7, :]
                below = around[k, spare + start + 1 : spare + start + 9, :]
                before = around[(k - 1) % planes, spare + start : spare + start + 8, :]
                after = around[(k + 1) % planes, spare + start : spare + start + 8, :]
                total = diagonal_ref[k, start : start + 8, :] * value
                total = total + (
                    low_x[start : start + 8, :] * (value - above)
                    - high_x[start : start + 8, :] * (below - value)
                )
                left = pltpu.roll(value, 1, 1)
                right = pltpu.roll(value, full - 1, 1)
                total = total + (low_y[...] * (value - left) - high_y[...] * (right - value))
                y_ref[k, start : start + 8, :] = total + (2.0 * value - before - after)
        if not last:
            mix_planes(lambda k, i, j: y_ref[k, i, j], mix_ref, ahead_lines, rows)

    if not last:

        @pl.when(step >= blocks)
        def _():
            send_lines(ahead_lines, ahead_ref, out_ref, rows)


def turn_lines(stage, last, got, operator, basis_z, basis_y, state):
    diagonal, low_x, high_x, low_y, high_y = operator
    planes, rows, full = diagonal.shape
    devices, _, columns = got.shape
    width = min(256, full)
    blocks = full // width
    parts = width // columns
    down = lambda n: jnp.minimum(n, blocks - 1)
    field = pl.BlockSpec((planes, rows, width), lambda n: (0, 0, down(n)))
    edge = pl.BlockSpec((planes, spare, width), lambda n: (0, 0, down(n)))
    scalars = whole((8, 128))
    field_shape = jax.ShapeDtypeStruct((planes, rows, full), jnp.float32)
    edge_shape = jax.ShapeDtypeStruct((planes, spare, full), jnp.float32)
    scalars_shape = jax.ShapeDtypeStruct((8, 128), jnp.float32)
    specs = [
        pl.BlockSpec(memory_space=pltpu.SMEM),
        whole(got.shape),
        pl.BlockSpec((width, full), lambda n: (down(n), 0)),
    ]
    given = [basis_z, got, basis_y]
    if not last:
        specs.append(pl.BlockSpec((full, width), lambda n: (0, jnp.maximum(n - blocks, 0))))
        given.append(basis_y)
    specs += [whole(part.shape) for part in operator]
    given += list(operator)
    if stage >= 1:
        specs += [field, edge]
        given += [state["z"], state["edge_z"]]
    if stage >= 2:
        specs += [field, edge, scalars]
        given += [state["v"], state["edge_v"], state["scalars"]]
    names = ["z", "edge_z", "y"]
    outs = [field, edge, whole((planes, rows, full))]
    shapes = [field_shape, edge_shape, field_shape]
    if stage >= 1:
        names += ["v", "edge_v", "scalars"]
        outs += [field, edge, scalars]
        shapes += [field_shape, edge_shape, scalars_shape]
    half = planes * (rows + spare)
    scratch = [
        pltpu.VMEM((2 * half, full), jnp.bfloat16),
        pltpu.VMEM((planes, rows + 2 * spare, full), jnp.float32),
    ]
    if not last:
        names.append("sent")
        outs.append(
            pl.BlockSpec((planes, parts, rows, columns), lambda n: (0, jnp.maximum(n - blocks, 0), 0, 0))
        )
        shapes.append(jax.ShapeDtypeStruct((planes, full // columns, rows, columns), jnp.float32))
        scratch.append(pltpu.VMEM((2 * planes * rows, full), jnp.bfloat16))
    results = pl.pallas_call(
        functools.partial(turn_kernel, stage, last, blocks, rows),
        grid=(blocks if last else 2 * blocks,),
        in_specs=specs,
        out_specs=outs,
        out_shape=shapes,
        scratch_shapes=scratch,
        compiler_params=params(),
    )(*given)
    return dict(zip(names, results))


def lanes_sum(value, columns):
    return jnp.sum(value.reshape(-1, value.shape[-1] // columns, columns), axis=(0, 1))


def per_device(
    velocity,
    cut_flags,
    redirect,
    share_weight,
    inverse_dx,
    inverse_dy,
    basis_x,
    basis_y,
    basis_z,
    eigen_x,
    eigen_y,
    eigen_z,
):
    x_parts = lax.axis_size("gx")
    y_parts = lax.axis_size("gy")
    devices = x_parts * y_parts
    x_index = lax.axis_index("gx")
    y_index = lax.axis_index("gy")
    own = x_index * y_parts + y_index
    x_count, planes, y_count = velocity.shape[1:]
    full_x = x_count * x_parts
    full_y = y_count * y_parts
    rows = full_x // devices
    columns = planes * full_y // devices
    column_blocks = devices // planes
    inverse_x = lax.dynamic_slice_in_dim(inverse_dx, x_index * x_count, x_count)
    inverse_y = lax.dynamic_slice_in_dim(inverse_dy, y_index * y_count, y_count)
    extended = extended_2(velocity, (("gx", 1), ("gy", 3)), 1, False)
    advect = (
        x_slope(extended[0][None] * extended, inverse_x)
        + y_slope(extended[1][None] * extended, inverse_y)
        + z_slope(velocity[2][None] * velocity)
    )
    flags_float = cut_flags.astype(jnp.float32)
    code = (cut_flags * (redirect + 1)).astype(jnp.float32)
    moved_part = share_weight * flags_float * advect
    stacked = jnp.concatenate([moved_part, code[None]], axis=0)
    beside_all = extended_2(stacked, (("gx", 1), ("gy", 3)), 1, False)
    shares = beside_all[:3]
    code_moved = beside_all[3]
    received = jnp.where(code_moved[:-2, :, 1:-1] == 1.0, shares[:, :-2, :, 1:-1], 0.0)
    received = received + jnp.where(code_moved[2:, :, 1:-1] == 2.0, shares[:, 2:, :, 1:-1], 0.0)
    received = received + jnp.where(code_moved[1:-1, :, :-2] == 3.0, shares[:, 1:-1, :, :-2], 0.0)
    received = received + jnp.where(code_moved[1:-1, :, 2:] == 4.0, shares[:, 1:-1, :, 2:], 0.0)
    settled = advect - moved_part + received
    predicted = velocity - time_step * settled
    predicted_ext = extended_2(predicted, (("gx", 1), ("gy", 3)), 1, False)
    source = -(
        x_slope(predicted_ext[0], inverse_x)
        + y_slope(predicted_ext[1], inverse_y)
        + z_slope(predicted[2])
    )
    diagonal_term = cell_shift + cut_shift * flags_float

    def to_lines(block_form):
        block_form = block_form.reshape(y_parts, rows, planes, y_count)
        block_form = block_form.transpose(0, 2, 1, 3)
        return lax.all_to_all(block_form, "gy", 0, 0, tiled=True)

    diagonal = to_lines(diagonal_term).transpose(1, 2, 0, 3).reshape(planes, rows, full_y)
    source = to_lines(source)
    whole_x = jnp.pad(inverse_dx, 1)
    face_x = lax.dynamic_slice_in_dim(whole_x[:-1] * whole_x[1:], own * rows, rows + 1)
    whole_y = jnp.pad(inverse_dy, 1)
    face_y = whole_y[:-1] * whole_y[1:]
    operator = (diagonal, face_x[:-1, None], face_x[1:, None], face_y[None, :-1], face_y[None, 1:])
    basis_xt = basis_x.T
    along = eigen_x[:, None]
    other = (
        lax.dynamic_slice_in_dim(eigen_y, (own % column_blocks) * columns, columns)
        + lax.dynamic_slice_in_dim(eigen_z, own // column_blocks, 1)
    )[None]

    def through_columns(sent, aux):
        sent = sent.reshape(devices, rows, columns)
        got = lax.all_to_all(sent, both, 0, 0, tiled=True).reshape(full_x, columns)
        got = column_lines(got, aux, basis_xt, basis_x, along, other, rows)
        return lax.all_to_all(got, both, 0, 0, tiled=True)

    residual, sent = start_lines(source, basis_z, basis_y, columns)
    got = through_columns(sent, jnp.zeros((spare, columns), jnp.float32))
    state = turn_lines(0, False, got, operator, basis_z, basis_y, {})
    direction, image, pressure = state["z"], state["y"], None
    for iteration in range(ITERS):
        final = iteration + 1 == ITERS
        if iteration > 0:
            length = state["scalars"][2, 0]
            turn = state["scalars"][3, 0]
            if iteration > 1:
                direction = old_z + turn * direction
                image = old_y + turn * image
            pressure = length * direction + (pressure if iteration > 1 else 0.0)
            residual = residual - length * image
        partial = jnp.stack(
            [lanes_sum(residual * state["z"], columns), lanes_sum(state["z"] * state["y"], columns)]
        )
        if not final:
            aux = jnp.pad(partial, ((2, spare - 4), (0, 0)))
            got = through_columns(state["sent"], aux)
            old_z, old_y = state["z"], state["y"]
            state = {**state, **turn_lines(iteration + 1, iteration + 2 == ITERS, got, operator, basis_z, basis_y, state)}
    sums = jnp.broadcast_to(jnp.pad(partial, ((0, spare - 2), (0, 0)))[None], (devices, spare, columns))
    sums = lax.all_to_all(sums, both, 0, 0, tiled=True)
    product = jnp.sum(sums[:, 0])
    turn = product / state["scalars"][0, 0]
    length = product / (jnp.sum(sums[:, 1]) - turn * turn * state["scalars"][1, 0])
    pressure = pressure + length * (state["z"] + turn * direction)
    pressure = pressure.reshape(planes, rows, y_parts, y_count).transpose(2, 0, 1, 3)
    pressure = lax.all_to_all(pressure, "gy", 0, 0, tiled=True)
    pressure = pressure.transpose(0, 2, 1, 3).reshape(x_count, planes, y_count)
    pressure_ext = extended_2(pressure, (("gx", 0), ("gy", 2)), 1, False)
    gradient = jnp.stack(
        [x_slope(pressure_ext, inverse_x), y_slope(pressure_ext, inverse_y), z_slope(pressure)]
    )
    return (predicted - gradient, pressure)


def solution(mesh):
    in_specs = (
        P(None, "gx", None, "gy"),
        P("gx", None, "gy"),
        P("gx", None, "gy"),
        P("gx", None, "gy"),
        P(),
        P(),
        P(),
        P(),
        P(),
        P(),
        P(),
        P(),
    )
    out_specs = (P(None, "gx", None, "gy"), P("gx", None, "gy"))
    return jax.shard_map(
        per_device, mesh=mesh, in_specs=in_specs, out_specs=out_specs, check_vma=False
    )
```

time: 1950 us -> 948 us (0.49)
  blocking collectives: 917 us -> 246 us
  local copies, waits for them, and re-layouts: 346 us -> 78.6 us
  matrix products: 188 us -> 0 us
  Pallas kernels: 0 us -> 169 us
  other arithmetic: 225 us -> 135 us
  waiting for transfers between devices: 139 us -> 222 us
  starting transfers between devices: 112 us -> 81.1 us
    all_to_all x15 -> x6, blocking collectives: 644 us -> 246 us  [the longest x3 178 us: through_columns(): return lax.all_to_all(got, both, 0, 0, tiled=True)]
    psum x7 -> x0, blocking collectives: 273 us -> none  [the longest x4 159 us: residual_inner(): return lax.psum(jnp.sum(residual * lifted), ('gx', 'gy'))]
    dot_general x24 -> x0, matrix products: 188 us -> none  [the longest x4 39.6 us: precondition(): lax.dot_general(basis_x, x_lines.reshape(full_x, planes * columns), (((0,...]
    pallas_call x0 -> x9, Pallas kernels: none -> 169 us  [the longest x4 93 us: turn_lines(): pl.pallas_call(functools.partial(turn_kernel, stage, last, blocks, rows),...]
    unnamed x135 -> x61, local copies, waits for them, and re-layouts: 156 us -> 26.2 us
    all_to_all x4 -> x6, waiting for transfers between devices: 117 us -> 215 us  [the longest x4 168 us: through_columns(): got = lax.all_to_all(sent, both, 0, 0, tiled=True).reshape(full_x, columns)]
    all_to_all x36 -> x0, local copies, waits for them, and re-layouts: 81.1 us -> none  [the longest x9 29.5 us: precondition(): lax.all_to_all(spread, 'gx', split_axis=0, concat_axis=2, tiled=True)]
    all_to_all x9 -> x0, other arithmetic: 75.5 us -> none  [the longest x4 34.9 us: precondition(): lax.all_to_all(back_y, 'gy', split_axis=2, concat_axis=0, tiled=True)]
  transfers between devices with their start and end apart: 36 -> 22, of which waited for: 14 -> 11; matrix products, arithmetic and copies ran while one was open for 5% -> 9% of each run, Pallas kernels for 0% -> 2%
where the time goes in v1:
time: 948 us; the launch traced here: 937 us
  blocking collectives  246 us (26%)
  waiting for transfers between devices  222 us (23%)
  Pallas kernels  169 us (18%)
  other arithmetic  135 us (14%)
  starting transfers between devices  81.1 us (9%)
  local copies, waits for them, and re-layouts  78.6 us (8%)
    all_to_all x3, blocking collectives, through_columns(): return lax.all_to_all(got, both, 0, 0, tiled=True)  178 us
    all_to_all x4, waiting for transfers between devices, through_columns(): got = lax.all_to_all(sent, both, 0, 0, tiled=True).reshape(full_x, columns)  168 us
    pallas_call x4, Pallas kernels, turn_lines(): pl.pallas_call(functools.partial(turn_kernel, stage, last, blocks, rows),...  93 us
    pallas_call x4, Pallas kernels, column_lines(): pl.pallas_call(functools.partial(column_kernel, rows, blocks), grid=(2 *...  64.7 us
    all_to_all x1, waiting for transfers between devices, through_columns(): return lax.all_to_all(got, both, 0, 0, tiled=True)  47 us
    all_to_all x1, blocking collectives, per_device(): pressure = lax.all_to_all(pressure, 'gy', 0, 0, tiled=True)  28.6 us
    ppermute x8, starting transfers between devices, extended_2(): before = lax.ppermute(last, axis, up)  26.7 us
    all_to_all x1, blocking collectives, to_lines(): return lax.all_to_all(block_form, 'gy', 0, 0, tiled=True)  26.6 us
  transfers between devices with their start and end apart: 22, of which 11 were waited for; matrix products, arithmetic and copies ran while one was open for 9% of the time, Pallas kernels for 2%

profile of v1, /device:TPU:9, one launch (start us, length us, event | category | flops | bytes accessed | tf_op | source)
XLA Modules:
  0.0 937.4 jit_solution(11834197020197489500)
XLA Ops:
  57.6 7.9 broadcast_multiply_fusion.1
  65.6 22.0 %broadcast_multiply_fusion.2 = (f32[3,256,4,512]{3,1,2,0:T(8,128)}, f32[3,256,4,512]{3,1,2,0:T(8,128)}) fusion(f32[256,4,512]{2,0,1:T(8,128)} %get-tuple-element.110, f32[3,256,3,512]{3,1,2,0:T(8,128)} %get-tuple-element.92, f32[3,256,1,512]{3,1,2,0:T(8,128)} %get-tuple-element.94, f32[3,256,1,512]{3,1,2,0:T(8,128)} %get-tuple-element.93, ...), kind=kLoop, calls=%fused_computation.34 | loop fusion | flops 17301504 | bytes 52431872 | tf_op jit(solution)/shard_map/mul | solution.py:414
  119.7 16.1 %fusion.4 = f32[3,256,4,512]{3,1,2,0:T(8,128)S(1)} fusion(f32[4,258,4,1]{3,1,2,0:T(8,128)} %copy.210, f32[4,1,4,512]{3,1,2,0:T(1,128)S(1)} %collective-permute-done.5, f32[4,1,4,512]{3,1,2,0:T(1,128)S(1)} %collective-permute-done.4, f32[1,256,4,512]{3,1,2,0:T(8,128)S(1)} %copy-done.3, f32[3,256,4,512]{3,1,2,0:T(8,128)S(1)} %bitcast.85, ...), kind=kLoop, calls=%fused_computation.6 | loop fusion | flops 36175872 | bytes 29458688 | tf_op jit(solution)/shard_map/sub | solution.py:424
  168.8 26.6 %all_to_all.60.field_ref = f32[4,4,64,512]{3,2,1,0:T(8,128)} all-to-all(f32[4,4,64,512]{3,2,1,0:T(8,128)S(1)} %bitcast.99), channel_id=1, replica_groups=mesh['gx'=8,'gy'=4] {'gy'}, dimensions={0} | all-to-all | bytes 4194304 | tf_op jit(solution)/shard_map/all_to_all | solution.py:436
  195.4 11.8 %shard_map.131 = (f32[4,64,2048]{2,1,0:T(8,128)}, f32[4,8,64,256]{3,2,1,0:T(8,128)}) custom-call(f32[4,4]{1,0:T(4,128)} %refs_0_.7, f32[4,4,64,512]{3,2,1,0:T(8,128)} %all_to_all.60.field_ref, bf16[2048,2048]{1,0:T(8,128)(2,1)} %refs_2_.7), custom_call_target="tpu_custom_call" | custom-call | tf_op jit(solution)/shard_map/pallas_call | solution.py:110
  213.1 45.7 %all-to-all-done.1 = f32[32,64,256]{2,1,0:T(8,128)} async-done(((f32[32,64,256]{2,1,0:T(8,128)}), f32[32,64,256]{2,1,0:T(8,128)}, u32[]{:S(2)}, u32[]{:S(2)}) %all-to-all-start.1) | async-done | bytes 2097184 | tf_op jit(solution)/shard_map/all_to_all | solution.py:454
  262.5 12.3 %copy.219 = bf16[2048,2048]{0,1:T(8,128)(2,1)} copy(bf16[2048,2048]{1,0:T(8,128)(2,1)} %back_ref.7) | data formatting | bytes 16777216 | tf_op args[6]
  279.4 16.1 %shard_map.132 = f32[32,72,256]{2,1,0:T(8,128)} custom-call(f32[2048,256]{1,0:T(8,128)} %bitcast.11.field_ref, f32[8,256]{1,0:T(8,128)} %broadcast_in_dim.64.aux_ref, bf16[2048,2048]{1,0:T(8,128)(2,1)} %bitcast.80, bf16[2048,2048]{1,0:T(8,128)(2,1)} %back_ref.7, f32[2048,1]{1,0:T(8,128)} %copy.220.along_ref, f32[1,256]{1,0:T(1,128)} %bitcast.117), custom_call_target="tpu_custom_call" | custom-call | tf_op jit(solution)/shard_map/pallas_call | solution.py:182
  308.6 47.0 %all-to-all-done.2.refs_1_ = f32[32,72,256]{2,1,0:T(8,128)S(1)} async-done(((f32[32,72,256]{2,1,0:T(8,128)}), f32[32,72,256]{2,1,0:T(8,128)S(1)}, u32[]{:S(2)}, u32[]{:S(2)}) %all-to-all-start.2) | async-done | bytes 2359328 | tf_op jit(solution)/shard_map/all_to_all | solution.py:456
  357.0 24.4 %shard_map.133 = (f32[4,64,2048]{2,1,0:T(8,128)}, f32[4,8,2048]{2,1,0:T(8,128)}, f32[4,64,2048]{2,1,0:T(8,128)}, f32[4,8,64,256]{3,2,1,0:T(8,128)}) custom-call(f32[4,4]{1,0:T(4,128)} %refs_0_.7, f32[32,72,256]{2,1,0:T(8,128)} %copy-done.10, bf16[2048,2048]{1,0:T(8,128)(2,1)} %refs_2_.7, bf16[2048,2048]{1,0:T(8,128)(2,1)} %refs_2_.7, ...), custom_call_target="tpu_custom_call" | custom-call | tf_op jit(solution)/shard_map/pallas_call | solution.py:362
  391.0 43.7 %all-to-all-done.4 = f32[32,64,256]{2,1,0:T(8,128)} async-done(((f32[32,64,256]{2,1,0:T(8,128)}), f32[32,64,256]{2,1,0:T(8,128)}, u32[]{:S(2)}, u32[]{:S(2)}) %all-to-all-start.4) | async-done | bytes 2097184 | tf_op jit(solution)/shard_map/all_to_all | solution.py:454
  434.7 16.2 %shard_map.134 = f32[32,72,256]{2,1,0:T(8,128)} custom-call(f32[2048,256]{1,0:T(8,128)} %bitcast.24.field_ref, f32[8,256]{1,0:T(8,128)} %select_maximum_fusion.3.aux_ref, bf16[2048,2048]{1,0:T(8,128)(2,1)} %bitcast.81, bf16[2048,2048]{1,0:T(8,128)(2,1)} %back_ref.7, f32[2048,1]{1,0:T(8,128)} %copy.220.along_ref, f32[1,256]{1,0:T(1,128)} %bitcast.118), custom_call_target="tpu_custom_call" | custom-call | tf_op jit(solution)/shard_map/pallas_call | solution.py:182
  450.9 59.5 %all_to_all.61.refs_1_ = f32[32,72,256]{2,1,0:T(8,128)} all-to-all(f32[32,72,256]{2,1,0:T(8,128)} %shard_map.134), channel_id=1, replica_groups=mesh['gx'=8,'gy'=4] {'gx','gy'}, dimensions={0} | all-to-all | bytes 4718592 | tf_op jit(solution)/shard_map/all_to_all | solution.py:456
  510.4 25.5 %shard_map.135 = (f32[4,64,2048]{2,1,0:T(8,128)}, f32[4,8,2048]{2,1,0:T(8,128)}, f32[4,64,2048]{2,1,0:T(8,128)}, f32[4,64,2048]{2,1,0:T(8,128)}, f32[4,8,2048]{2...) custom-call(f32[4,4]{1,0:T(4,128)} %refs_0_.7, f32[32,72,256]{2,1,0:T(8,128)} %all_to_all.61.refs_1_, ...), custom_call_target="tpu_custom_call" | custom-call | tf_op jit(solution)/shard_map/pallas_call | solution.py:362
  549.3 39.4 %all-to-all-done.6 = f32[32,64,256]{2,1,0:T(8,128)} async-done(((f32[32,64,256]{2,1,0:T(8,128)}), f32[32,64,256]{2,1,0:T(8,128)}, u32[]{:S(2)}, u32[]{:S(2)}) %all-to-all-start.6) | async-done | bytes 2097184 | tf_op jit(solution)/shard_map/all_to_all | solution.py:454
  588.7 16.2 %shard_map.136 = f32[32,72,256]{2,1,0:T(8,128)} custom-call(f32[2048,256]{1,0:T(8,128)} %bitcast.28.field_ref, f32[8,256]{1,0:T(8,128)} %select_maximum_fusion.2.aux_ref, bf16[2048,2048]{1,0:T(8,128)(2,1)} %bitcast.82, bf16[2048,2048]{1,0:T(8,128)(2,1)} %back_ref.7, f32[2048,1]{1,0:T(8,128)} %copy.220.along_ref, f32[1,256]{1,0:T(1,128)} %bitcast.119), custom_call_target="tpu_custom_call" | custom-call | tf_op jit(solution)/shard_map/pallas_call | solution.py:182
  605.0 59.4 %all_to_all.62.refs_1_ = f32[32,72,256]{2,1,0:T(8,128)} all-to-all(f32[32,72,256]{2,1,0:T(8,128)} %shard_map.136), channel_id=1, replica_groups=mesh['gx'=8,'gy'=4] {'gx','gy'}, dimensions={0} | all-to-all | bytes 4718592 | tf_op jit(solution)/shard_map/all_to_all | solution.py:456
  664.4 26.1 %shard_map.137 = (f32[4,64,2048]{2,1,0:T(8,128)}, f32[4,8,2048]{2,1,0:T(8,128)}, f32[4,64,2048]{2,1,0:T(8,128)}, f32[4,64,2048]{2,1,0:T(8,128)}, f32[4,8,2048]{2...) custom-call(f32[4,4]{1,0:T(4,128)} %refs_0_.7, f32[32,72,256]{2,1,0:T(8,128)} %all_to_all.62.refs_1_, ...), custom_call_target="tpu_custom_call" | custom-call | tf_op jit(solution)/shard_map/pallas_call | solution.py:362
  703.8 39.4 %all-to-all-done.8 = f32[32,64,256]{2,1,0:T(8,128)} async-done(((f32[32,64,256]{2,1,0:T(8,128)}), f32[32,64,256]{2,1,0:T(8,128)}, u32[]{:S(2)}, u32[]{:S(2)}) %all-to-all-start.8) | async-done | bytes 2097184 | tf_op jit(solution)/shard_map/all_to_all | solution.py:454
  743.2 16.1 %shard_map.138 = f32[32,72,256]{2,1,0:T(8,128)} custom-call(f32[2048,256]{1,0:T(8,128)} %bitcast.33.field_ref, f32[8,256]{1,0:T(8,128)} %select_maximum_fusion.1.aux_ref, bf16[2048,2048]{1,0:T(8,128)(2,1)} %bitcast.83, bf16[2048,2048]{1,0:T(8,128)(2,1)} %back_ref.7, f32[2048,1]{1,0:T(8,128)} %copy.220.along_ref, f32[1,256]{1,0:T(1,128)} %bitcast.120), custom_call_target="tpu_custom_call" | custom-call | tf_op jit(solution)/shard_map/pallas_call | solution.py:182
  759.3 59.5 %all_to_all.63.refs_1_ = f32[32,72,256]{2,1,0:T(8,128)} all-to-all(f32[32,72,256]{2,1,0:T(8,128)} %shard_map.138), channel_id=1, replica_groups=mesh['gx'=8,'gy'=4] {'gx','gy'}, dimensions={0} | all-to-all | bytes 4718592 | tf_op jit(solution)/shard_map/all_to_all | solution.py:456
  818.8 17.0 %shard_map.139 = (f32[4,64,2048]{2,1,0:T(8,128)}, f32[4,8,2048]{2,1,0:T(8,128)}, f32[4,64,2048]{2,1,0:T(8,128)}, f32[4,64,2048]{2,1,0:T(8,128)}, f32[4,8,2048]{2,1,0:T(8,128)}, /*index=5*/f32[8,128]{1,0:T(8,128)}) custom-call(f32[4,4]{1,0:T(4,128)} %refs_0_.7, f32[32,72,256]{2,1,0:T(8,128)} %all_to_all.63.refs_1_, bf16[2048,2048]{1,0:T(8,128)(2,1)} %refs_2_.7, ...), custom_call_target="tpu_custom_call" | custom-call | tf_op jit(solution)/shard_map/pallas_call | solution.py:362
  844.4 12.8 %all_to_all.64 = f32[32,8,256]{2,1,0:T(8,128)S(1)} all-to-all(f32[32,8,256]{2,1,0:T(8,128)S(1)} %broadcast_in_dim.71), channel_id=1, replica_groups=mesh['gx'=8,'gy'=4] {'gx','gy'}, dimensions={0} | all-to-all | bytes 524288 | tf_op jit(solution)/shard_map/all_to_all | solution.py:481
  868.9 28.6 %all_to_all.65 = f32[4,4,64,512]{3,2,1,0:T(8,128)S(1)} all-to-all(f32[4,4,64,512]{3,2,1,0:T(8,128)S(1)} %bitcast.100), channel_id=1, replica_groups=mesh['gx'=8,'gy'=4] {'gy'}, dimensions={0} | all-to-all | bytes 4194304 | tf_op jit(solution)/shard_map/all_to_all | solution.py:487
  (196 shorter events, 243.2 us)
Async XLA Ops:
  1.4 32.1 %collective-permute-start = (f32[3,1,4,512]{3,1,2,0:T(1,128)S(1)}, f32[3,1,4,512]{3,1,2,0:T(1,128)S(1)}, u32[]{:S(2)}, u32[]{:S(2)}) collective-permute-start(f32[3,1,4,512]{3,1,2,0:T(1,128)S(1)} %copy.194), channel_id=1, source_target_pairs={{0,4},{4,8},{8,12},{12,16},{16,20},{20,24},{24,28},{1,5},{5,9},{9,... | collective-permute-start | bytes 73736 | tf_op jit(solution)/shard_map/ppermute | solution.py:28
  4.6 29.0 %collective-permute-start.1 = (f32[3,1,4,512]{3,1,2,0:T(1,128)S(1)}, f32[3,1,4,512]{3,1,2,0:T(1,128)S(1)}, u32[]{:S(2)}, u32[]{:S(2)}) collective-permute-start(f32[3,1,4,512]{3,1,2,0:T(1,128)S(1)} %copy.195), channel_id=1, source_target_pairs={{4,0},{8,4},{12,8},{16,12},{20,16},{24,20},{28,24},{5,1},{9,5},{13... | collective-permute-start | bytes 73736 | tf_op jit(solution)/shard_map/ppermute | solution.py:29
  36.8 7.5 collective-permute-start.2
  41.7 5.1 collective-permute-start.3
  65.6 22.0 %copy-start.2 = (f32[1,256,4,512]{3,1,2,0:T(8,128)S(1)}, f32[1,256,4,512]{3,1,2,0:T(8,128)}, u32[]{:S(2)}) copy-start(f32[1,256,4,512]{3,1,2,0:T(8,128)} %fusion.32) | copy-start | bytes 6291460
  88.8 6.3 collective-permute-start.4
  91.1 5.4 collective-permute-start.5
  102.0 7.0 collective-permute-start.6
  106.8 5.1 collective-permute-start.7
  136.0 8.6 collective-permute-start.8
  140.5 4.6 collective-permute-start.9
  149.5 9.4 %collective-permute-start.10 = (f32[3,258,4,1]{1,2,3,0:T(4,128)S(1)}, f32[3,258,4,1]{1,2,3,0:T(4,128)S(1)}, u32[]{:S(2)}, u32[]{:S(2)}) collective-permute-start(f32[3,258,4,1]{1,2,3,0:T(4,128)S(1)} %copy.214), channel_id=1, source_target_pairs={{0,1},{1,2},{2,3},{4,5},{5,6},{6,7},{8,9},{9,10},{10,11},{12,13},{... | collective-permute-start | bytes 37160 | tf_op jit(solution)/shard_map/ppermute | solution.py:28
  155.8 5.1 collective-permute-start.11
  207.2 51.6 %all-to-all-start.1 = ((f32[32,64,256]{2,1,0:T(8,128)}), f32[32,64,256]{2,1,0:T(8,128)}, u32[]{:S(2)}, u32[]{:S(2)}) async-start(f32[32,64,256]{2,1,0:T(8,128)} %bitcast.108), calls=%async_computation.1 | async-start | bytes 4194304 | tf_op jit(solution)/shard_map/all_to_all | solution.py:454
  258.8 36.7 %all-to-all-start.3 = ((f32[4,4,64,512]{3,2,1,0:T(8,128)}), f32[4,4,64,512]{3,2,1,0:T(8,128)S(1)}, u32[]{:S(2)}, u32[]{:S(2)}) async-start(f32[4,4,64,512]{3,2,1,0:T(8,128)} %copy.221), calls=%async_computation.3 | async-start | bytes 4194304 | tf_op jit(solution)/shard_map/all_to_all | solution.py:436
  296.9 58.6 %all-to-all-start.2 = ((f32[32,72,256]{2,1,0:T(8,128)}), f32[32,72,256]{2,1,0:T(8,128)S(1)}, u32[]{:S(2)}, u32[]{:S(2)}) async-start(f32[32,72,256]{2,1,0:T(8,128)} %shard_map.132), calls=%async_computation.2 | async-start | bytes 4718592 | tf_op jit(solution)/shard_map/all_to_all | solution.py:456
  381.4 53.3 %all-to-all-start.4 = ((f32[32,64,256]{2,1,0:T(8,128)}), f32[32,64,256]{2,1,0:T(8,128)}, u32[]{:S(2)}, u32[]{:S(2)}) async-start(f32[32,64,256]{2,1,0:T(8,128)} %bitcast.107), calls=%async_computation.4 | async-start | bytes 4194304 | tf_op jit(solution)/shard_map/all_to_all | solution.py:454
  535.8 52.9 %all-to-all-start.6 = ((f32[32,64,256]{2,1,0:T(8,128)}), f32[32,64,256]{2,1,0:T(8,128)}, u32[]{:S(2)}, u32[]{:S(2)}) async-start(f32[32,64,256]{2,1,0:T(8,128)} %bitcast.106), calls=%async_computation.6 | async-start | bytes 4194304 | tf_op jit(solution)/shard_map/all_to_all | solution.py:454
  690.5 52.7 %all-to-all-start.8 = ((f32[32,64,256]{2,1,0:T(8,128)}), f32[32,64,256]{2,1,0:T(8,128)}, u32[]{:S(2)}, u32[]{:S(2)}) async-start(f32[32,64,256]{2,1,0:T(8,128)} %bitcast.105), calls=%async_computation.8 | async-start | bytes 4194304 | tf_op jit(solution)/shard_map/all_to_all | solution.py:454
  818.8 18.5 %copy-start.7 = (f32[4,64,2048]{2,1,0:T(8,128)S(1)}, f32[4,64,2048]{2,1,0:T(8,128)}, u32[]{:S(2)}) copy-start(f32[4,64,2048]{2,1,0:T(8,128)} %get-tuple-element.68) | copy-start | bytes 6291460
  899.8 6.3 collective-permute-start.12
  902.9 5.3 collective-permute-start.13
  908.7 13.5 %collective-permute-start.14 = (f32[258,4,1]{0,1,2:T(4,128)S(1)}, f32[258,4,1]{0,1,2:T(4,128)S(1)}, u32[]{:S(2)}, u32[]{:S(2)}) collective-permute-start(f32[258,4,1]{0,1,2:T(4,128)S(1)} %copy.238), channel_id=1, source_target_pairs={{1,0},{2,1},{3,2},{5,4},{6,5},{7,6},{9,8},{10,9},{11,10},{13,12},{... | collective-permute-start | bytes 12392 | tf_op jit(solution)/shard_map/ppermute | solution.py:29
  913.3 9.1 collective-permute-start.15
  (27 other events, 164.7 us)

commit v2 on v1

--- a/solution.py
+++ b/solution.py
@@ -16,31 +16,6 @@
 both = ("gx", "gy")
 spare = 8
 vmem_bytes = 56 * 1024 * 1024
-
-
-def extended_2(value, sides, width, wrap):
-    for axis, dim in sides:
-        size, length = (lax.axis_size(axis), value.shape[dim])
-        up = [(i, (i + 1) % size) for i in range(size if wrap else size - 1)]
-        down = [(j, i) for i, j in up]
-        last = lax.slice_in_dim(value, length - width, length, axis=dim)
-        leading = lax.slice_in_dim(value, 0, width, axis=dim)
-        before = lax.ppermute(last, axis, up)
-        after = lax.ppermute(leading, axis, down)
-        value = jnp.concatenate([before, value, after], axis=dim)
-    return value
-
-
-def x_slope(extended, inverse):
-    return 0.5 * inverse[:, None, None] * (extended[..., 2:, :, 1:-1] - extended[..., :-2, :, 1:-1])
-
-
-def y_slope(extended, inverse):
-    return 0.5 * inverse * (extended[..., 1:-1, :, 2:] - extended[..., 1:-1, :, :-2])
-
-
-def z_slope(values):
-    return 0.5 * (jnp.roll(values, -1, axis=-2) - jnp.roll(values, 1, axis=-2))
 
 
 def halves(value):
@@ -371,6 +346,152 @@
     return dict(zip(names, results))
 
 
+def first_kernel(
+    rows, velocity_ref, weight_ref, code_ref, above_ref, below_ref, side_ref, half_x_ref, half_y_ref,
+    source_ref, predicted_ref, fields, moved, kept, semaphores,
+):
+    planes, count, span = weight_ref.shape
+    wide = half_y_ref.shape[1]
+    pad = 16
+    copies = []
+    for channel in range(5):
+        if channel < 3:
+            main = velocity_ref.at[channel]
+        else:
+            main = weight_ref if channel == 3 else code_ref
+        target = fields.at[channel]
+        copies.append((main, target.at[:, pad : pad + count, :span]))
+        copies.append((above_ref.at[channel], target.at[:, pad - 8 : pad, :span]))
+        copies.append((below_ref.at[channel], target.at[:, pad + count : pad + count + 8, :span]))
+        copies.append((side_ref.at[channel], target.at[:, :, span:]))
+    copies = [
+        pltpu.make_async_copy(given, target, semaphores.at[index])
+        for index, (given, target) in enumerate(copies)
+    ]
+    for copy in copies:
+        copy.start()
+    for copy in copies:
+        copy.wait()
+    tiles = count // 8 + 2
+    half_y = half_y_ref[...]
+
+    def lane_slope(value):
+        return pltpu.roll(value, wide - 1, 1) - pltpu.roll(value, 1, 1)
+
+    def advance(index, carry):
+        k = index // tiles
+        start = pl.multiple_of(8 + (index - k * tiles) * 8, 8)
+        window = pl.ds(pl.multiple_of(start - 8, 8), 24)
+        own = pl.ds(start, 8)
+        before = jnp.where(k == 0, planes - 1, k - 1)
+        after = jnp.where(k == planes - 1, 0, k + 1)
+        half_x = half_x_ref[own, :]
+        first = fields[0, k, window, :]
+        second = fields[1, k, own, :]
+        third_before = fields[2, before, own, :]
+        third_after = fields[2, after, own, :]
+        weight = fields[3, k, own, :]
+        for c in range(3):
+            value = first if c == 0 else fields[c, k, window, :]
+            along = first * value
+            center = value[8:16]
+            total = half_x * (pltpu.roll(along, 23, 0)[8:16] - pltpu.roll(along, 1, 0)[8:16])
+            total = total + half_y * lane_slope(second * center)
+            total = total + 0.5 * (third_after * fields[c, after, own, :] - third_before * fields[c, before, own, :])
+            share = weight * total
+            moved[c, k, own, :] = share
+            kept[c, k, own, :] = total - share
+        return carry
+
+    lax.fori_loop(0, planes * tiles, advance, 0, unroll=4)
+
+    def settle(index, carry):
+        k = index // tiles
+        start = pl.multiple_of(8 + (index - k * tiles) * 8, 8)
+        window = pl.ds(pl.multiple_of(start - 8, 8), 24)
+        own = pl.ds(start, 8)
+        code = fields[4, k, window, :]
+        inside_x = half_x_ref[own, :] > 0.0
+        inside_y = half_y > 0.0
+        for c in range(3):
+            share = moved[c, k, window, :]
+            received = pltpu.roll(jnp.where(code == 1.0, share, 0.0), 1, 0)[8:16] + pltpu.roll(jnp.where(code == 2.0, share, 0.0), 23, 0)[8:16]
+            center = share[8:16]
+            middle = code[8:16]
+            received = received + pltpu.roll(jnp.where(middle == 3.0, center, 0.0), 1, 1)
+            received = received + pltpu.roll(jnp.where(middle == 4.0, center, 0.0), wide - 1, 1)
+            result = fields[c, k, own, :] - time_step * (kept[c, k, own, :] + received)
+            if c == 0:
+                result = jnp.where(inside_x, result, 0.0)
+            if c == 1:
+                result = jnp.where(inside_y, result, 0.0)
+            kept[c, k, own, :] = result
+        return carry
+
+    lax.fori_loop(0, planes * tiles, settle, 0, unroll=4)
+    inner = count // 8
+    group = rows // 8
+
+    def collect(index, carry):
+        k = index // inner
+        tile = index - k * inner
+        start = pl.multiple_of(pad + tile * 8, 8)
+        window = pl.ds(pl.multiple_of(start - 8, 8), 24)
+        own = pl.ds(start, 8)
+        before = jnp.where(k == 0, planes - 1, k - 1)
+        after = jnp.where(k == planes - 1, 0, k + 1)
+        first = kept[0, k, window, :]
+        second = kept[1, k, own, :]
+        total = half_x_ref[own, :] * (pltpu.roll(first, 23, 0)[8:16] - pltpu.roll(first, 1, 0)[8:16])
+        total = total + half_y * lane_slope(second)
+        total = total + 0.5 * (kept[2, after, own, :] - kept[2, before, own, :])
+        target = tile // group
+        spot = pl.multiple_of((tile - target * group) * 8, 8)
+        source_ref[target, k, pl.ds(spot, 8), :] = -total[:, :span]
+        out = pl.ds(pl.multiple_of(tile * 8, 8), 8)
+        predicted_ref[0, k, out, :] = first[8:16, :span]
+        predicted_ref[1, k, out, :] = second[:, :span]
+        predicted_ref[2, k, out, :] = kept[2, k, own, :span]
+        return carry
+
+    lax.fori_loop(0, planes * inner, collect, 0, unroll=8)
+
+
+def first_step(velocity, weight, code, above, below, side, half_x, half_y, rows):
+    planes, count, span = weight.shape
+    tall, wide = half_x.shape[0], half_y.shape[1]
+    anywhere = pl.BlockSpec(memory_space=pl.ANY)
+    vector = pl.BlockSpec(memory_space=pltpu.VMEM)
+    return pl.pallas_call(
+        functools.partial(first_kernel, rows),
+        in_specs=[anywhere] * 6 + [vector] * 2,
+        out_specs=[vector] * 2,
+        out_shape=[
+            jax.ShapeDtypeStruct((count // rows, planes, rows, span), jnp.float32),
+            jax.ShapeDtypeStruct((3, planes, count, span), jnp.float32),
+        ],
+        scratch_shapes=[
+            pltpu.VMEM((5, planes, tall, wide), jnp.float32),
+            pltpu.VMEM((3, planes, tall, wide), jnp.float32),
+            pltpu.VMEM((3, planes, tall, wide), jnp.float32),
+            pltpu.SemaphoreType.DMA((20,)),
+        ],
+        compiler_params=params(False),
+    )(velocity, weight, code, above, below, side, half_x, half_y)
+
+
+def neighbours(axis, last, leading):
+    size = lax.axis_size(axis)
+    up = [(i, i + 1) for i in range(size - 1)]
+    down = [(i + 1, i) for i in range(size - 1)]
+    return lax.ppermute(last, axis, up), lax.ppermute(leading, axis, down)
+
+
+def extended_1(value, start, count, before, after):
+    padded = jnp.pad(value, (before, after))
+    return lax.dynamic_slice_in_dim(padded, start, count + before + after)
+
+
 def lanes_sum(value, columns):
     return jnp.sum(value.reshape(-1, value.shape[-1] // columns, columns), axis=(0, 1))
 
@@ -403,46 +524,45 @@
     column_blocks = devices // planes
     inverse_x = lax.dynamic_slice_in_dim(inverse_dx, x_index * x_count, x_count)
     inverse_y = lax.dynamic_slice_in_dim(inverse_dy, y_index * y_count, y_count)
-    extended = extended_2(velocity, (("gx", 1), ("gy", 3)), 1, False)
-    advect = (
-        x_slope(extended[0][None] * extended, inverse_x)
-        + y_slope(extended[1][None] * extended, inverse_y)
-        + z_slope(velocity[2][None] * velocity)
-    )
-    flags_float = cut_flags.astype(jnp.float32)
+    flags = cut_flags.astype(jnp.float32)
     code = (cut_flags * (redirect + 1)).astype(jnp.float32)
-    moved_part = share_weight * flags_float * advect
-    stacked = jnp.concatenate([moved_part, code[None]], axis=0)
-    beside_all = extended_2(stacked, (("gx", 1), ("gy", 3)), 1, False)
-    shares = beside_all[:3]
-    code_moved = beside_all[3]
-    received = jnp.where(code_moved[:-2, :, 1:-1] == 1.0, shares[:, :-2, :, 1:-1], 0.0)
-    received = received + jnp.where(code_moved[2:, :, 1:-1] == 2.0, shares[:, 2:, :, 1:-1], 0.0)
-    received = received + jnp.where(code_moved[1:-1, :, :-2] == 3.0, shares[:, 1:-1, :, :-2], 0.0)
-    received = received + jnp.where(code_moved[1:-1, :, 2:] == 4.0, shares[:, 1:-1, :, 2:], 0.0)
-    settled = advect - moved_part + received
-    predicted = velocity - time_step * settled
-    predicted_ext = extended_2(predicted, (("gx", 1), ("gy", 3)), 1, False)
-    source = -(
-        x_slope(predicted_ext[0], inverse_x)
-        + y_slope(predicted_ext[1], inverse_y)
-        + z_slope(predicted[2])
-    )
-    diagonal_term = cell_shift + cut_shift * flags_float
-
-    def to_lines(block_form):
-        block_form = block_form.reshape(y_parts, rows, planes, y_count)
-        block_form = block_form.transpose(0, 2, 1, 3)
-        return lax.all_to_all(block_form, "gy", 0, 0, tiled=True)
-
-    diagonal = to_lines(diagonal_term).transpose(1, 2, 0, 3).reshape(planes, rows, full_y)
-    source = to_lines(source)
+    weight = share_weight * flags
+    reach = 3
+
+    def edge_rows(part):
+        return jnp.concatenate([velocity[:, part], weight[None, part], code[None, part]])
+
+    above, below = neighbours("gx", edge_rows(slice(x_count - reach, None)), edge_rows(slice(0, reach)))
+    velocity = velocity.transpose(0, 2, 1, 3)
+    weight = weight.transpose(1, 0, 2)
+    code = code.transpose(1, 0, 2)
+    above = above.transpose(0, 2, 1, 3)
+    below = below.transpose(0, 2, 1, 3)
+
+    def edge_columns(part):
+        middle = jnp.concatenate([velocity[..., part], weight[None, ..., part], code[None, ..., part]])
+        return jnp.concatenate([above[..., part], middle, below[..., part]], axis=2).swapaxes(2, 3)
+
+    left, right = neighbours("gy", edge_columns(slice(y_count - reach, None)), edge_columns(slice(0, reach)))
+    side = jnp.concatenate([right, jnp.zeros((5, planes, 128 - 2 * reach, x_count + 2 * reach), jnp.float32), left], axis=2)
+    side = jnp.pad(side.swapaxes(2, 3), ((0, 0), (0, 0), (16 - reach, 16 - reach), (0, 0)))
+    above = jnp.pad(above, ((0, 0), (0, 0), (8 - reach, 0), (0, 0)))
+    below = jnp.pad(below, ((0, 0), (0, 0), (0, 8 - reach), (0, 0)))
+    half_x = 0.5 * extended_1(inverse_dx, x_index * x_count, x_count, 16, 16)[:, None]
+    half_y = 0.5 * extended_1(inverse_dy, y_index * y_count, y_count, reach, reach)
+    half_y = jnp.concatenate([half_y[reach:], jnp.zeros((128 - 2 * reach,), jnp.float32), half_y[:reach]])[None]
+    source, predicted = first_step(velocity, weight, code, above, below, side, half_x, half_y, rows)
+    diagonal = (cell_shift + cut_shift * flags).reshape(y_parts, rows, planes, y_count).transpose(0, 2, 1, 3)
+    diagonal = lax.all_to_all(diagonal, "gy", 0, 0, tiled=True)
+    source, diagonal = lax.optimization_barrier((source, diagonal))
+    source = lax.all_to_all(source, "gy", 0, 0, tiled=True)
+    source, basis_xt = lax.optimization_barrier((source, basis_x.T))
+    diagonal = diagonal.transpose(1, 2, 0, 3).reshape(planes, rows, full_y)
     whole_x = jnp.pad(inverse_dx, 1)
     face_x = lax.dynamic_slice_in_dim(whole_x[:-1] * whole_x[1:], own * rows, rows + 1)
     whole_y = jnp.pad(inverse_dy, 1)
     face_y = whole_y[:-1] * whole_y[1:]
     operator = (diagonal, face_x[:-1, None], face_x[1:, None], face_y[None, :-1], face_y[None, 1:])
-    basis_xt = basis_x.T
     along = eigen_x[:, None]
     other = (
         lax.dynamic_slice_in_dim(eigen_y, (own % column_blocks) * columns, columns)
@@ -485,12 +605,22 @@
     pressure = pressure + length * (state["z"] + turn * direction)
     pressure = pressure.reshape(planes, rows, y_parts, y_count).transpose(2, 0, 1, 3)
     pressure = lax.all_to_all(pressure, "gy", 0, 0, tiled=True)
-    pressure = pressure.transpose(0, 2, 1, 3).reshape(x_count, planes, y_count)
-    pressure_ext = extended_2(pressure, (("gx", 0), ("gy", 2)), 1, False)
-    gradient = jnp.stack(
-        [x_slope(pressure_ext, inverse_x), y_slope(pressure_ext, inverse_y), z_slope(pressure)]
+    pressure = pressure.transpose(1, 0, 2, 3).reshape(planes, x_count, y_count)
+    above, below = neighbours("gx", pressure[:, -1:], pressure[:, :1])
+    left, right = neighbours("gy", pressure[:, :, -1], pressure[:, :, 0])
+    slope_x = jnp.concatenate([pressure[:, 1:], below], axis=1) - jnp.concatenate([above, pressure[:, :-1]], axis=1)
+    slope_y = jnp.concatenate([pressure[:, :, 1:], right[:, :, None]], axis=2) - jnp.concatenate(
+        [left[:, :, None], pressure[:, :, :-1]], axis=2
     )
-    return (predicted - gradient, pressure)
+    slope_z = jnp.roll(pressure, -1, axis=0) - jnp.roll(pressure, 1, axis=0)
+    corrected = jnp.stack(
+        [
+            predicted[0] - 0.5 * inverse_x[:, None] * slope_x,
+            predicted[1] - 0.5 * inverse_y * slope_y,
+            predicted[2] - 0.5 * slope_z,
+        ]
+    )
+    return corrected.transpose(0, 2, 1, 3), pressure.transpose(1, 0, 2)
 
 
 def solution(mesh):

time: 948 us -> 855 us (0.902)
  other arithmetic: 135 us -> 51.1 us
  blocking collectives: 246 us -> 191 us
  Pallas kernels: 169 us -> 201 us
  waiting for transfers between devices: 222 us -> 249 us
  starting transfers between devices: 81.1 us -> 65.7 us
    all_to_all x2 -> x0, blocking collectives: 55.2 us -> none  [the longest x1 28.6 us: per_device(): pressure = lax.all_to_all(pressure, 'gy', 0, 0, tiled=True)]
    all_to_all x1 -> x3, waiting for transfers between devices: 0.01 us -> 35.7 us  [the longest x1 24.7 us: per_device(): pressure = lax.all_to_all(pressure, 'gy', 0, 0, tiled=True)]
    mul x5 -> x4, other arithmetic: 34 us -> 0.31 us  [the longest x1 0.09 us: per_device(): 0.5 * extended_1(inverse_dx, x_index * x_count, x_count, 16, 16)[:, None]]
    pallas_call x0 -> x1, Pallas kernels: none -> 31.8 us  [first_step(): pl.pallas_call(functools.partial(first_kernel, rows), in_specs=[anywhere]...]
    ppermute x16 -> x8, starting transfers between devices: 49.7 us -> 22.8 us  [neighbours(): return (lax.ppermute(last, axis, up), lax.ppermute(leading, axis, down))]
    sub x2 -> x1, other arithmetic: 19.7 us -> 7.11 us  [per_device(): predicted[0] - 0.5 * inverse_x[:, None] * slope_x]
    all_to_all x1 -> x3, starting transfers between devices: 3.6 us -> 14.7 us  [the longest x1 5.63 us: per_device(): diagonal = lax.all_to_all(diagonal, 'gy', 0, 0, tiled=True)]
    slice x17 -> x18, local copies, waits for them, and re-layouts: 21.1 us -> 13.4 us  [the longest x3 6.52 us: edge_columns(): velocity[..., part]]
  transfers between devices with their start and end apart: 22 -> 16, of which waited for: 11 -> 7; matrix products, arithmetic and copies ran while one was open for 9% -> 10% of each run, Pallas kernels for 2% -> 4%
where the time goes in v2:
time: 855 us; the launch traced here: 842 us
  waiting for transfers between devices  249 us (29%)
  Pallas kernels  201 us (24%)
  blocking collectives  191 us (22%)
  local copies, waits for them, and re-layouts  79.7 us (9%)
  starting transfers between devices  65.7 us (8%)
  other arithmetic  51.1 us (6%)
    all_to_all x3, blocking collectives, through_columns(): return lax.all_to_all(got, both, 0, 0, tiled=True)  178 us
    all_to_all x4, waiting for transfers between devices, through_columns(): got = lax.all_to_all(sent, both, 0, 0, tiled=True).reshape(full_x, columns)  166 us
    pallas_call x4, Pallas kernels, turn_lines(): pl.pallas_call(functools.partial(turn_kernel, stage, last, blocks, rows),...  92.8 us
    pallas_call x4, Pallas kernels, column_lines(): pl.pallas_call(functools.partial(column_kernel, rows, blocks), grid=(2 *...  64.4 us
    all_to_all x1, waiting for transfers between devices, through_columns(): return lax.all_to_all(got, both, 0, 0, tiled=True)  47.1 us
    unnamed x40, local copies, waits for them, and re-layouts  32.7 us
    pallas_call x1, Pallas kernels, first_step(): pl.pallas_call(functools.partial(first_kernel, rows), in_specs=[anywhere]...  31.8 us
    all_to_all x1, waiting for transfers between devices, per_device(): pressure = lax.all_to_all(pressure, 'gy', 0, 0, tiled=True)  24.7 us
  transfers between devices with their start and end apart: 16, of which 7 were waited for; matrix products, arithmetic and copies ran while one was open for 10% of the time, Pallas kernels for 4%

profile of v2, /device:TPU:9, one launch (start us, length us, event | category | flops | bytes accessed | tf_op | source)
XLA Modules:
  0.0 841.8 jit_solution(5252633000323010007)
XLA Ops:
  22.0 7.4 copy.251
  58.4 31.8 %shard_map.131 = (f32[4,4,64,512]{3,2,1,0:T(8,128)}, f32[3,4,256,512]{3,2,1,0:T(8,128)}) custom-call(f32[3,4,256,512]{3,2,1,0:T(8,128)} %bitcast.112, f32[4,256,512]{2,1,0:T(8,128)} %bitcast.119, f32[4,256,512]{2,1,0:T(8,128)} %bitcast.117, f32[5,4,8,512]{3,2,1,0:T(8,128)} %pad.41.above_ref, f32[5,4,8,512]{3,2,1,0:T(8,128)} %pad.42.below_ref, ...), custom_call_target="tpu_custom_call" | custom-call | tf_op jit(solution)/shard_map/pallas_call | solution.py:465
  94.3 12.3 %copy.207 = bf16[2048,2048]{0,1:T(8,128)(2,1)} copy(bf16[2048,2048]{1,0:T(8,128)(2,1)} %back_ref.7) | data formatting | bytes 16777216 | tf_op args[6]
  106.7 11.0 %all-to-all-done.1.field_ref = f32[4,4,64,512]{3,2,1,0:T(8,128)S(1)} async-done(((f32[4,4,64,512]{3,2,1,0:T(8,128)}), f32[4,4,64,512]{3,2,1,0:T(8,128)S(1)}, u32[]{:S(2)}, u32[]{:S(2)}) %all-to-all-start.1) | async-done | bytes 2097184 | tf_op jit(solution)/shard_map/all_to_all | solution.py:558
  119.0 11.8 %shard_map.132 = (f32[4,64,2048]{2,1,0:T(8,128)}, f32[4,8,64,256]{3,2,1,0:T(8,128)}) custom-call(f32[4,4]{1,0:T(4,128)} %refs_0_.7, f32[4,4,64,512]{3,2,1,0:T(8,128)} %copy-done.8, bf16[2048,2048]{1,0:T(8,128)(2,1)} %refs_2_.7), custom_call_target="tpu_custom_call" | custom-call | tf_op jit(solution)/shard_map/pallas_call | solution.py:85
  139.7 43.2 %all-to-all-done.2 = f32[32,64,256]{2,1,0:T(8,128)S(1)} async-done(((f32[32,64,256]{2,1,0:T(8,128)}), f32[32,64,256]{2,1,0:T(8,128)S(1)}, u32[]{:S(2)}, u32[]{:S(2)}) %all-to-all-start.2) | async-done | bytes 2097184 | tf_op jit(solution)/shard_map/all_to_all | solution.py:574
  184.2 16.1 %shard_map.133 = f32[32,72,256]{2,1,0:T(8,128)} custom-call(f32[2048,256]{1,0:T(8,128)} %bitcast.124, f32[8,256]{1,0:T(8,128)} %broadcast_in_dim.77.aux_ref, bf16[2048,2048]{1,0:T(8,128)(2,1)} %bitcast.98, bf16[2048,2048]{1,0:T(8,128)(2,1)} %back_ref.7, f32[2048,1]{1,0:T(8,128)} %copy.208.along_ref, f32[1,256]{1,0:T(1,128)} %bitcast.145), custom_call_target="tpu_custom_call" | custom-call | tf_op jit(solution)/shard_map/pallas_call | solution.py:157
  211.6 47.1 %all-to-all-done.3.refs_1_ = f32[32,72,256]{2,1,0:T(8,128)S(1)} async-done(((f32[32,72,256]{2,1,0:T(8,128)}), f32[32,72,256]{2,1,0:T(8,128)S(1)}, u32[]{:S(2)}, u32[]{:S(2)}) %all-to-all-start.3) | async-done | bytes 2359328 | tf_op jit(solution)/shard_map/all_to_all | solution.py:576
  260.1 24.4 %shard_map.134 = (f32[4,64,2048]{2,1,0:T(8,128)}, f32[4,8,2048]{2,1,0:T(8,128)}, f32[4,64,2048]{2,1,0:T(8,128)}, f32[4,8,64,256]{3,2,1,0:T(8,128)}) custom-call(f32[4,4]{1,0:T(4,128)} %refs_0_.7, f32[32,72,256]{2,1,0:T(8,128)} %copy-done.5, bf16[2048,2048]{1,0:T(8,128)(2,1)} %refs_2_.7, bf16[2048,2048]{1,0:T(8,128)(2,1)} %refs_2_.7, ...), custom_call_target="tpu_custom_call" | custom-call | tf_op jit(solution)/shard_map/pallas_call | solution.py:337
  294.1 43.7 %all-to-all-done.4 = f32[32,64,256]{2,1,0:T(8,128)} async-done(((f32[32,64,256]{2,1,0:T(8,128)}), f32[32,64,256]{2,1,0:T(8,128)}, u32[]{:S(2)}, u32[]{:S(2)}) %all-to-all-start.4) | async-done | bytes 2097184 | tf_op jit(solution)/shard_map/all_to_all | solution.py:574
  337.8 16.1 %shard_map.135 = f32[32,72,256]{2,1,0:T(8,128)} custom-call(f32[2048,256]{1,0:T(8,128)} %bitcast.30.field_ref, f32[8,256]{1,0:T(8,128)} %select_maximum_fusion.3.aux_ref, bf16[2048,2048]{1,0:T(8,128)(2,1)} %bitcast.99, bf16[2048,2048]{1,0:T(8,128)(2,1)} %back_ref.7, f32[2048,1]{1,0:T(8,128)} %copy.208.along_ref, f32[1,256]{1,0:T(1,128)} %bitcast.146), custom_call_target="tpu_custom_call" | custom-call | tf_op jit(solution)/shard_map/pallas_call | solution.py:157
  353.9 59.6 %all_to_all.60.refs_1_ = f32[32,72,256]{2,1,0:T(8,128)} all-to-all(f32[32,72,256]{2,1,0:T(8,128)} %shard_map.135), channel_id=1, replica_groups=mesh['gx'=8,'gy'=4] {'gx','gy'}, dimensions={0} | all-to-all | bytes 4718592 | tf_op jit(solution)/shard_map/all_to_all | solution.py:576
  413.5 25.4 %shard_map.136 = (f32[4,64,2048]{2,1,0:T(8,128)}, f32[4,8,2048]{2,1,0:T(8,128)}, f32[4,64,2048]{2,1,0:T(8,128)}, f32[4,64,2048]{2,1,0:T(8,128)}, f32[4,8,2048]{2...) custom-call(f32[4,4]{1,0:T(4,128)} %refs_0_.7, f32[32,72,256]{2,1,0:T(8,128)} %all_to_all.60.refs_1_, ...), custom_call_target="tpu_custom_call" | custom-call | tf_op jit(solution)/shard_map/pallas_call | solution.py:337
  452.0 39.6 %all-to-all-done.6 = f32[32,64,256]{2,1,0:T(8,128)} async-done(((f32[32,64,256]{2,1,0:T(8,128)}), f32[32,64,256]{2,1,0:T(8,128)}, u32[]{:S(2)}, u32[]{:S(2)}) %all-to-all-start.6) | async-done | bytes 2097184 | tf_op jit(solution)/shard_map/all_to_all | solution.py:574
  491.6 16.1 %shard_map.137 = f32[32,72,256]{2,1,0:T(8,128)} custom-call(f32[2048,256]{1,0:T(8,128)} %bitcast.34.field_ref, f32[8,256]{1,0:T(8,128)} %select_maximum_fusion.2.aux_ref, bf16[2048,2048]{1,0:T(8,128)(2,1)} %bitcast.100, bf16[2048,2048]{1,0:T(8,128)(2,1)} %back_ref.7, f32[2048,1]{1,0:T(8,128)} %copy.208.along_ref, f32[1,256]{1,0:T(1,128)} %bitcast.147), custom_call_target="tpu_custom_call" | custom-call | tf_op jit(solution)/shard_map/pallas_call | solution.py:157
  507.7 59.3 %all_to_all.61.refs_1_ = f32[32,72,256]{2,1,0:T(8,128)} all-to-all(f32[32,72,256]{2,1,0:T(8,128)} %shard_map.137), channel_id=1, replica_groups=mesh['gx'=8,'gy'=4] {'gx','gy'}, dimensions={0} | all-to-all | bytes 4718592 | tf_op jit(solution)/shard_map/all_to_all | solution.py:576
  567.1 26.0 %shard_map.138 = (f32[4,64,2048]{2,1,0:T(8,128)}, f32[4,8,2048]{2,1,0:T(8,128)}, f32[4,64,2048]{2,1,0:T(8,128)}, f32[4,64,2048]{2,1,0:T(8,128)}, f32[4,8,2048]{2...) custom-call(f32[4,4]{1,0:T(4,128)} %refs_0_.7, f32[32,72,256]{2,1,0:T(8,128)} %all_to_all.61.refs_1_, ...), custom_call_target="tpu_custom_call" | custom-call | tf_op jit(solution)/shard_map/pallas_call | solution.py:337
  606.8 39.3 %all-to-all-done.8 = f32[32,64,256]{2,1,0:T(8,128)} async-done(((f32[32,64,256]{2,1,0:T(8,128)}), f32[32,64,256]{2,1,0:T(8,128)}, u32[]{:S(2)}, u32[]{:S(2)}) %all-to-all-start.8) | async-done | bytes 2097184 | tf_op jit(solution)/shard_map/all_to_all | solution.py:574
  646.1 16.1 %shard_map.139 = f32[32,72,256]{2,1,0:T(8,128)} custom-call(f32[2048,256]{1,0:T(8,128)} %bitcast.39.field_ref, f32[8,256]{1,0:T(8,128)} %select_maximum_fusion.1.aux_ref, bf16[2048,2048]{1,0:T(8,128)(2,1)} %bitcast.101, bf16[2048,2048]{1,0:T(8,128)(2,1)} %back_ref.7, f32[2048,1]{1,0:T(8,128)} %copy.208.along_ref, f32[1,256]{1,0:T(1,128)} %bitcast.148), custom_call_target="tpu_custom_call" | custom-call | tf_op jit(solution)/shard_map/pallas_call | solution.py:157
  662.2 59.4 %all_to_all.62.refs_1_ = f32[32,72,256]{2,1,0:T(8,128)} all-to-all(f32[32,72,256]{2,1,0:T(8,128)} %shard_map.139), channel_id=1, replica_groups=mesh['gx'=8,'gy'=4] {'gx','gy'}, dimensions={0} | all-to-all | bytes 4718592 | tf_op jit(solution)/shard_map/all_to_all | solution.py:576
  721.6 17.0 %shard_map.140 = (f32[4,64,2048]{2,1,0:T(8,128)}, f32[4,8,2048]{2,1,0:T(8,128)}, f32[4,64,2048]{2,1,0:T(8,128)}, f32[4,64,2048]{2,1,0:T(8,128)}, f32[4,8,2048]{2,1,0:T(8,128)}, /*index=5*/f32[8,128]{1,0:T(8,128)}) custom-call(f32[4,4]{1,0:T(4,128)} %refs_0_.7, f32[32,72,256]{2,1,0:T(8,128)} %all_to_all.62.refs_1_, bf16[2048,2048]{1,0:T(8,128)(2,1)} %refs_2_.7, ...), custom_call_target="tpu_custom_call" | custom-call | tf_op jit(solution)/shard_map/pallas_call | solution.py:337
  746.8 12.9 %all_to_all.63 = f32[32,8,256]{2,1,0:T(8,128)S(1)} all-to-all(f32[32,8,256]{2,1,0:T(8,128)S(1)} %broadcast_in_dim.84), channel_id=1, replica_groups=mesh['gx'=8,'gy'=4] {'gx','gy'}, dimensions={0} | all-to-all | bytes 524288 | tf_op jit(solution)/shard_map/all_to_all | solution.py:601
  763.6 7.4 multiply_add_fusion
  777.7 24.7 %all-to-all-done.11 = f32[4,4,64,512]{3,2,1,0:T(8,128)S(1)} async-done(((f32[4,4,64,512]{3,2,1,0:T(8,128)}), f32[4,4,64,512]{3,2,1,0:T(8,128)S(1)}, u32[]{:S(2)}, u32[]{:S(2)}) %all-to-all-start.11) | async-done | bytes 2097184 | tf_op jit(solution)/shard_map/all_to_all | solution.py:607
  (160 shorter events, 169.4 us)
Async XLA Ops:
  5.9 29.0 %copy-start.3 = (f32[256,4,512]{2,0,1:T(8,128)}, f32[256,4,512]{2,0,1:T(8,128)S(1)}, u32[]{:S(2)}) copy-start(f32[256,4,512]{2,0,1:T(8,128)S(1)} %fusion.7) | copy-start | bytes 6291460
  7.8 33.6 %collective-permute-start = (f32[5,3,4,512]{3,1,2,0:T(4,128)}, f32[5,3,4,512]{3,1,2,0:T(4,128)S(1)}, u32[]{:S(2)}, u32[]{:S(2)}) collective-permute-start(f32[5,3,4,512]{3,1,2,0:T(4,128)} %pad_maximum_fusion), channel_id=1, source_target_pairs={{0,4},{4,8},{8,12},{12,16},{16,20},{20,24},{24,28},{1,5},{5,9},{9,... | collective-permute-start | bytes 368648 | tf_op jit(solution)/shard_map/ppermute | solution.py:487
  11.7 30.0 %collective-permute-start.1 = (f32[5,3,4,512]{3,1,2,0:T(4,128)}, f32[5,3,4,512]{3,1,2,0:T(4,128)S(1)}, u32[]{:S(2)}, u32[]{:S(2)}) collective-permute-start(f32[5,3,4,512]{3,1,2,0:T(4,128)} %pad_maximum_fusion.1), channel_id=1, source_target_pairs={{4,0},{8,4},{12,8},{16,12},{20,16},{24,20},{28,24},{5,1},{9,5},{13... | collective-permute-start | bytes 368648 | tf_op jit(solution)/shard_map/ppermute | solution.py:487
  16.3 73.9 %all-to-all-start = ((f32[4,4,64,512]{3,2,1,0:T(8,128)}), f32[4,4,64,512]{3,2,1,0:T(8,128)}, u32[]{:S(2)}, u32[]{:S(2)}) async-start(f32[4,4,64,512]{3,2,1,0:T(8,128)} %bitcast.120), calls=%async_computation | async-start | bytes 4194304 | tf_op jit(solution)/shard_map/all_to_all | solution.py:556
  36.0 4.0 copy-start.10
  39.7 8.6 %copy-start.14 = (f32[2048]{0:T(1024)S(1)}, f32[2048]{0:T(1024)}, u32[]{:S(2)}) copy-start(f32[2048]{0:T(1024)} %param.16) | copy-start | bytes 24580
  42.1 8.6 %collective-permute-start.2 = (f32[5,4,3,262]{3,1,2,0:T(4,128)S(1)}, f32[5,4,3,262]{3,1,2,0:T(4,128)S(1)}, u32[]{:S(2)}, u32[]{:S(2)}) collective-permute-start(f32[5,4,3,262]{3,1,2,0:T(4,128)S(1)} %maximum_bitcast_fusion.2), channel_id=1, source_target_pairs={{1,0},{2,1},{3,2},{5,4},{6,5},{7,6},{9,8},{10,9},{11,10},{13,12},{... | collective-permute-start | bytes 188648 | tf_op jit(solution)/shard_map/ppermute | solution.py:487
  44.7 6.9 collective-permute-start.3
  90.3 27.4 %all-to-all-start.1 = ((f32[4,4,64,512]{3,2,1,0:T(8,128)}), f32[4,4,64,512]{3,2,1,0:T(8,128)S(1)}, u32[]{:S(2)}, u32[]{:S(2)}) async-start(f32[4,4,64,512]{3,2,1,0:T(8,128)} %get-tuple-element.33), calls=%async_computation.1 | async-start | bytes 4194304 | tf_op jit(solution)/shard_map/all_to_all | solution.py:558
  130.8 5.0 copy-start.15
  130.8 6.4 copy-start.16
  130.8 52.1 %all-to-all-start.2 = ((f32[32,64,256]{2,1,0:T(8,128)}), f32[32,64,256]{2,1,0:T(8,128)S(1)}, u32[]{:S(2)}, u32[]{:S(2)}) async-start(f32[32,64,256]{2,1,0:T(8,128)} %bitcast.127), calls=%async_computation.2 | async-start | bytes 4194304 | tf_op jit(solution)/shard_map/all_to_all | solution.py:574
  200.3 58.3 %all-to-all-start.3 = ((f32[32,72,256]{2,1,0:T(8,128)}), f32[32,72,256]{2,1,0:T(8,128)S(1)}, u32[]{:S(2)}, u32[]{:S(2)}) async-start(f32[32,72,256]{2,1,0:T(8,128)} %shard_map.133), calls=%async_computation.3 | async-start | bytes 4718592 | tf_op jit(solution)/shard_map/all_to_all | solution.py:576
  284.4 6.2 copy-start
  284.4 53.4 %all-to-all-start.4 = ((f32[32,64,256]{2,1,0:T(8,128)}), f32[32,64,256]{2,1,0:T(8,128)}, u32[]{:S(2)}, u32[]{:S(2)}) async-start(f32[32,64,256]{2,1,0:T(8,128)} %bitcast.130), calls=%async_computation.4 | async-start | bytes 4194304 | tf_op jit(solution)/shard_map/all_to_all | solution.py:574
  438.9 52.7 %all-to-all-start.6 = ((f32[32,64,256]{2,1,0:T(8,128)}), f32[32,64,256]{2,1,0:T(8,128)}, u32[]{:S(2)}, u32[]{:S(2)}) async-start(f32[32,64,256]{2,1,0:T(8,128)} %bitcast.129), calls=%async_computation.6 | async-start | bytes 4194304 | tf_op jit(solution)/shard_map/all_to_all | solution.py:574
  593.1 53.0 %all-to-all-start.8 = ((f32[32,64,256]{2,1,0:T(8,128)}), f32[32,64,256]{2,1,0:T(8,128)}, u32[]{:S(2)}, u32[]{:S(2)}) async-start(f32[32,64,256]{2,1,0:T(8,128)} %bitcast.128), calls=%async_computation.8 | async-start | bytes 4194304 | tf_op jit(solution)/shard_map/all_to_all | solution.py:574
  721.6 18.4 %copy-start.1 = (f32[4,64,2048]{2,1,0:T(8,128)S(1)}, f32[4,64,2048]{2,1,0:T(8,128)}, u32[]{:S(2)}) copy-start(f32[4,64,2048]{2,1,0:T(8,128)} %get-tuple-element.46) | copy-start | bytes 6291460
  721.6 18.4 %copy-start.2 = (f32[4,64,2048]{2,1,0:T(8,128)S(1)}, f32[4,64,2048]{2,1,0:T(8,128)}, u32[]{:S(2)}) copy-start(f32[4,64,2048]{2,1,0:T(8,128)} %get-tuple-element.84) | copy-start | bytes 6291460
  772.6 29.9 %all-to-all-start.11 = ((f32[4,4,64,512]{3,2,1,0:T(8,128)}), f32[4,4,64,512]{3,2,1,0:T(8,128)S(1)}, u32[]{:S(2)}, u32[]{:S(2)}) async-start(f32[4,4,64,512]{3,2,1,0:T(8,128)} %bitcast.121), calls=%async_computation.11 | async-start | bytes 4194304 | tf_op jit(solution)/shard_map/all_to_all | solution.py:607
  808.8 17.4 %collective-permute-start.6 = (f32[4,256]{1,0:T(4,128)S(1)}, f32[4,256]{1,0:T(4,128)S(1)}, u32[]{:S(2)}, u32[]{:S(2)}) collective-permute-start(f32[4,256]{1,0:T(4,128)S(1)} %get-tuple-element.73), channel_id=1, source_target_pairs={{1,0},{2,1},{3,2},{5,4},{6,5},{7,6},{9,8},{10,9},{11,10},{13,12},{... | collective-permute-start | bytes 12296 | tf_op jit(solution)/shard_map/ppermute | solution.py:487
  811.6 14.9 %collective-permute-start.7 = (f32[4,256]{1,0:T(4,128)S(1)}, f32[4,256]{1,0:T(4,128)S(1)}, u32[]{:S(2)}, u32[]{:S(2)}) collective-permute-start(f32[4,256]{1,0:T(4,128)S(1)} %get-tuple-element.72), channel_id=1, source_target_pairs={{0,1},{1,2},{2,3},{4,5},{5,6},{6,7},{8,9},{9,10},{10,11},{12,13},{... | collective-permute-start | bytes 12296 | tf_op jit(solution)/shard_map/ppermute | solution.py:487
  814.4 12.3 %collective-permute-start.4 = (f32[4,1,512]{2,1,0:T(1,128)S(1)}, f32[4,1,512]{2,1,0:T(1,128)S(1)}, u32[]{:S(2)}, u32[]{:S(2)}) collective-permute-start(f32[4,1,512]{2,1,0:T(1,128)S(1)} %get-tuple-element.93), channel_id=1, source_target_pairs={{4,0},{8,4},{12,8},{16,12},{20,16},{24,20},{28,24},{5,1},{9,5},{13... | collective-permute-start | bytes 24584 | tf_op jit(solution)/shard_map/ppermute | solution.py:487
  817.5 9.3 %collective-permute-start.5 = (f32[4,1,512]{2,1,0:T(1,128)S(1)}, f32[4,1,512]{2,1,0:T(1,128)S(1)}, u32[]{:S(2)}, u32[]{:S(2)}) collective-permute-start(f32[4,1,512]{2,1,0:T(1,128)S(1)} %get-tuple-element.92), channel_id=1, source_target_pairs={{0,4},{4,8},{8,12},{12,16},{16,20},{20,24},{24,28},{1,5},{5,9},{9,... | collective-permute-start | bytes 24584 | tf_op jit(solution)/shard_map/ppermute | solution.py:487
  (9 other events, 21.3 us)

commit v3 on v2

--- a/solution.py
+++ b/solution.py
@@ -24,14 +24,8 @@
     return high, low
 
 
-def params(steps=True):
-    return pltpu.CompilerParams(
-        dimension_semantics=("arbitrary",) if steps else None, vmem_limit_bytes=vmem_bytes
-    )
-
-
-def whole(shape):
-    return pl.BlockSpec(shape, lambda n: (0,) * len(shape))
+def params():
+    return pltpu.CompilerParams(vmem_limit_bytes=vmem_bytes)
 
 
 def mix_planes(read, mix_ref, lines, rows):
@@ -56,130 +50,362 @@
     lax.fori_loop(0, rows // 16, strip, 0)
 
 
-def send_lines(lines, basis_ref, out_ref, rows):
-    planes, parts, _, columns = out_ref.shape
+anywhere = pl.BlockSpec(memory_space=pl.ANY)
+vector = pl.BlockSpec(memory_space=pltpu.VMEM)
+scalar = pl.BlockSpec(memory_space=pltpu.SMEM)
+
+
+class Stream:
+    def __init__(self, pairs, count, semaphores):
+        self.pairs = pairs
+        self.count = count
+        self.semaphores = semaphores
+
+    def copies(self, n):
+        pairs = self.pairs(n)
+        return [
+            pltpu.make_async_copy(given, target, self.semaphores.at[n, index])
+            for index, (given, target) in enumerate(pairs)
+        ]
+
+    def start(self, n):
+        for copy in self.copies(n):
+            copy.start()
+
+    def begin(self):
+        for n in range(min(2, self.count)):
+            self.start(n)
+
+    def take(self, n):
+        for copy in self.copies(n):
+            copy.wait()
+
+        @pl.when(n + 2 < self.count)
+        def _():
+            self.start(n + 2)
+
+    def end(self):
+        def step(n, carry):
+            for copy in self.copies(n):
+                copy.wait()
+            return carry
+
+        lax.fori_loop(0, self.count, step, 0)
+
+
+def start_all(pairs, semaphores):
+    copies = [
+        pltpu.make_async_copy(given, target, semaphores.at[index])
+        for index, (given, target) in enumerate(pairs)
+    ]
+    for copy in copies:
+        copy.start()
+    return copies
+
+
+def wait_all(copies):
+    for copy in copies:
+        copy.wait()
+
+
+def piece(index, size):
+    return pl.ds(pl.multiple_of(index * size, size), size)
+
+
+def send_lines(lines, basis, sent, out_ref, block, chunk, semaphores, stream=None):
+    planes, all_parts, rows, columns = sent.shape
     half = planes * rows
-    result = jnp.dot(lines[...], basis_ref[...], preferred_element_type=jnp.float32)
-    result = result[:half] + result[half:]
-    for m in range(planes):
-        for part in range(parts):
-            out_ref[m, part] = result[m * rows : (m + 1) * rows, part * columns : (part + 1) * columns]
-
-
-def start_kernel(rows, mix_ref, field_ref, basis_ref, kept_ref, out_ref, lines):
-    @pl.when(pl.program_id(0) == 0)
-    def _():
-        pieces, planes, _, span = field_ref.shape
-        for piece in range(pieces):
-            kept_ref[:, :, piece * span : (piece + 1) * span] = field_ref[piece]
-        mix_planes(lambda k, i, j: kept_ref[k, i, j], mix_ref, lines, rows)
-
-    send_lines(lines, basis_ref, out_ref, rows)
-
-
-def start_lines(field, basis_z, basis_y, columns):
+    parts = block // columns
+    blocks = all_parts // parts
+    out = Stream(
+        lambda n: [(sent.at[:, pl.ds(n * parts, parts)], out_ref.at[:, pl.ds(n * parts, parts)])],
+        blocks,
+        semaphores,
+    )
+
+    def step(n, carry):
+        if stream is not None:
+            stream.take(n)
+        result = jnp.dot(lines[...], basis[:, piece(chunk * blocks + n, block)], preferred_element_type=jnp.float32)
+        result = result[:half] + result[half:]
+        for m in range(planes):
+            for part in range(parts):
+                sent[m, n * parts + part] = result[
+                    m * rows : (m + 1) * rows, part * columns : (part + 1) * columns
+                ]
+        out.start(n)
+        return carry
+
+    lax.fori_loop(0, blocks, step, 0)
+    out.end()
+
+
+def column_stream(basis_ref, basis, block, chunk, blocks, semaphores):
+    def pairs(n):
+        own = piece(chunk * blocks + n, block)
+        return [(basis_ref.at[:, own], basis.at[:, own])]
+
+    return Stream(pairs, blocks, semaphores)
+
+
+def start_kernel(
+    block, mix_ref, field_ref, basis_ref, kept_ref, out_ref, lines_ref,
+    field, basis, lines, sent, semaphores, basis_semaphores, out_semaphores,
+):
+    pieces, planes, rows, span = field_ref.shape
+    given = [(field_ref.at[n], field.at[:, :, n * span : (n + 1) * span]) for n in range(pieces)]
+    given = start_all(given, semaphores)
+    stream = column_stream(basis_ref, basis, block, 0, basis_semaphores.shape[0], basis_semaphores)
+    stream.begin()
+    wait_all(given)
+    kept = pltpu.make_async_copy(field, kept_ref, semaphores.at[pieces])
+    kept.start()
+    mix_planes(lambda k, i, j: field[k, i, j], mix_ref, lines, rows)
+    mixed = pltpu.make_async_copy(lines, lines_ref, semaphores.at[pieces + 1])
+    mixed.start()
+    send_lines(lines, basis, sent, out_ref, block, 0, out_semaphores, stream)
+    kept.wait()
+    mixed.wait()
+
+
+def start_lines(field, basis_z, basis_y, columns, chunks):
     pieces, planes, rows, span = field.shape
     full = pieces * span
-    width = min(256, full)
-    parts = width // columns
+    block = min(256, full // chunks)
+    blocks = full // chunks // block
+    sent = (planes, full // chunks // columns, rows, columns)
     return pl.pallas_call(
-        functools.partial(start_kernel, rows),
-        grid=(full // width,),
-        in_specs=[
-            pl.BlockSpec(memory_space=pltpu.SMEM),
-            whole(field.shape),
-            pl.BlockSpec((full, width), lambda n: (0, n)),
-        ],
-        out_specs=[
-            whole((planes, rows, full)),
-            pl.BlockSpec((planes, parts, rows, columns), lambda n: (0, n, 0, 0)),
-        ],
+        functools.partial(start_kernel, block),
+        in_specs=[scalar, anywhere, anywhere],
+        out_specs=[anywhere] * 3,
         out_shape=[
             jax.ShapeDtypeStruct((planes, rows, full), jnp.float32),
-            jax.ShapeDtypeStruct((planes, full // columns, rows, columns), jnp.float32),
+            jax.ShapeDtypeStruct(sent, jnp.float32),
+            jax.ShapeDtypeStruct((2 * planes * rows, full), jnp.bfloat16),
         ],
-        scratch_shapes=[pltpu.VMEM((2 * planes * rows, full), jnp.bfloat16)],
+        scratch_shapes=[
+            pltpu.VMEM((planes, rows, full), jnp.float32),
+            pltpu.VMEM(basis_y.shape, jnp.bfloat16),
+            pltpu.VMEM((2 * planes * rows, full), jnp.bfloat16),
+            pltpu.VMEM(sent, jnp.float32),
+            pltpu.SemaphoreType.DMA((pieces + 2,)),
+            pltpu.SemaphoreType.DMA((blocks, 1)),
+            pltpu.SemaphoreType.DMA((blocks, 1)),
+        ],
         compiler_params=params(),
     )(basis_z, field, basis_y)
 
 
-def column_kernel(rows, blocks, field_ref, aux_ref, ahead_ref, back_ref, along_ref, other_ref, out_ref, lines, spectral):
-    step = pl.program_id(0)
+def more_kernel(block, chunk, lines_ref, basis_ref, out_ref, basis, lines, sent, semaphore, basis_semaphores, out_semaphores):
+    given = pltpu.make_async_copy(lines_ref, lines, semaphore)
+    given.start()
+    stream = column_stream(basis_ref, basis, block, chunk, basis_semaphores.shape[0], basis_semaphores)
+    stream.begin()
+    given.wait()
+    send_lines(lines, basis, sent, out_ref, block, chunk, out_semaphores, stream)
+
+
+def more_lines(lines, basis_y, planes, rows, columns, chunks, chunk):
+    full = lines.shape[1]
+    block = min(256, full // chunks)
+    blocks = full // chunks // block
+    sent = (planes, full // chunks // columns, rows, columns)
+    return pl.pallas_call(
+        functools.partial(more_kernel, block, chunk),
+        in_specs=[anywhere, anywhere],
+        out_specs=anywhere,
+        out_shape=jax.ShapeDtypeStruct(sent, jnp.float32),
+        scratch_shapes=[
+            pltpu.VMEM(basis_y.shape, jnp.bfloat16),
+            pltpu.VMEM(lines.shape, jnp.bfloat16),
+            pltpu.VMEM(sent, jnp.float32),
+            pltpu.SemaphoreType.DMA,
+            pltpu.SemaphoreType.DMA((blocks, 1)),
+            pltpu.SemaphoreType.DMA((blocks, 1)),
+        ],
+        compiler_params=params(),
+    )(lines, basis_y)
+
+
+def take_lines(got, lines, planes, rows):
+    devices, _, columns = got.shape
+    parts = devices // planes
+    half = planes * (rows + spare)
+    main = planes * rows
+    edge_rows = lax.broadcasted_iota(jnp.int32, (spare, columns), 0) < 2
+    for part in range(parts):
+        lanes = slice(part * columns, (part + 1) * columns)
+        edges = []
+        for m in range(planes):
+            high, low = halves(got[m * parts + part, :rows, :])
+            lines[m * rows : (m + 1) * rows, lanes] = high
+            lines[half + m * rows : half + (m + 1) * rows, lanes] = low
+            edges.append(jnp.where(edge_rows, got[m * parts + part, rows:, :], 0.0))
+        high, low = halves(jnp.concatenate(edges, axis=0))
+        lines[main:half, lanes] = high
+        lines[half + main :, lanes] = low
+
+
+def part_kernel(planes, rows, block, got_ref, basis_ref, out_ref, got, basis, lines, out, given_semaphores, semaphores, out_semaphores):
+    parts = got.shape[0] // planes
+    width = lines.shape[1]
+    half = planes * (rows + spare)
+    blocks = basis.shape[0] // block
+    groups = [slice(m * parts, (m + 1) * parts) for m in range(planes)]
+    given = start_all([(got_ref.at[group], got.at[group]) for group in groups], given_semaphores)
+    stream = Stream(
+        lambda n: [(basis_ref.at[piece(n, block), :width], basis.at[piece(n, block)])], blocks, semaphores
+    )
+    sink = Stream(
+        lambda n: [(out.at[:, piece(n, block)], out_ref.at[:, piece(n, block)])], blocks, out_semaphores
+    )
+    stream.begin()
+    wait_all(given)
+    take_lines(got, lines, planes, rows)
+
+    def step(n, carry):
+        stream.take(n)
+        result = lax.dot_general(
+            lines[...], basis[piece(n, block), :], (((1,), (1,)), ((), ())), preferred_element_type=jnp.float32
+        )
+        out[:, piece(n, block)] = result[:half] + result[half:]
+        sink.start(n)
+        return carry
+
+    lax.fori_loop(0, blocks, step, 0)
+    sink.end()
+
+
+def part_lines(got, basis_y, planes, rows, chunks):
+    full = basis_y.shape[0]
+    block = min(256, full)
+    half = planes * (rows + spare)
+    return pl.pallas_call(
+        functools.partial(part_kernel, planes, rows, block),
+        in_specs=[anywhere, anywhere],
+        out_specs=anywhere,
+        out_shape=jax.ShapeDtypeStruct((half, full), jnp.float32),
+        scratch_shapes=[
+            pltpu.VMEM(got.shape, jnp.float32),
+            pltpu.VMEM((full, full // chunks), jnp.bfloat16),
+            pltpu.VMEM((2 * half, full // chunks), jnp.bfloat16),
+            pltpu.VMEM((half, full), jnp.float32),
+            pltpu.SemaphoreType.DMA((planes,)),
+            pltpu.SemaphoreType.DMA((full // block, 1)),
+            pltpu.SemaphoreType.DMA((full // block, 1)),
+        ],
+        compiler_params=params(),
+    )(got, basis_y)
+
+
+def column_kernel(
+    rows, block, field_ref, aux_ref, ahead_ref, back_ref, along_ref, other_ref, out_ref,
+    field, ahead, back, lines, spectral, buffer, given_semaphores, semaphores, out_semaphores,
+):
     full, columns = field_ref.shape
-    block = full // blocks
-
-    @pl.when(step == 0)
-    def _():
-        def strip(index, carry):
-            start = pl.multiple_of(index * 64, 64)
-            high, low = halves(field_ref[pl.ds(start, 64), :])
-            lines[pl.ds(start, 64), :columns] = high
-            lines[pl.ds(start, 64), columns:] = low
-            return carry
-
-        lax.fori_loop(0, full // 64, strip, 0)
-
-    @pl.when(step < blocks)
-    def _():
-        result = jnp.dot(ahead_ref[...], lines[...], preferred_element_type=jnp.float32)
+    blocks = full // block
+    group = block // rows
+    devices = full // rows
+    given = Stream(
+        lambda n: [(field_ref.at[piece(n, block)], field.at[piece(n, block)])], blocks, given_semaphores
+    )
+    aheads = Stream(
+        lambda n: [(ahead_ref.at[piece(n, block)], ahead.at[piece(n, block)])], blocks, semaphores.at[0]
+    )
+    backs = Stream(
+        lambda n: [(back_ref.at[piece(n, block)], back.at[piece(n, block)])], blocks, semaphores.at[1]
+    )
+    out = Stream(
+        lambda n: [(buffer.at[pl.ds(n * group, group)], out_ref.at[pl.ds(n * group, group)])],
+        blocks,
+        out_semaphores,
+    )
+    for n in range(blocks):
+        given.start(n)
+    aheads.begin()
+    given.end()
+
+    def strip(index, carry):
+        own = piece(index, 64)
+        high, low = halves(field[own, :])
+        lines[own, :columns] = high
+        lines[own, columns:] = low
+        return carry
+
+    lax.fori_loop(0, full // 64, strip, 0, unroll=4)
+
+    def forth(n, carry):
+        aheads.take(n)
+
+        @pl.when(n == blocks - 1)
+        def _():
+            backs.begin()
+
+        own = piece(n, block)
+        result = jnp.dot(ahead[own, :], lines[...], preferred_element_type=jnp.float32)
         result = result[:, :columns] + result[:, columns:]
-        result = result / (along_ref[...] + other_ref[...])
-        high, low = halves(result)
-        start = pl.multiple_of(step * block, block)
-        spectral[pl.ds(start, block), :columns] = high
-        spectral[pl.ds(start, block), columns:] = low
-
-    @pl.when(step >= blocks)
-    def _():
-        result = jnp.dot(back_ref[...], spectral[...], preferred_element_type=jnp.float32)
+        high, low = halves(result / (along_ref[own, :] + other_ref[...]))
+        spectral[own, :columns] = high
+        spectral[own, columns:] = low
+        return carry
+
+    lax.fori_loop(0, blocks, forth, 0)
+
+    def reverse(n, carry):
+        backs.take(n)
+        result = jnp.dot(back[piece(n, block), :], spectral[...], preferred_element_type=jnp.float32)
         result = result[:, :columns] + result[:, columns:]
-        group = block // rows
-        first = (step - blocks) * group
         for part in range(group):
-            out_ref[first + part, :rows, :] = result[part * rows : (part + 1) * rows]
-
-    @pl.when(step == 2 * blocks - 1)
-    def _():
-        devices = full // rows
-        edge = jnp.zeros((1, columns), jnp.float32)
-        rest = aux_ref[2:, :]
-        for part in range(devices):
-            above = out_ref[part - 1, rows - 1 : rows, :] if part > 0 else edge
-            below = out_ref[part + 1, 0:1, :] if part + 1 < devices else edge
-            out_ref[part, rows:, :] = jnp.concatenate([above, below, rest], axis=0)
+            buffer[n * group + part, :rows, :] = result[part * rows : (part + 1) * rows]
+        return carry
+
+    lax.fori_loop(0, blocks, reverse, 0)
+    rest = aux_ref[2:, :]
+
+    def close(n, carry):
+        for part in range(group):
+            own = n * group + part
+            above = buffer[jnp.maximum(own - 1, 0), rows - 1 : rows, :]
+            above = jnp.where(own > 0, above, 0.0)
+            below = buffer[jnp.minimum(own + 1, devices - 1), 0:1, :]
+            below = jnp.where(own + 1 < devices, below, 0.0)
+            buffer[own, rows:, :] = jnp.concatenate([above, below, rest], axis=0)
+        out.start(n)
+        return carry
+
+    lax.fori_loop(0, blocks, close, 0)
+    out.end()
 
 
 def column_lines(field, aux, basis_xt, basis_x, along, other, rows):
     full, columns = field.shape
     block = min(512, full)
-    blocks = full // block
     devices = full // rows
     return pl.pallas_call(
-        functools.partial(column_kernel, rows, blocks),
-        grid=(2 * blocks,),
-        in_specs=[
-            whole(field.shape),
-            whole(aux.shape),
-            pl.BlockSpec((block, full), lambda n: (jnp.minimum(n, blocks - 1), 0)),
-            pl.BlockSpec((block, full), lambda n: (jnp.maximum(n - blocks, 0), 0)),
-            pl.BlockSpec((block, 1), lambda n: (jnp.minimum(n, blocks - 1), 0)),
-            whole(other.shape),
-        ],
-        out_specs=whole((devices, rows + spare, columns)),
+        functools.partial(column_kernel, rows, block),
+        in_specs=[anywhere, vector, anywhere, anywhere, vector, vector],
+        out_specs=anywhere,
         out_shape=jax.ShapeDtypeStruct((devices, rows + spare, columns), jnp.float32),
         scratch_shapes=[
+            pltpu.VMEM((full, columns), jnp.float32),
+            pltpu.VMEM((full, full), jnp.bfloat16),
+            pltpu.VMEM((full, full), jnp.bfloat16),
             pltpu.VMEM((full, 2 * columns), jnp.bfloat16),
             pltpu.VMEM((full, 2 * columns), jnp.bfloat16),
+            pltpu.VMEM((devices, rows + spare, columns), jnp.float32),
+            pltpu.SemaphoreType.DMA((full // block, 1)),
+            pltpu.SemaphoreType.DMA((2, full // block, 1)),
+            pltpu.SemaphoreType.DMA((full // block, 1)),
         ],
         compiler_params=params(),
     )(field, aux, basis_xt, basis_x, along, other)
 
 
-def turn_kernel(stage, last, blocks, rows, *refs):
+def turn_kernel(stage, last, block, chunks, *refs):
     refs = list(refs)
     take = lambda: refs.pop(0)
-    mix_ref, got_ref, rows_ref = take(), take(), take()
-    ahead_ref = None if last else take()
+    mix_ref, got_ref, basis_ref = take(), take(), take()
+    part_ref = take() if chunks > 1 else None
     diagonal_ref, low_x, high_x, low_y, high_y = take(), take(), take(), take(), take()
     if stage >= 1:
         old_z, old_edge_z = take(), take()
@@ -188,51 +414,65 @@
     z_ref, edge_z_ref, y_ref = take(), take(), take()
     if stage >= 1:
         v_ref, edge_v_ref, scalars_ref = take(), take(), take()
-    out_ref = None if last else take()
-    lines, around = take(), take()
-    ahead_lines = None if last else take()
-    step = pl.program_id(0)
-    planes, _, full = y_ref.shape
-    devices, _, columns = got_ref.shape
+    if not last:
+        out_ref, lines_ref = take(), take()
+    got, basis, diagonal, lines, around, edge_z, image = [take() for _ in range(7)]
+    if stage >= 1:
+        z, v, edge_v = take(), take(), take()
+    if not last:
+        ahead_lines, sent = take(), take()
+    part = take() if chunks > 1 else None
+    given_semaphores, semaphores, late_semaphores = take(), take(), take()
+    if not last:
+        basis_semaphores, out_semaphores = take(), take()
+    planes, rows, full = diagonal.shape
+    devices, _, columns = got.shape
     parts = devices // planes
     half = planes * (rows + spare)
     main = planes * rows
-    width = rows_ref.shape[0]
-
-    @pl.when(step == 0)
-    def _():
-        edge_rows = lax.broadcasted_iota(jnp.int32, (spare, columns), 0) < 2
-        for part in range(parts):
-            lanes = slice(part * columns, (part + 1) * columns)
-            edges = []
-            for m in range(planes):
-                high, low = halves(got_ref[m * parts + part, :rows, :])
-                lines[m * rows : (m + 1) * rows, lanes] = high
-                lines[half + m * rows : half + (m + 1) * rows, lanes] = low
-                edges.append(jnp.where(edge_rows, got_ref[m * parts + part, rows:, :], 0.0))
-            high, low = halves(jnp.concatenate(edges, axis=0))
-            lines[main:half, lanes] = high
-            lines[half + main :, lanes] = low
-        if stage >= 1:
-            product = jnp.sum(jnp.sum(got_ref[:, rows + 2, :], axis=0, keepdims=True), axis=1, keepdims=True)
-            image = jnp.sum(jnp.sum(got_ref[:, rows + 3, :], axis=0, keepdims=True), axis=1, keepdims=True)
-            if stage >= 2:
-                turn = product / old_scalars[0:1, 0:1]
-                image = image - turn * turn * old_scalars[1:2, 0:1]
-            else:
-                turn = jnp.zeros_like(product)
-            length = product / image
-            kept = [product, image, length, turn]
-            kept = [jnp.broadcast_to(value, (1, 128)) for value in kept]
-            scalars_ref[...] = jnp.concatenate(kept + [jnp.zeros((4, 128), jnp.float32)], axis=0)
-
-    @pl.when(step < blocks)
-    def _():
+    blocks = full // block
+    groups = [slice(m * parts, (m + 1) * parts) for m in range(planes)]
+    given = start_all([(got_ref.at[group], got.at[group]) for group in groups], given_semaphores)
+    width = full // chunks
+    turned = slice(full - width, full)
+    fields = []
+    if stage >= 1:
+        fields += [(old_z, z), (old_edge_z, edge_z)]
+    if stage >= 2:
+        fields += [(old_v, v), (old_edge_v, edge_v)]
+
+    def needed(n):
+        own = piece(n, block)
+        pairs = [(basis_ref.at[own, turned], basis.at[own, turned])]
+        if chunks > 1:
+            pairs.append((part_ref.at[:, own], part.at[:, own]))
+        return pairs + [(old.at[:, :, own], target.at[:, :, own]) for old, target in fields]
+
+    stream = Stream(needed, blocks, semaphores)
+    stream.begin()
+    wait_all(given)
+    take_lines(got, lines, planes, rows)
+    if stage >= 1:
+        product = jnp.sum(jnp.sum(got[:, rows + 2, :], axis=0, keepdims=True), axis=1, keepdims=True)
+        bend = jnp.sum(jnp.sum(got[:, rows + 3, :], axis=0, keepdims=True), axis=1, keepdims=True)
+        if stage >= 2:
+            turn = product / old_scalars[0:1, 0:1]
+            bend = bend - turn * turn * old_scalars[1:2, 0:1]
+        else:
+            turn = jnp.zeros_like(product)
+        length = product / bend
+        numbers = [jnp.broadcast_to(value, (1, 128)) for value in (product, bend, length, turn)]
+        scalars_ref[...] = jnp.concatenate(numbers + [jnp.zeros((4, 128), jnp.float32)], axis=0)
+
+    def finish_block(n, carry):
+        stream.take(n)
+        lanes = piece(n, block)
         result = lax.dot_general(
-            lines[...], rows_ref[...], (((1,), (1,)), ((), ())), preferred_element_type=jnp.float32
+            lines[...], basis[lanes, turned], (((1,), (1,)), ((), ())), preferred_element_type=jnp.float32
         )
         result = result[:half] + result[half:]
-        lanes = pl.ds(pl.multiple_of(step * width, width), width)
+        if chunks > 1:
+            result = result + part[:, lanes]
         if stage >= 1:
             length = scalars_ref[2:3, 0:1]
             turn = scalars_ref[3:4, 0:1]
@@ -244,99 +484,116 @@
                 edge = edge + result[main + m * spare : main + (m + 1) * spare] * mix_ref[k, m]
             if stage >= 1:
                 if stage >= 2:
-                    value = value + turn * old_v[k]
-                    edge = edge + turn * old_edge_v[k]
-                v_ref[k] = value
-                edge_v_ref[k] = edge
-                value = old_z[k] - length * value
-                edge = old_edge_z[k] - length * edge
-            z_ref[k] = value
-            edge_z_ref[k] = edge
+                    value = value + turn * v[k, :, lanes]
+                    edge = edge + turn * edge_v[k, :, lanes]
+                v[k, :, lanes] = value
+                edge_v[k, :, lanes] = edge
+                value = z[k, :, lanes] - length * value
+                edge = edge_z[k, :, lanes] - length * edge
+            edge_z[k, :, lanes] = edge
             around[k, spare : spare + rows, lanes] = value
             around[k, spare - 1 : spare, lanes] = edge[0:1]
             around[k, spare + rows : spare + rows + 1, lanes] = edge[1:2]
-
-    @pl.when(step == blocks - 1 if last else step == blocks)
-    def _():
-        for k in range(planes):
-            for start in range(0, rows, 8):
-                value = around[k, spare + start : spare + start + 8, :]
-                above = around[k, spare + start - 1 : spare + start + 7, :]
-                below = around[k, spare + start + 1 : spare + start + 9, :]
-                before = around[(k - 1) % planes, spare + start : spare + start + 8, :]
-                after = around[(k + 1) % planes, spare + start : spare + start + 8, :]
-                total = diagonal_ref[k, start : start + 8, :] * value
-                total = total + (
-                    low_x[start : start + 8, :] * (value - above)
-                    - high_x[start : start + 8, :] * (below - value)
-                )
-                left = pltpu.roll(value, 1, 1)
-                right = pltpu.roll(value, full - 1, 1)
-                total = total + (low_y[...] * (value - left) - high_y[...] * (right - value))
-                y_ref[k, start : start + 8, :] = total + (2.0 * value - before - after)
-        if not last:
-            mix_planes(lambda k, i, j: y_ref[k, i, j], mix_ref, ahead_lines, rows)
-
+        return carry
+
+    diagonal_copy = pltpu.make_async_copy(diagonal_ref, diagonal, late_semaphores.at[0])
+    diagonal_copy.start()
+    lax.fori_loop(0, blocks, finish_block, 0)
+    done = [(around.at[:, spare : spare + rows], z_ref), (edge_z, edge_z_ref)]
+    if stage >= 1:
+        done += [(v, v_ref), (edge_v, edge_v_ref)]
+    done = start_all(done, late_semaphores.at[2:6])
+    ahead = None
+    if not last and chunks > 1:
+        ahead = column_stream(basis_ref, basis, block, 0, width // block, basis_semaphores)
+        ahead.begin()
+    diagonal_copy.wait()
+
+    def operate(index, carry):
+        k = index // (rows // 8)
+        tile = index - k * (rows // 8)
+        own = piece(tile, 8)
+        window = around[k, pl.ds(pl.multiple_of(tile * 8, 8), 24), :]
+        value = window[8:16]
+        above = pltpu.roll(window, 1, 0)[8:16]
+        below = pltpu.roll(window, 23, 0)[8:16]
+        middle = pl.ds(pl.multiple_of(tile * 8 + spare, 8), 8)
+        before = around[jnp.where(k == 0, planes - 1, k - 1), middle, :]
+        after = around[jnp.where(k == planes - 1, 0, k + 1), middle, :]
+        total = diagonal[k, own, :] * value
+        total = total + (low_x[own, :] * (value - above) - high_x[own, :] * (below - value))
+        left = pltpu.roll(value, 1, 1)
+        right = pltpu.roll(value, full - 1, 1)
+        total = total + (low_y[...] * (value - left) - high_y[...] * (right - value))
+        image[k, own, :] = total + (2.0 * value - before - after)
+        return carry
+
+    lax.fori_loop(0, planes * (rows // 8), operate, 0, unroll=2)
+    image_copy = pltpu.make_async_copy(image, y_ref, late_semaphores.at[1])
+    image_copy.start()
     if not last:
-
-        @pl.when(step >= blocks)
-        def _():
-            send_lines(ahead_lines, ahead_ref, out_ref, rows)
-
-
-def turn_lines(stage, last, got, operator, basis_z, basis_y, state):
-    diagonal, low_x, high_x, low_y, high_y = operator
-    planes, rows, full = diagonal.shape
-    devices, _, columns = got.shape
-    width = min(256, full)
-    blocks = full // width
-    parts = width // columns
-    down = lambda n: jnp.minimum(n, blocks - 1)
-    field = pl.BlockSpec((planes, rows, width), lambda n: (0, 0, down(n)))
-    edge = pl.BlockSpec((planes, spare, width), lambda n: (0, 0, down(n)))
-    scalars = whole((8, 128))
+        mix_planes(lambda k, i, j: image[k, i, j], mix_ref, ahead_lines, rows)
+        mixed = pltpu.make_async_copy(ahead_lines, lines_ref, late_semaphores.at[6])
+        mixed.start()
+        send_lines(ahead_lines, basis, sent, out_ref, block, 0, out_semaphores, ahead)
+        mixed.wait()
+    image_copy.wait()
+    wait_all(done)
+
+
+def turn_lines(stage, last, got, part, operator, basis_z, basis_y, state, chunks):
+    planes, rows, full = operator[0].shape
+    _, _, columns = got.shape
+    block = min(256, full // chunks)
+    blocks = full // block
     field_shape = jax.ShapeDtypeStruct((planes, rows, full), jnp.float32)
     edge_shape = jax.ShapeDtypeStruct((planes, spare, full), jnp.float32)
-    scalars_shape = jax.ShapeDtypeStruct((8, 128), jnp.float32)
-    specs = [
-        pl.BlockSpec(memory_space=pltpu.SMEM),
-        whole(got.shape),
-        pl.BlockSpec((width, full), lambda n: (down(n), 0)),
-    ]
-    given = [basis_z, got, basis_y]
-    if not last:
-        specs.append(pl.BlockSpec((full, width), lambda n: (0, jnp.maximum(n - blocks, 0))))
-        given.append(basis_y)
-    specs += [whole(part.shape) for part in operator]
-    given += list(operator)
+    specs = [scalar] + [anywhere] * (4 if chunks > 1 else 3) + [vector] * 4
+    given = [basis_z, got, basis_y] + ([part] if chunks > 1 else []) + list(operator)
     if stage >= 1:
-        specs += [field, edge]
+        specs += [anywhere] * 2
         given += [state["z"], state["edge_z"]]
     if stage >= 2:
-        specs += [field, edge, scalars]
+        specs += [anywhere] * 2 + [vector]
         given += [state["v"], state["edge_v"], state["scalars"]]
     names = ["z", "edge_z", "y"]
-    outs = [field, edge, whole((planes, rows, full))]
+    outs = [anywhere] * 3
     shapes = [field_shape, edge_shape, field_shape]
     if stage >= 1:
         names += ["v", "edge_v", "scalars"]
-        outs += [field, edge, scalars]
-        shapes += [field_shape, edge_shape, scalars_shape]
-    half = planes * (rows + spare)
+        outs += [anywhere, anywhere, vector]
+        shapes += [field_shape, edge_shape, jax.ShapeDtypeStruct((8, 128), jnp.float32)]
+    field = pltpu.VMEM((planes, rows, full), jnp.float32)
+    edge = pltpu.VMEM((planes, spare, full), jnp.float32)
     scratch = [
-        pltpu.VMEM((2 * half, full), jnp.bfloat16),
+        pltpu.VMEM(got.shape, jnp.float32),
+        pltpu.VMEM(basis_y.shape, jnp.bfloat16),
+        field,
+        pltpu.VMEM((2 * planes * (rows + spare), full // chunks), jnp.bfloat16),
         pltpu.VMEM((planes, rows + 2 * spare, full), jnp.float32),
+        edge,
+        field,
+    ]
+    if stage >= 1:
+        scratch += [field, field, edge]
+    if not last:
+        sent = (planes, full // chunks // columns, rows, columns)
+        mixed = (2 * planes * rows, full)
+        names += ["sent", "lines"]
+        outs += [anywhere] * 2
+        shapes += [jax.ShapeDtypeStruct(sent, jnp.float32), jax.ShapeDtypeStruct(mixed, jnp.bfloat16)]
+        scratch += [pltpu.VMEM(mixed, jnp.bfloat16), pltpu.VMEM(sent, jnp.float32)]
+    if chunks > 1:
+        scratch.append(pltpu.VMEM(part.shape, jnp.float32))
+    scratch += [
+        pltpu.SemaphoreType.DMA((planes,)),
+        pltpu.SemaphoreType.DMA((blocks, 6)),
+        pltpu.SemaphoreType.DMA((7,)),
     ]
     if not last:
-        names.append("sent")
-        outs.append(
-            pl.BlockSpec((planes, parts, rows, columns), lambda n: (0, jnp.maximum(n - blocks, 0), 0, 0))
-        )
-        shapes.append(jax.ShapeDtypeStruct((planes, full // columns, rows, columns), jnp.float32))
-        scratch.append(pltpu.VMEM((2 * planes * rows, full), jnp.bfloat16))
+        scratch += [pltpu.SemaphoreType.DMA((blocks // chunks, 1))] * 2
     results = pl.pallas_call(
-        functools.partial(turn_kernel, stage, last, blocks, rows),
-        grid=(blocks if last else 2 * blocks,),
+        functools.partial(turn_kernel, stage, last, block, chunks),
         in_specs=specs,
         out_specs=outs,
         out_shape=shapes,
@@ -460,8 +717,6 @@
 def first_step(velocity, weight, code, above, below, side, half_x, half_y, rows):
     planes, count, span = weight.shape
     tall, wide = half_x.shape[0], half_y.shape[1]
-    anywhere = pl.BlockSpec(memory_space=pl.ANY)
-    vector = pl.BlockSpec(memory_space=pltpu.VMEM)
     return pl.pallas_call(
         functools.partial(first_kernel, rows),
         in_specs=[anywhere] * 6 + [vector] * 2,
@@ -476,7 +731,7 @@
             pltpu.VMEM((3, planes, tall, wide), jnp.float32),
             pltpu.SemaphoreType.DMA((20,)),
         ],
-        compiler_params=params(False),
+        compiler_params=params(),
     )(velocity, weight, code, above, below, side, half_x, half_y)
 
 
@@ -521,6 +776,8 @@
     full_y = y_count * y_parts
     rows = full_x // devices
     columns = planes * full_y // devices
+    chunks = 2 if columns % 256 == 0 else 1
+    columns = columns // chunks
     column_blocks = devices // planes
     inverse_x = lax.dynamic_slice_in_dim(inverse_dx, x_index * x_count, x_count)
     inverse_y = lax.dynamic_slice_in_dim(inverse_dy, y_index * y_count, y_count)
@@ -564,20 +821,35 @@
     face_y = whole_y[:-1] * whole_y[1:]
     operator = (diagonal, face_x[:-1, None], face_x[1:, None], face_y[None, :-1], face_y[None, 1:])
     along = eigen_x[:, None]
-    other = (
-        lax.dynamic_slice_in_dim(eigen_y, (own % column_blocks) * columns, columns)
-        + lax.dynamic_slice_in_dim(eigen_z, own // column_blocks, 1)
-    )[None]
-
-    def through_columns(sent, aux):
-        sent = sent.reshape(devices, rows, columns)
-        got = lax.all_to_all(sent, both, 0, 0, tiled=True).reshape(full_x, columns)
-        got = column_lines(got, aux, basis_xt, basis_x, along, other, rows)
-        return lax.all_to_all(got, both, 0, 0, tiled=True)
-
-    residual, sent = start_lines(source, basis_z, basis_y, columns)
-    got = through_columns(sent, jnp.zeros((spare, columns), jnp.float32))
-    state = turn_lines(0, False, got, operator, basis_z, basis_y, {})
+    other = [
+        (
+            lax.dynamic_slice_in_dim(
+                eigen_y, full_y // chunks * chunk + (own % column_blocks) * columns, columns
+            )
+            + lax.dynamic_slice_in_dim(eigen_z, own // column_blocks, 1)
+        )[None]
+        for chunk in range(chunks)
+    ]
+
+    def apply(sent, lines, aux):
+        part = None
+        sents = [sent] + [
+            more_lines(lines, basis_y, planes, rows, columns, chunks, chunk) for chunk in range(1, chunks)
+        ]
+        for chunk, sent in enumerate(sents):
+            final = chunk + 1 == chunks
+            sent = sent.reshape(devices, rows, columns)
+            got = lax.all_to_all(sent, both, 0, 0, tiled=True).reshape(full_x, columns)
+            given = aux if final else jnp.zeros((spare, columns), jnp.float32)
+            got = column_lines(got, given, basis_xt, basis_x, along, other[chunk], rows)
+            got = lax.all_to_all(got, both, 0, 0, tiled=True)
+            if not final:
+                part = part_lines(got, basis_y, planes, rows, chunks)
+        return got, part
+
+    residual, sent, lines = start_lines(source, basis_z, basis_y, columns, chunks)
+    got, part = apply(sent, lines, jnp.zeros((spare, columns), jnp.float32))
+    state = turn_lines(0, False, got, part, operator, basis_z, basis_y, {}, chunks)
     direction, image, pressure = state["z"], state["y"], None
     for iteration in range(ITERS):
         final = iteration + 1 == ITERS
@@ -594,9 +866,10 @@
         )
         if not final:
             aux = jnp.pad(partial, ((2, spare - 4), (0, 0)))
-            got = through_columns(state["sent"], aux)
+            got, part = apply(state["sent"], state["lines"], aux)
             old_z, old_y = state["z"], state["y"]
-            state = {**state, **turn_lines(iteration + 1, iteration + 2 == ITERS, got, operator, basis_z, basis_y, state)}
+            last = iteration + 2 == ITERS
+            state |= turn_lines(iteration + 1, last, got, part, operator, basis_z, basis_y, state, chunks)
     sums = jnp.broadcast_to(jnp.pad(partial, ((0, spare - 2), (0, 0)))[None], (devices, spare, columns))
     sums = lax.all_to_all(sums, both, 0, 0, tiled=True)
     product = jnp.sum(sums[:, 0])

time: 855 us -> 817 us (0.956)
  blocking collectives: 191 us -> 10.6 us
  Pallas kernels: 201 us -> 251 us
  starting transfers between devices: 65.7 us -> 112 us
  waiting for transfers between devices: 249 us -> 288 us
    all_to_all x3 -> x0, blocking collectives: 178 us -> none  [through_columns(): return lax.all_to_all(got, both, 0, 0, tiled=True)]
    pallas_call x9 -> x21, Pallas kernels: 169 us -> 219 us  [the longest x8 93.6 us: column_lines(): pl.pallas_call(functools.partial(column_kernel, rows, block), in_specs=[a...]
    all_to_all x5 -> x16, starting transfers between devices: 28.2 us -> 74.8 us  [the longest x8 37.5 us: apply(): got = lax.all_to_all(got, both, 0, 0, tiled=True)]
    all_to_all x5 -> x16, waiting for transfers between devices: 213 us -> 252 us  [the longest x8 128 us: apply(): got = lax.all_to_all(sent, both, 0, 0, tiled=True).reshape(full_x, columns)]
    unnamed x40 -> x62, local copies, waits for them, and re-layouts: 32.7 us -> 36.5 us
    reduce_sum x12 -> x11, other arithmetic: 21.3 us -> 21.6 us  [lanes_sum(): jnp.sum(value.reshape(-1, value.shape[-1] // columns, columns), axis=(0, 1))]
  transfers between devices with their start and end apart: 16 -> 27, of which waited for: 7 -> 18; matrix products, arithmetic and copies ran while one was open for 10% -> 10% of each run, Pallas kernels for 4% -> 22%
where the time goes in v3:
time: 817 us; the launch traced here: 803 us
  waiting for transfers between devices  288 us (35%)
  Pallas kernels  251 us (31%)
  starting transfers between devices  112 us (14%)
  local copies, waits for them, and re-layouts  83.7 us (10%)
  other arithmetic  52.2 us (6%)
  blocking collectives  10.6 us (1%)
    all_to_all x8, waiting for transfers between devices, apply(): got = lax.all_to_all(sent, both, 0, 0, tiled=True).reshape(full_x, columns)  128 us
    all_to_all x8, waiting for transfers between devices, apply(): got = lax.all_to_all(got, both, 0, 0, tiled=True)  125 us
    pallas_call x8, Pallas kernels, column_lines(): pl.pallas_call(functools.partial(column_kernel, rows, block), in_specs=[a...  93.6 us
    pallas_call x4, Pallas kernels, turn_lines(): pl.pallas_call(functools.partial(turn_kernel, stage, last, block, chunks)...  66.6 us
    all_to_all x8, starting transfers between devices, apply(): got = lax.all_to_all(got, both, 0, 0, tiled=True)  37.5 us
    all_to_all x8, starting transfers between devices, apply(): got = lax.all_to_all(sent, both, 0, 0, tiled=True).reshape(full_x, columns)  37.3 us
    unnamed x62, local copies, waits for them, and re-layouts  36.5 us
    pallas_call x1, Pallas kernels, first_step(): pl.pallas_call(functools.partial(first_kernel, rows), in_specs=[anywhere]...  31.8 us
  transfers between devices with their start and end apart: 27, of which 18 were waited for; matrix products, arithmetic and copies ran while one was open for 10% of the time, Pallas kernels for 22%

profile of v3, /device:TPU:9, one launch (start us, length us, event | category | flops | bytes accessed | tf_op | source)
XLA Modules:
  0.0 802.7 jit_solution(2628573233070607937)
XLA Ops:
  58.5 31.8 %shard_map.131 = (f32[4,4,64,512]{3,2,1,0:T(8,128)}, f32[3,4,256,512]{3,2,1,0:T(8,128)}) custom-call(f32[3,4,256,512]{3,2,1,0:T(8,128)} %bitcast.145, f32[4,256,512]{2,1,0:T(8,128)} %bitcast.152, f32[4,256,512]{2,1,0:T(8,128)} %bitcast.150, f32[5,4,8,512]{3,2,1,0:T(8,128)} %pad.41.above_ref, f32[5,4,8,512]{3,2,1,0:T(8,128)} %pad.42.below_ref, ...), custom_call_target="tpu_custom_call" | custom-call | tf_op jit(solution)/shard_map/pallas_call | solution.py:720
  94.4 12.3 %copy.223 = bf16[2048,2048]{0,1:T(8,128)(2,1)} copy(bf16[2048,2048]{1,0:T(8,128)(2,1)} %back_ref.15) | data formatting | bytes 16777216 | tf_op args[6]
  137.4 19.5 %all-to-all-done.4 = f32[32,64,128]{2,1,0:T(8,128)S(1)} async-done(((f32[32,64,128]{2,1,0:T(8,128)}), f32[32,64,128]{2,1,0:T(8,128)S(1)}, u32[]{:S(2)}, u32[]{:S(2)}) %all-to-all-start.4) | async-done | bytes 1048608 | tf_op jit(solution)/shard_map/all_to_all | solution.py:842
  191.4 11.7 %shard_map.134 = f32[32,72,128]{2,1,0:T(8,128)} custom-call(f32[2048,128]{1,0:T(8,128)} %bitcast.159, f32[8,128]{1,0:T(8,128)} %broadcast_1_aux_ref.2.aux_ref, bf16[2048,2048]{1,0:T(8,128)(2,1)} %bitcast.128, bf16[2048,2048]{1,0:T(8,128)(2,1)} %back_ref.15, f32[2048,1]{1,0:T(8,128)} %copy.224.along_ref, f32[1,128]{1,0:T(1,128)} %get-tuple-element.129.other_ref), custom_call_target="tpu_custom_call" | custom-call | tf_op jit(solution)/shard_map/pallas_call | solution.py:384
  203.2 16.3 %all-to-all-done.5.got_ref = f32[32,72,128]{2,1,0:T(8,128)S(1)} async-done(((f32[32,72,128]{2,1,0:T(8,128)}), f32[32,72,128]{2,1,0:T(8,128)S(1)}, u32[]{:S(2)}, u32[]{:S(2)}) %all-to-all-start.5) | async-done | bytes 1179680 | tf_op jit(solution)/shard_map/all_to_all | solution.py:845
  236.7 15.4 %all-to-all-done.3.refs_1_ = f32[32,72,128]{2,1,0:T(8,128)S(1)} async-done(((f32[32,72,128]{2,1,0:T(8,128)}), f32[32,72,128]{2,1,0:T(8,128)S(1)}, u32[]{:S(2)}, u32[]{:S(2)}) %all-to-all-start.3) | async-done | bytes 1179680 | tf_op jit(solution)/shard_map/all_to_all | solution.py:845
  253.2 16.2 %shard_map.137 = (f32[4,64,2048]{2,1,0:T(8,128)}, f32[4,8,2048]{2,1,0:T(8,128)}, f32[4,64,2048]{2,1,0:T(8,128)}, f32[4,8,64,128]{3,2,1,0:T(8,128)}, bf16[512,2048]{1,0:T(8,128)(2,1)}) custom-call(f32[4,4]{1,0:T(4,128)} %refs_0_.7, f32[32,72,128]{2,1,0:T(8,128)} %copy-done.10, bf16[2048,2048]{1,0:T(8,128)(2,1)} %refs_2_.7, f32[288,2048]{1,0:T(8,128)} %shard_map.136.refs_3_, ...), custom_call_target="tpu_custom_call" | custom-call | tf_op jit(solution)/shard_map/pallas_call | solution.py:595
  279.7 19.5 %all-to-all-done.8 = f32[32,64,128]{2,1,0:T(8,128)S(1)} async-done(((f32[32,64,128]{2,1,0:T(8,128)}), f32[32,64,128]{2,1,0:T(8,128)S(1)}, u32[]{:S(2)}, u32[]{:S(2)}) %all-to-all-start.8) | async-done | bytes 1048608 | tf_op jit(solution)/shard_map/all_to_all | solution.py:842
  315.6 13.5 %all-to-all-done.6 = f32[32,64,128]{2,1,0:T(8,128)S(1)} async-done(((f32[32,64,128]{2,1,0:T(8,128)}), f32[32,64,128]{2,1,0:T(8,128)S(1)}, u32[]{:S(2)}, u32[]{:S(2)}) %all-to-all-start.6) | async-done | bytes 1048608 | tf_op jit(solution)/shard_map/all_to_all | solution.py:842
  338.2 11.7 %shard_map.139 = f32[32,72,128]{2,1,0:T(8,128)} custom-call(f32[2048,128]{1,0:T(8,128)} %bitcast.162, f32[8,128]{1,0:T(8,128)} %select_maximum_fusion.3.aux_ref, bf16[2048,2048]{1,0:T(8,128)(2,1)} %bitcast.130, bf16[2048,2048]{1,0:T(8,128)(2,1)} %back_ref.15, f32[2048,1]{1,0:T(8,128)} %copy.224.along_ref, f32[1,128]{1,0:T(1,128)} %get-tuple-element.129.other_ref), custom_call_target="tpu_custom_call" | custom-call | tf_op jit(solution)/shard_map/pallas_call | solution.py:384
  349.9 12.9 %all-to-all-done.9.got_ref = f32[32,72,128]{2,1,0:T(8,128)S(1)} async-done(((f32[32,72,128]{2,1,0:T(8,128)}), f32[32,72,128]{2,1,0:T(8,128)S(1)}, u32[]{:S(2)}, u32[]{:S(2)}) %all-to-all-start.9) | async-done | bytes 1179680 | tf_op jit(solution)/shard_map/all_to_all | solution.py:845
  374.5 21.0 %all-to-all-done.7.refs_1_ = f32[32,72,128]{2,1,0:T(8,128)} async-done(((f32[32,72,128]{2,1,0:T(8,128)}), f32[32,72,128]{2,1,0:T(8,128)}, u32[]{:S(2)}, u32[]{:S(2)}) %all-to-all-start.7) | async-done | bytes 1179680 | tf_op jit(solution)/shard_map/all_to_all | solution.py:845
  395.5 17.5 %shard_map.142 = (f32[4,64,2048]{2,1,0:T(8,128)}, f32[4,8,2048]{2,1,0:T(8,128)}, f32[4,64,2048]{2,1,0:T(8,128)}, f32[4,64,2048]{2,1,0:T(8,128)}, f32[4,8,2048]{2...) custom-call(f32[4,4]{1,0:T(4,128)} %refs_0_.7, ...), custom_call_target="tpu_custom_call" | custom-call | tf_op jit(solution)/shard_map/pallas_call | solution.py:595
  423.5 19.5 %all-to-all-done.12 = f32[32,64,128]{2,1,0:T(8,128)S(1)} async-done(((f32[32,64,128]{2,1,0:T(8,128)}), f32[32,64,128]{2,1,0:T(8,128)S(1)}, u32[]{:S(2)}, u32[]{:S(2)}) %all-to-all-start.12) | async-done | bytes 1048608 | tf_op jit(solution)/shard_map/all_to_all | solution.py:842
  460.3 13.6 %all-to-all-done.10 = f32[32,64,128]{2,1,0:T(8,128)S(1)} async-done(((f32[32,64,128]{2,1,0:T(8,128)}), f32[32,64,128]{2,1,0:T(8,128)S(1)}, u32[]{:S(2)}, u32[]{:S(2)}) %all-to-all-start.10) | async-done | bytes 1048608 | tf_op jit(solution)/shard_map/all_to_all | solution.py:842
  487.1 11.7 %shard_map.144 = f32[32,72,128]{2,1,0:T(8,128)} custom-call(f32[2048,128]{1,0:T(8,128)} %bitcast.163, f32[8,128]{1,0:T(8,128)} %select_maximum_fusion.2.aux_ref, bf16[2048,2048]{1,0:T(8,128)(2,1)} %bitcast.132, bf16[2048,2048]{1,0:T(8,128)(2,1)} %back_ref.15, f32[2048,1]{1,0:T(8,128)} %copy.224.along_ref, f32[1,128]{1,0:T(1,128)} %get-tuple-element.129.other_ref), custom_call_target="tpu_custom_call" | custom-call | tf_op jit(solution)/shard_map/pallas_call | solution.py:384
  519.2 21.0 %all-to-all-done.11.refs_1_ = f32[32,72,128]{2,1,0:T(8,128)} async-done(((f32[32,72,128]{2,1,0:T(8,128)}), f32[32,72,128]{2,1,0:T(8,128)}, u32[]{:S(2)}, u32[]{:S(2)}) %all-to-all-start.11) | async-done | bytes 1179680 | tf_op jit(solution)/shard_map/all_to_all | solution.py:845
  540.2 18.1 %shard_map.147 = (f32[4,64,2048]{2,1,0:T(8,128)}, f32[4,8,2048]{2,1,0:T(8,128)}, f32[4,64,2048]{2,1,0:T(8,128)}, f32[4,64,2048]{2,1,0:T(8,128)}, f32[4,8,2048]{2...) custom-call(f32[4,4]{1,0:T(4,128)} %refs_0_.7, ...), custom_call_target="tpu_custom_call" | custom-call | tf_op jit(solution)/shard_map/pallas_call | solution.py:595
  568.7 19.6 %all-to-all-done.16 = f32[32,64,128]{2,1,0:T(8,128)S(1)} async-done(((f32[32,64,128]{2,1,0:T(8,128)}), f32[32,64,128]{2,1,0:T(8,128)S(1)}, u32[]{:S(2)}, u32[]{:S(2)}) %all-to-all-start.16) | async-done | bytes 1048608 | tf_op jit(solution)/shard_map/all_to_all | solution.py:842
  605.6 13.6 %all-to-all-done.14 = f32[32,64,128]{2,1,0:T(8,128)S(1)} async-done(((f32[32,64,128]{2,1,0:T(8,128)}), f32[32,64,128]{2,1,0:T(8,128)S(1)}, u32[]{:S(2)}, u32[]{:S(2)}) %all-to-all-start.14) | async-done | bytes 1048608 | tf_op jit(solution)/shard_map/all_to_all | solution.py:842
  632.9 11.7 %shard_map.149 = f32[32,72,128]{2,1,0:T(8,128)} custom-call(f32[2048,128]{1,0:T(8,128)} %bitcast.161, f32[8,128]{1,0:T(8,128)} %select_maximum_fusion.1.aux_ref, bf16[2048,2048]{1,0:T(8,128)(2,1)} %bitcast.134, bf16[2048,2048]{1,0:T(8,128)(2,1)} %back_ref.15, f32[2048,1]{1,0:T(8,128)} %copy.224.along_ref, f32[1,128]{1,0:T(1,128)} %get-tuple-element.129.other_ref), custom_call_target="tpu_custom_call" | custom-call | tf_op jit(solution)/shard_map/pallas_call | solution.py:384
  664.7 21.0 %all-to-all-done.15.refs_1_ = f32[32,72,128]{2,1,0:T(8,128)} async-done(((f32[32,72,128]{2,1,0:T(8,128)}), f32[32,72,128]{2,1,0:T(8,128)}, u32[]{:S(2)}, u32[]{:S(2)}) %all-to-all-start.15) | async-done | bytes 1179680 | tf_op jit(solution)/shard_map/all_to_all | solution.py:845
  685.7 14.8 %shard_map.152 = (f32[4,64,2048]{2,1,0:T(8,128)}, f32[4,8,2048]{2,1,0:T(8,128)}, f32[4,64,2048]{2,1,0:T(8,128)}, f32[4,64,2048]{2,1,0:T(8,128)}, f32[4,8,2048]{2,1,0:T(8,128)}, /*index=5*/f32[8,128]{1,0:T(8,128)}) custom-call(f32[4,4]{1,0:T(4,128)} %refs_0_.7, f32[32,72,128]{2,1,0:T(8,128)} %all-to-all-done.15.refs_1_, bf16[2048,2048]{1,0:T(8,128)(2,1)} %refs_2_.7, ...), custom_call_target="tpu_custom_call" | custom-call | tf_op jit(solution)/shard_map/pallas_call | solution.py:595
  738.5 24.7 %all-to-all-done.19 = f32[4,4,64,512]{3,2,1,0:T(8,128)S(1)} async-done(((f32[4,4,64,512]{3,2,1,0:T(8,128)}), f32[4,4,64,512]{3,2,1,0:T(8,128)S(1)}, u32[]{:S(2)}, u32[]{:S(2)}) %all-to-all-start.19) | async-done | bytes 2097184 | tf_op jit(solution)/shard_map/all_to_all | solution.py:880
  (206 shorter events, 388.8 us)
Async XLA Ops:
  7.8 33.6 %collective-permute-start = (f32[5,3,4,512]{3,1,2,0:T(4,128)}, f32[5,3,4,512]{3,1,2,0:T(4,128)S(1)}, u32[]{:S(2)}, u32[]{:S(2)}) collective-permute-start(f32[5,3,4,512]{3,1,2,0:T(4,128)} %pad_maximum_fusion), channel_id=1, source_target_pairs={{0,4},{4,8},{8,12},{12,16},{16,20},{20,24},{24,28},{1,5},{5,9},{9,... | collective-permute-start | bytes 368648 | tf_op jit(solution)/shard_map/ppermute | solution.py:742
  11.7 30.0 %collective-permute-start.1 = (f32[5,3,4,512]{3,1,2,0:T(4,128)}, f32[5,3,4,512]{3,1,2,0:T(4,128)S(1)}, u32[]{:S(2)}, u32[]{:S(2)}) collective-permute-start(f32[5,3,4,512]{3,1,2,0:T(4,128)} %pad_maximum_fusion.1), channel_id=1, source_target_pairs={{4,0},{8,4},{12,8},{16,12},{20,16},{24,20},{28,24},{5,1},{9,5},{13... | collective-permute-start | bytes 368648 | tf_op jit(solution)/shard_map/ppermute | solution.py:742
  16.3 74.0 %all-to-all-start = ((f32[4,4,64,512]{3,2,1,0:T(8,128)}), f32[4,4,64,512]{3,2,1,0:T(8,128)}, u32[]{:S(2)}, u32[]{:S(2)}) async-start(f32[4,4,64,512]{3,2,1,0:T(8,128)} %bitcast.153), calls=%async_computation | async-start | bytes 4194304 | tf_op jit(solution)/shard_map/all_to_all | solution.py:813
  90.3 27.5 %all-to-all-start.1 = ((f32[4,4,64,512]{3,2,1,0:T(8,128)}), f32[4,4,64,512]{3,2,1,0:T(8,128)S(1)}, u32[]{:S(2)}, u32[]{:S(2)}) async-start(f32[4,4,64,512]{3,2,1,0:T(8,128)} %get-tuple-element.37), calls=%async_computation.1 | async-start | bytes 4194304 | tf_op jit(solution)/shard_map/all_to_all | solution.py:815
  126.8 30.2 %all-to-all-start.4 = ((f32[32,64,128]{2,1,0:T(8,128)}), f32[32,64,128]{2,1,0:T(8,128)S(1)}, u32[]{:S(2)}, u32[]{:S(2)}) async-start(f32[32,64,128]{2,1,0:T(8,128)} %bitcast.176), calls=%async_computation.4 | async-start | bytes 2097152 | tf_op jit(solution)/shard_map/all_to_all | solution.py:842
  157.0 29.9 %all-to-all-start.2 = ((f32[32,64,128]{2,1,0:T(8,128)}), f32[32,64,128]{2,1,0:T(8,128)S(1)}, u32[]{:S(2)}, u32[]{:S(2)}) async-start(f32[32,64,128]{2,1,0:T(8,128)} %bitcast.167), calls=%async_computation.2 | async-start | bytes 2097152 | tf_op jit(solution)/shard_map/all_to_all | solution.py:842
  186.8 32.6 %all-to-all-start.5 = ((f32[32,72,128]{2,1,0:T(8,128)}), f32[32,72,128]{2,1,0:T(8,128)S(1)}, u32[]{:S(2)}, u32[]{:S(2)}) async-start(f32[32,72,128]{2,1,0:T(8,128)} %shard_map.135), calls=%async_computation.5 | async-start | bytes 2359296 | tf_op jit(solution)/shard_map/all_to_all | solution.py:845
  219.5 32.7 %all-to-all-start.3 = ((f32[32,72,128]{2,1,0:T(8,128)}), f32[32,72,128]{2,1,0:T(8,128)S(1)}, u32[]{:S(2)}, u32[]{:S(2)}) async-start(f32[32,72,128]{2,1,0:T(8,128)} %shard_map.134), calls=%async_computation.3 | async-start | bytes 2359296 | tf_op jit(solution)/shard_map/all_to_all | solution.py:845
  269.4 29.9 %all-to-all-start.8 = ((f32[32,64,128]{2,1,0:T(8,128)}), f32[32,64,128]{2,1,0:T(8,128)S(1)}, u32[]{:S(2)}, u32[]{:S(2)}) async-start(f32[32,64,128]{2,1,0:T(8,128)} %bitcast.175), calls=%async_computation.8 | async-start | bytes 2097152 | tf_op jit(solution)/shard_map/all_to_all | solution.py:842
  299.3 29.9 %all-to-all-start.6 = ((f32[32,64,128]{2,1,0:T(8,128)}), f32[32,64,128]{2,1,0:T(8,128)S(1)}, u32[]{:S(2)}, u32[]{:S(2)}) async-start(f32[32,64,128]{2,1,0:T(8,128)} %bitcast.169), calls=%async_computation.6 | async-start | bytes 2097152 | tf_op jit(solution)/shard_map/all_to_all | solution.py:842
  330.1 32.6 %all-to-all-start.9 = ((f32[32,72,128]{2,1,0:T(8,128)}), f32[32,72,128]{2,1,0:T(8,128)S(1)}, u32[]{:S(2)}, u32[]{:S(2)}) async-start(f32[32,72,128]{2,1,0:T(8,128)} %shard_map.140), calls=%async_computation.9 | async-start | bytes 2359296 | tf_op jit(solution)/shard_map/all_to_all | solution.py:845
  362.8 32.8 %all-to-all-start.7 = ((f32[32,72,128]{2,1,0:T(8,128)}), f32[32,72,128]{2,1,0:T(8,128)}, u32[]{:S(2)}, u32[]{:S(2)}) async-start(f32[32,72,128]{2,1,0:T(8,128)} %shard_map.139), calls=%async_computation.7 | async-start | bytes 2359296 | tf_op jit(solution)/shard_map/all_to_all | solution.py:845
  413.1 29.9 %all-to-all-start.12 = ((f32[32,64,128]{2,1,0:T(8,128)}), f32[32,64,128]{2,1,0:T(8,128)S(1)}, u32[]{:S(2)}, u32[]{:S(2)}) async-start(f32[32,64,128]{2,1,0:T(8,128)} %bitcast.174), calls=%async_computation.12 | async-start | bytes 2097152 | tf_op jit(solution)/shard_map/all_to_all | solution.py:842
  444.0 29.9 %all-to-all-start.10 = ((f32[32,64,128]{2,1,0:T(8,128)}), f32[32,64,128]{2,1,0:T(8,128)S(1)}, u32[]{:S(2)}, u32[]{:S(2)}) async-start(f32[32,64,128]{2,1,0:T(8,128)} %bitcast.170), calls=%async_computation.10 | async-start | bytes 2097152 | tf_op jit(solution)/shard_map/all_to_all | solution.py:842
  474.8 32.6 %all-to-all-start.13 = ((f32[32,72,128]{2,1,0:T(8,128)}), f32[32,72,128]{2,1,0:T(8,128)S(1)}, u32[]{:S(2)}, u32[]{:S(2)}) async-start(f32[32,72,128]{2,1,0:T(8,128)} %shard_map.145), calls=%async_computation.13 | async-start | bytes 2359296 | tf_op jit(solution)/shard_map/all_to_all | solution.py:845
  507.5 32.8 %all-to-all-start.11 = ((f32[32,72,128]{2,1,0:T(8,128)}), f32[32,72,128]{2,1,0:T(8,128)}, u32[]{:S(2)}, u32[]{:S(2)}) async-start(f32[32,72,128]{2,1,0:T(8,128)} %shard_map.144), calls=%async_computation.11 | async-start | bytes 2359296 | tf_op jit(solution)/shard_map/all_to_all | solution.py:845
  558.4 29.9 %all-to-all-start.16 = ((f32[32,64,128]{2,1,0:T(8,128)}), f32[32,64,128]{2,1,0:T(8,128)S(1)}, u32[]{:S(2)}, u32[]{:S(2)}) async-start(f32[32,64,128]{2,1,0:T(8,128)} %bitcast.173), calls=%async_computation.16 | async-start | bytes 2097152 | tf_op jit(solution)/shard_map/all_to_all | solution.py:842
  589.2 29.9 %all-to-all-start.14 = ((f32[32,64,128]{2,1,0:T(8,128)}), f32[32,64,128]{2,1,0:T(8,128)S(1)}, u32[]{:S(2)}, u32[]{:S(2)}) async-start(f32[32,64,128]{2,1,0:T(8,128)} %bitcast.168), calls=%async_computation.14 | async-start | bytes 2097152 | tf_op jit(solution)/shard_map/all_to_all | solution.py:842
  620.1 32.8 %all-to-all-start.17 = ((f32[32,72,128]{2,1,0:T(8,128)}), f32[32,72,128]{2,1,0:T(8,128)S(1)}, u32[]{:S(2)}, u32[]{:S(2)}) async-start(f32[32,72,128]{2,1,0:T(8,128)} %shard_map.150), calls=%async_computation.17 | async-start | bytes 2359296 | tf_op jit(solution)/shard_map/all_to_all | solution.py:845
  652.9 32.8 %all-to-all-start.15 = ((f32[32,72,128]{2,1,0:T(8,128)}), f32[32,72,128]{2,1,0:T(8,128)}, u32[]{:S(2)}, u32[]{:S(2)}) async-start(f32[32,72,128]{2,1,0:T(8,128)} %shard_map.149), calls=%async_computation.15 | async-start | bytes 2359296 | tf_op jit(solution)/shard_map/all_to_all | solution.py:845
  733.5 29.7 %all-to-all-start.19 = ((f32[4,4,64,512]{3,2,1,0:T(8,128)}), f32[4,4,64,512]{3,2,1,0:T(8,128)S(1)}, u32[]{:S(2)}, u32[]{:S(2)}) async-start(f32[4,4,64,512]{3,2,1,0:T(8,128)} %bitcast.154), calls=%async_computation.19 | async-start | bytes 4194304 | tf_op jit(solution)/shard_map/all_to_all | solution.py:880
  769.6 17.5 %collective-permute-start.6 = (f32[4,256]{1,0:T(4,128)S(1)}, f32[4,256]{1,0:T(4,128)S(1)}, u32[]{:S(2)}, u32[]{:S(2)}) collective-permute-start(f32[4,256]{1,0:T(4,128)S(1)} %get-tuple-element.81), channel_id=1, source_target_pairs={{1,0},{2,1},{3,2},{5,4},{6,5},{7,6},{9,8},{10,9},{11,10},{13,12},{... | collective-permute-start | bytes 12296 | tf_op jit(solution)/shard_map/ppermute | solution.py:742
  772.4 14.9 %collective-permute-start.7 = (f32[4,256]{1,0:T(4,128)S(1)}, f32[4,256]{1,0:T(4,128)S(1)}, u32[]{:S(2)}, u32[]{:S(2)}) collective-permute-start(f32[4,256]{1,0:T(4,128)S(1)} %get-tuple-element.80), channel_id=1, source_target_pairs={{0,1},{1,2},{2,3},{4,5},{5,6},{6,7},{8,9},{9,10},{10,11},{12,13},{... | collective-permute-start | bytes 12296 | tf_op jit(solution)/shard_map/ppermute | solution.py:742
  775.2 12.4 %collective-permute-start.4 = (f32[4,1,512]{2,1,0:T(1,128)S(1)}, f32[4,1,512]{2,1,0:T(1,128)S(1)}, u32[]{:S(2)}, u32[]{:S(2)}) collective-permute-start(f32[4,1,512]{2,1,0:T(1,128)S(1)} %get-tuple-element.99), channel_id=1, source_target_pairs={{4,0},{8,4},{12,8},{16,12},{20,16},{24,20},{28,24},{5,1},{9,5},{13... | collective-permute-start | bytes 24584 | tf_op jit(solution)/shard_map/ppermute | solution.py:742
  (31 other events, 235.2 us)

commit v4 on v3

--- a/solution.py
+++ b/solution.py
@@ -407,16 +407,17 @@
     mix_ref, got_ref, basis_ref = take(), take(), take()
     part_ref = take() if chunks > 1 else None
     diagonal_ref, low_x, high_x, low_y, high_y = take(), take(), take(), take(), take()
+    residual_ref = take()
     if stage >= 1:
-        old_z, old_edge_z = take(), take()
+        old_z, old_edge_z, scalars_ref = take(), take(), take()
     if stage >= 2:
-        old_v, old_edge_v, old_scalars = take(), take(), take()
-    z_ref, edge_z_ref, y_ref = take(), take(), take()
+        old_v, old_edge_v = take(), take()
+    z_ref, edge_z_ref, y_ref, aux_ref = take(), take(), take(), take()
     if stage >= 1:
-        v_ref, edge_v_ref, scalars_ref = take(), take(), take()
+        v_ref, edge_v_ref = take(), take()
     if not last:
         out_ref, lines_ref = take(), take()
-    got, basis, diagonal, lines, around, edge_z, image = [take() for _ in range(7)]
+    got, basis, diagonal, lines, around, edge_z, image, residual = [take() for _ in range(8)]
     if stage >= 1:
         z, v, edge_v = take(), take(), take()
     if not last:
@@ -435,7 +436,7 @@
     given = start_all([(got_ref.at[group], got.at[group]) for group in groups], given_semaphores)
     width = full // chunks
     turned = slice(full - width, full)
-    fields = []
+    fields = [(residual_ref, residual)]
     if stage >= 1:
         fields += [(old_z, z), (old_edge_z, edge_z)]
     if stage >= 2:
@@ -452,17 +453,11 @@
     stream.begin()
     wait_all(given)
     take_lines(got, lines, planes, rows)
-    if stage >= 1:
-        product = jnp.sum(jnp.sum(got[:, rows + 2, :], axis=0, keepdims=True), axis=1, keepdims=True)
-        bend = jnp.sum(jnp.sum(got[:, rows + 3, :], axis=0, keepdims=True), axis=1, keepdims=True)
-        if stage >= 2:
-            turn = product / old_scalars[0:1, 0:1]
-            bend = bend - turn * turn * old_scalars[1:2, 0:1]
-        else:
-            turn = jnp.zeros_like(product)
-        length = product / bend
-        numbers = [jnp.broadcast_to(value, (1, 128)) for value in (product, bend, length, turn)]
-        scalars_ref[...] = jnp.concatenate(numbers + [jnp.zeros((4, 128), jnp.float32)], axis=0)
+    def fold(value):
+        total = value[:, :columns]
+        for left in range(columns, value.shape[1], columns):
+            total = total + value[:, left : left + columns]
+        return total
 
     def finish_block(n, carry):
         stream.take(n)
@@ -491,6 +486,9 @@
                 value = z[k, :, lanes] - length * value
                 edge = edge_z[k, :, lanes] - length * edge
             edge_z[k, :, lanes] = edge
+            shared = fold(residual[k, :, lanes] * value)
+            for start in range(0, rows, 8):
+                carry = carry + shared[start : start + 8]
             around[k, spare : spare + rows, lanes] = value
             around[k, spare - 1 : spare, lanes] = edge[0:1]
             around[k, spare + rows : spare + rows + 1, lanes] = edge[1:2]
@@ -498,7 +496,8 @@
 
     diagonal_copy = pltpu.make_async_copy(diagonal_ref, diagonal, late_semaphores.at[0])
     diagonal_copy.start()
-    lax.fori_loop(0, blocks, finish_block, 0)
+    nothing = jnp.zeros((8, columns), jnp.float32)
+    product = lax.fori_loop(0, blocks, finish_block, nothing)
     done = [(around.at[:, spare : spare + rows], z_ref), (edge_z, edge_z_ref)]
     if stage >= 1:
         done += [(v, v_ref), (edge_v, edge_v_ref)]
@@ -525,10 +524,20 @@
         left = pltpu.roll(value, 1, 1)
         right = pltpu.roll(value, full - 1, 1)
         total = total + (low_y[...] * (value - left) - high_y[...] * (right - value))
-        image[k, own, :] = total + (2.0 * value - before - after)
-        return carry
-
-    lax.fori_loop(0, planes * (rows // 8), operate, 0, unroll=2)
+        total = total + (2.0 * value - before - after)
+        image[k, own, :] = total
+        return carry + fold(value * total)
+
+    bend = lax.fori_loop(0, planes * (rows // 8), operate, nothing, unroll=2)
+    aux_ref[...] = jnp.concatenate(
+        [
+            nothing[:2],
+            jnp.sum(product, axis=0, keepdims=True),
+            jnp.sum(bend, axis=0, keepdims=True),
+            nothing[4:],
+        ],
+        axis=0,
+    )
     image_copy = pltpu.make_async_copy(image, y_ref, late_semaphores.at[1])
     image_copy.start()
     if not last:
@@ -550,19 +559,21 @@
     edge_shape = jax.ShapeDtypeStruct((planes, spare, full), jnp.float32)
     specs = [scalar] + [anywhere] * (4 if chunks > 1 else 3) + [vector] * 4
     given = [basis_z, got, basis_y] + ([part] if chunks > 1 else []) + list(operator)
+    specs.append(anywhere)
+    given.append(state["residual"])
     if stage >= 1:
+        specs += [anywhere] * 2 + [vector]
+        given += [state["z"], state["edge_z"], state["scalars"]]
+    if stage >= 2:
         specs += [anywhere] * 2
-        given += [state["z"], state["edge_z"]]
-    if stage >= 2:
-        specs += [anywhere] * 2 + [vector]
-        given += [state["v"], state["edge_v"], state["scalars"]]
-    names = ["z", "edge_z", "y"]
-    outs = [anywhere] * 3
-    shapes = [field_shape, edge_shape, field_shape]
+        given += [state["v"], state["edge_v"]]
+    names = ["z", "edge_z", "y", "aux"]
+    outs = [anywhere] * 3 + [vector]
+    shapes = [field_shape, edge_shape, field_shape, jax.ShapeDtypeStruct((spare, columns), jnp.float32)]
     if stage >= 1:
-        names += ["v", "edge_v", "scalars"]
-        outs += [anywhere, anywhere, vector]
-        shapes += [field_shape, edge_shape, jax.ShapeDtypeStruct((8, 128), jnp.float32)]
+        names += ["v", "edge_v"]
+        outs += [anywhere, anywhere]
+        shapes += [field_shape, edge_shape]
     field = pltpu.VMEM((planes, rows, full), jnp.float32)
     edge = pltpu.VMEM((planes, spare, full), jnp.float32)
     scratch = [
@@ -572,6 +583,7 @@
         pltpu.VMEM((2 * planes * (rows + spare), full // chunks), jnp.bfloat16),
         pltpu.VMEM((planes, rows + 2 * spare, full), jnp.float32),
         edge,
+        field,
         field,
     ]
     if stage >= 1:
@@ -587,7 +599,7 @@
         scratch.append(pltpu.VMEM(part.shape, jnp.float32))
     scratch += [
         pltpu.SemaphoreType.DMA((planes,)),
-        pltpu.SemaphoreType.DMA((blocks, 6)),
+        pltpu.SemaphoreType.DMA((blocks, 7)),
         pltpu.SemaphoreType.DMA((7,)),
     ]
     if not last:
@@ -747,8 +759,81 @@
     return lax.dynamic_slice_in_dim(padded, start, count + before + after)
 
 
-def lanes_sum(value, columns):
-    return jnp.sum(value.reshape(-1, value.shape[-1] // columns, columns), axis=(0, 1))
+def add_kernel(numbers_ref, pressure_ref, direction_ref, lifted_ref, out_ref):
+    length = numbers_ref[2:3, 0:1]
+    turn = numbers_ref[3:4, 0:1]
+    for k in range(pressure_ref.shape[0]):
+        direction = lifted_ref[k] + turn * direction_ref[k]
+        out_ref[0, k] = pressure_ref[k] + length * direction
+
+
+def add_step(numbers, pressure, direction, lifted, pieces):
+    planes, rows, full = pressure.shape
+    span = full // pieces
+    field = pl.BlockSpec((planes, rows, span), lambda n: (0, 0, n))
+    return pl.pallas_call(
+        add_kernel,
+        grid=(pieces,),
+        in_specs=[vector] + [field] * 3,
+        out_specs=pl.BlockSpec((1, planes, rows, span), lambda n: (n, 0, 0, 0)),
+        out_shape=jax.ShapeDtypeStruct((pieces, planes, rows, span), jnp.float32),
+        compiler_params=params(),
+    )(numbers, pressure, direction, lifted)
+
+
+def correct_kernel(
+    predicted_ref, own_ref, previous_ref, next_ref, above_ref, below_ref, left_ref, right_ref,
+    half_x_ref, half_y_ref, corrected_ref, pressure_ref,
+):
+    n = pl.program_id(0)
+    last = pl.num_programs(0) - 1
+    _, planes, rows, _ = own_ref.shape
+    for k in range(planes):
+        value = own_ref[0, k]
+        above = jnp.where(n == 0, above_ref[k], previous_ref[0, k, rows - 1 : rows, :])
+        below = jnp.where(n == last, below_ref[k], next_ref[0, k, 0:1, :])
+        rising = jnp.concatenate([value[1:], below], axis=0) - jnp.concatenate([above, value[:-1]], axis=0)
+        ahead = jnp.concatenate([value[:, 1:], right_ref[0, k]], axis=1)
+        behind = jnp.concatenate([left_ref[0, k], value[:, :-1]], axis=1)
+        across = own_ref[0, (k + 1) % planes] - own_ref[0, (k - 1) % planes]
+        pressure_ref[:, k, :] = value
+        corrected_ref[0, :, k, :] = predicted_ref[0, k] - half_x_ref[...] * rising
+        corrected_ref[1, :, k, :] = predicted_ref[1, k] - half_y_ref[...] * (ahead - behind)
+        corrected_ref[2, :, k, :] = predicted_ref[2, k] - 0.5 * across
+
+
+def correct_step(predicted, pressure, above, below, left, right, half_x, half_y):
+    pieces, planes, rows, span = pressure.shape
+    count = pieces * rows
+    own = lambda shift: pl.BlockSpec(
+        (1, planes, rows, span), lambda n: (jnp.clip(n + shift, 0, pieces - 1), 0, 0, 0)
+    )
+    column = pl.BlockSpec((1, planes, rows, 1), lambda n: (n, 0, 0, 0))
+    return pl.pallas_call(
+        correct_kernel,
+        grid=(pieces,),
+        in_specs=[
+            pl.BlockSpec((3, planes, rows, span), lambda n: (0, 0, n, 0)),
+            own(0),
+            own(-1),
+            own(1),
+            vector,
+            vector,
+            column,
+            column,
+            pl.BlockSpec((rows, 1), lambda n: (n, 0)),
+            vector,
+        ],
+        out_specs=[
+            pl.BlockSpec((3, rows, planes, span), lambda n: (0, n, 0, 0)),
+            pl.BlockSpec((rows, planes, span), lambda n: (n, 0, 0)),
+        ],
+        out_shape=[
+            jax.ShapeDtypeStruct((3, count, planes, span), jnp.float32),
+            jax.ShapeDtypeStruct((count, planes, span), jnp.float32),
+        ],
+        compiler_params=params(),
+    )(predicted, pressure, pressure, pressure, above, below, left, right, half_x, half_y)
 
 
 def per_device(
@@ -832,68 +917,65 @@
     ]
 
     def apply(sent, lines, aux):
-        part = None
+        part = sums = None
         sents = [sent] + [
             more_lines(lines, basis_y, planes, rows, columns, chunks, chunk) for chunk in range(1, chunks)
         ]
         for chunk, sent in enumerate(sents):
-            final = chunk + 1 == chunks
             sent = sent.reshape(devices, rows, columns)
             got = lax.all_to_all(sent, both, 0, 0, tiled=True).reshape(full_x, columns)
-            given = aux if final else jnp.zeros((spare, columns), jnp.float32)
+            given = aux if chunk == 0 else jnp.zeros((spare, columns), jnp.float32)
             got = column_lines(got, given, basis_xt, basis_x, along, other[chunk], rows)
             got = lax.all_to_all(got, both, 0, 0, tiled=True)
-            if not final:
+            if chunk == 0:
+                sums = got[:, rows:]
+            if chunk + 1 < chunks:
                 part = part_lines(got, basis_y, planes, rows, chunks)
-        return got, part
+        return got, part, sums
+
+    def numbers_of(sums, numbers):
+        product = jnp.sum(sums[:, 2])
+        bend = jnp.sum(sums[:, 3])
+        turn = jnp.zeros_like(product)
+        if numbers is not None:
+            turn = product / numbers[0, 0]
+            bend = bend - turn * turn * numbers[1, 0]
+        numbers = jnp.stack([product, bend, product / bend, turn])
+        return jnp.broadcast_to(jnp.pad(numbers, (0, 4))[:, None], (8, 128))
 
     residual, sent, lines = start_lines(source, basis_z, basis_y, columns, chunks)
-    got, part = apply(sent, lines, jnp.zeros((spare, columns), jnp.float32))
-    state = turn_lines(0, False, got, part, operator, basis_z, basis_y, {}, chunks)
-    direction, image, pressure = state["z"], state["y"], None
-    for iteration in range(ITERS):
-        final = iteration + 1 == ITERS
-        if iteration > 0:
-            length = state["scalars"][2, 0]
-            turn = state["scalars"][3, 0]
-            if iteration > 1:
-                direction = old_z + turn * direction
-                image = old_y + turn * image
-            pressure = length * direction + (pressure if iteration > 1 else 0.0)
-            residual = residual - length * image
-        partial = jnp.stack(
-            [lanes_sum(residual * state["z"], columns), lanes_sum(state["z"] * state["y"], columns)]
-        )
-        if not final:
-            aux = jnp.pad(partial, ((2, spare - 4), (0, 0)))
-            got, part = apply(state["sent"], state["lines"], aux)
-            old_z, old_y = state["z"], state["y"]
-            last = iteration + 2 == ITERS
-            state |= turn_lines(iteration + 1, last, got, part, operator, basis_z, basis_y, state, chunks)
-    sums = jnp.broadcast_to(jnp.pad(partial, ((0, spare - 2), (0, 0)))[None], (devices, spare, columns))
+    got, part, _ = apply(sent, lines, jnp.zeros((spare, columns), jnp.float32))
+    state = {"residual": residual}
+    state |= turn_lines(0, False, got, part, operator, basis_z, basis_y, state, chunks)
+    numbers = None
+    for stage in range(1, ITERS):
+        got, part, sums = apply(state["sent"], state["lines"], state["aux"])
+        numbers = numbers_of(sums, numbers)
+        length, turn = numbers[2, 0], numbers[3, 0]
+        if stage == 1:
+            direction, image = state["z"], state["y"]
+            pressure = length * direction
+        else:
+            direction = state["z"] + turn * direction
+            image = state["y"] + turn * image
+            pressure = pressure + length * direction
+        state["residual"] = state["residual"] - length * image
+        state["scalars"] = numbers
+        last = stage + 1 == ITERS
+        state |= turn_lines(stage, last, got, part, operator, basis_z, basis_y, state, chunks)
+    sums = jnp.broadcast_to(state["aux"][None], (devices, spare, columns))
     sums = lax.all_to_all(sums, both, 0, 0, tiled=True)
-    product = jnp.sum(sums[:, 0])
-    turn = product / state["scalars"][0, 0]
-    length = product / (jnp.sum(sums[:, 1]) - turn * turn * state["scalars"][1, 0])
-    pressure = pressure + length * (state["z"] + turn * direction)
-    pressure = pressure.reshape(planes, rows, y_parts, y_count).transpose(2, 0, 1, 3)
+    numbers = numbers_of(sums, numbers)
+    pressure = add_step(numbers, pressure, direction, state["z"], y_parts)
     pressure = lax.all_to_all(pressure, "gy", 0, 0, tiled=True)
-    pressure = pressure.transpose(1, 0, 2, 3).reshape(planes, x_count, y_count)
-    above, below = neighbours("gx", pressure[:, -1:], pressure[:, :1])
-    left, right = neighbours("gy", pressure[:, :, -1], pressure[:, :, 0])
-    slope_x = jnp.concatenate([pressure[:, 1:], below], axis=1) - jnp.concatenate([above, pressure[:, :-1]], axis=1)
-    slope_y = jnp.concatenate([pressure[:, :, 1:], right[:, :, None]], axis=2) - jnp.concatenate(
-        [left[:, :, None], pressure[:, :, :-1]], axis=2
-    )
-    slope_z = jnp.roll(pressure, -1, axis=0) - jnp.roll(pressure, 1, axis=0)
-    corrected = jnp.stack(
-        [
-            predicted[0] - 0.5 * inverse_x[:, None] * slope_x,
-            predicted[1] - 0.5 * inverse_y * slope_y,
-            predicted[2] - 0.5 * slope_z,
-        ]
-    )
-    return corrected.transpose(0, 2, 1, 3), pressure.transpose(1, 0, 2)
+    above, below = neighbours("gx", pressure[-1, :, -1:], pressure[0, :, :1])
+    left, right = neighbours("gy", pressure[..., -1], pressure[..., 0])
+    half_x = 0.5 * inverse_x[:, None]
+    half_y = 0.5 * inverse_y[None]
+    corrected, pressure = correct_step(
+        predicted, pressure, above, below, left[..., None], right[..., None], half_x, half_y
+    )
+    return corrected, pressure
 
 
 def solution(mesh):

time: 817 us -> 792 us (0.969)
  local copies, waits for them, and re-layouts: 83.7 us -> 60.7 us
  other arithmetic: 52.2 us -> 32 us
  Pallas kernels: 251 us -> 269 us
  blocking collectives: 10.6 us -> 0 us
    reduce_sum x13 -> x5, other arithmetic: 22.9 us -> 3.36 us  [the longest x4 2.69 us: numbers_of(): bend = jnp.sum(sums[:, 3])]
    pallas_call x0 -> x2, Pallas kernels: none -> 14.8 us  [the longest x1 9.88 us: correct_step(): pl.pallas_call(correct_kernel, grid=(pieces,), in_specs=[pl.BlockSpec((3,...]
    unnamed x62 -> x80, local copies, waits for them, and re-layouts: 36.5 us -> 25.2 us
    all_to_all x1 -> x0, blocking collectives: 10.6 us -> none  [per_device(): sums = lax.all_to_all(sums, both, 0, 0, tiled=True)]
  transfers between devices with their start and end apart: 27 -> 28, of which waited for: 18 -> 21; matrix products, arithmetic and copies ran while one was open for 10% -> 9% of each run, Pallas kernels for 22% -> 23%
where the time goes in v4:
time: 792 us; the launch traced here: 779 us
  waiting for transfers between devices  289 us (36%)
  Pallas kernels  269 us (34%)
  starting transfers between devices  117 us (15%)
  local copies, waits for them, and re-layouts  60.7 us (8%)
  other arithmetic  32 us (4%)
  between operations  11.5 us (1%)
    all_to_all x8, waiting for transfers between devices, apply(): got = lax.all_to_all(sent, both, 0, 0, tiled=True).reshape(full_x, columns)  128 us
    all_to_all x8, waiting for transfers between devices, apply(): got = lax.all_to_all(got, both, 0, 0, tiled=True)  123 us
    pallas_call x8, Pallas kernels, column_lines(): pl.pallas_call(functools.partial(column_kernel, rows, block), in_specs=[a...  93.6 us
    pallas_call x4, Pallas kernels, turn_lines(): pl.pallas_call(functools.partial(turn_kernel, stage, last, block, chunks)...  68.9 us
    all_to_all x8, starting transfers between devices, apply(): got = lax.all_to_all(got, both, 0, 0, tiled=True)  37.8 us
    all_to_all x8, starting transfers between devices, apply(): got = lax.all_to_all(sent, both, 0, 0, tiled=True).reshape(full_x, columns)  37.5 us
    pallas_call x1, Pallas kernels, first_step(): pl.pallas_call(functools.partial(first_kernel, rows), in_specs=[anywhere]...  31.7 us
    pallas_call x4, Pallas kernels, part_lines(): pl.pallas_call(functools.partial(part_kernel, planes, rows, block), in_sp...  29.2 us
  transfers between devices with their start and end apart: 28, of which 21 were waited for; matrix products, arithmetic and copies ran while one was open for 9% of the time, Pallas kernels for 23%

profile of v4, /device:TPU:9, one launch (start us, length us, event | category | flops | bytes accessed | tf_op | source)
XLA Modules:
  0.0 779.0 jit_solution(17985711716807341304)
XLA Ops:
  56.0 31.7 %shard_map.131 = (f32[4,4,64,512]{3,2,1,0:T(8,128)}, f32[3,4,256,512]{3,2,1,0:T(8,128)}) custom-call(f32[3,4,256,512]{3,2,1,0:T(8,128)} %bitcast.103, f32[4,256,512]{2,1,0:T(8,128)} %bitcast.106, f32[4,256,512]{2,1,0:T(8,128)} %bitcast.105, f32[5,4,8,512]{3,2,1,0:T(8,128)} %pad.40.above_ref, f32[5,4,8,512]{3,2,1,0:T(8,128)} %pad.41.below_ref, ...), custom_call_target="tpu_custom_call" | custom-call | tf_op jit(solution)/shard_map/pallas_call | solution.py:732
  91.5 12.4 %copy.245 = bf16[2048,2048]{0,1:T(8,128)(2,1)} copy(bf16[2048,2048]{1,0:T(8,128)(2,1)} %back_ref.15) | data formatting | bytes 16777216 | tf_op args[6]
  134.7 19.5 %all-to-all-done.4 = f32[32,64,128]{2,1,0:T(8,128)S(1)} async-done(((f32[32,64,128]{2,1,0:T(8,128)}), f32[32,64,128]{2,1,0:T(8,128)S(1)}, u32[]{:S(2)}, u32[]{:S(2)}) %all-to-all-start.4) | async-done | bytes 1048608 | tf_op jit(solution)/shard_map/all_to_all | solution.py:926
  200.5 16.3 %all-to-all-done.5.got_ref = f32[32,72,128]{2,1,0:T(8,128)S(1)} async-done(((f32[32,72,128]{2,1,0:T(8,128)}), f32[32,72,128]{2,1,0:T(8,128)S(1)}, u32[]{:S(2)}, u32[]{:S(2)}) %all-to-all-start.5) | async-done | bytes 1179680 | tf_op jit(solution)/shard_map/all_to_all | solution.py:929
  234.0 15.4 %all-to-all-done.3.refs_1_ = f32[32,72,128]{2,1,0:T(8,128)S(1)} async-done(((f32[32,72,128]{2,1,0:T(8,128)}), f32[32,72,128]{2,1,0:T(8,128)S(1)}, u32[]{:S(2)}, u32[]{:S(2)}) %all-to-all-start.3) | async-done | bytes 1179680 | tf_op jit(solution)/shard_map/all_to_all | solution.py:929
  250.6 17.4 %shard_map.137 = (f32[4,64,2048]{2,1,0:T(8,128)}, f32[4,8,2048]{2,1,0:T(8,128)}, f32[4,64,2048]{2,1,0:T(8,128)}, f32[8,128]{1,0:T(8,128)}, f32[4,8,64,128]{3,2,1,0:T(8,128)}, /*index=5*/bf16[512,2048]{1,0:T(8,128)(2,1)}) custom-call(f32[4,4]{1,0:T(4,128)} %refs_0_.7, f32[32,72,128]{2,1,0:T(8,128)} %copy-done.19, bf16[2048,2048]{1,0:T(8,128)(2,1)} %refs_2_.7, ...), custom_call_target="tpu_custom_call" | custom-call | tf_op jit(solution)/shard_map/pallas_call | solution.py:607
  278.3 19.6 %all-to-all-done.8 = f32[32,64,128]{2,1,0:T(8,128)S(1)} async-done(((f32[32,64,128]{2,1,0:T(8,128)}), f32[32,64,128]{2,1,0:T(8,128)S(1)}, u32[]{:S(2)}, u32[]{:S(2)}) %all-to-all-start.8) | async-done | bytes 1048608 | tf_op jit(solution)/shard_map/all_to_all | solution.py:926
  314.2 13.5 %all-to-all-done.6 = f32[32,64,128]{2,1,0:T(8,128)S(1)} async-done(((f32[32,64,128]{2,1,0:T(8,128)}), f32[32,64,128]{2,1,0:T(8,128)S(1)}, u32[]{:S(2)}, u32[]{:S(2)}) %all-to-all-start.6) | async-done | bytes 1048608 | tf_op jit(solution)/shard_map/all_to_all | solution.py:926
  332.4 11.7 %shard_map.139 = f32[32,72,128]{2,1,0:T(8,128)} custom-call(f32[2048,128]{1,0:T(8,128)} %bitcast.115, f32[8,128]{1,0:T(8,128)} %broadcast_1_aux_ref.2.aux_ref, bf16[2048,2048]{1,0:T(8,128)(2,1)} %bitcast.93, bf16[2048,2048]{1,0:T(8,128)(2,1)} %back_ref.15, f32[2048,1]{1,0:T(8,128)} %copy.246.along_ref, f32[1,128]{1,0:T(1,128)} %get-tuple-element.105.other_ref), custom_call_target="tpu_custom_call" | custom-call | tf_op jit(solution)/shard_map/pallas_call | solution.py:384
  344.1 16.3 %all-to-all-done.9.got_ref = f32[32,72,128]{2,1,0:T(8,128)S(1)} async-done(((f32[32,72,128]{2,1,0:T(8,128)}), f32[32,72,128]{2,1,0:T(8,128)S(1)}, u32[]{:S(2)}, u32[]{:S(2)}) %all-to-all-start.9) | async-done | bytes 1179680 | tf_op jit(solution)/shard_map/all_to_all | solution.py:929
  377.5 15.8 %all-to-all-done.7.refs_1_ = f32[32,72,128]{2,1,0:T(8,128)S(1)} async-done(((f32[32,72,128]{2,1,0:T(8,128)}), f32[32,72,128]{2,1,0:T(8,128)S(1)}, u32[]{:S(2)}, u32[]{:S(2)}) %all-to-all-start.7) | async-done | bytes 1179680 | tf_op jit(solution)/shard_map/all_to_all | solution.py:929
  394.3 18.0 %shard_map.142 = (f32[4,64,2048]{2,1,0:T(8,128)}, f32[4,8,2048]{2,1,0:T(8,128)}, f32[4,64,2048]{2,1,0:T(8,128)}, f32[8,128]{1,0:T(8,128)}, f32[4,64,2048]{2,1,0:...) custom-call(f32[4,4]{1,0:T(4,128)} %refs_0_.7, f32[32,72,128]{2,1,0:T(8,128)} %copy-done.21, ...), custom_call_target="tpu_custom_call" | custom-call | tf_op jit(solution)/shard_map/pallas_call | solution.py:607
  422.7 19.5 %all-to-all-done.12 = f32[32,64,128]{2,1,0:T(8,128)S(1)} async-done(((f32[32,64,128]{2,1,0:T(8,128)}), f32[32,64,128]{2,1,0:T(8,128)S(1)}, u32[]{:S(2)}, u32[]{:S(2)}) %all-to-all-start.12) | async-done | bytes 1048608 | tf_op jit(solution)/shard_map/all_to_all | solution.py:926
  458.5 13.6 %all-to-all-done.10 = f32[32,64,128]{2,1,0:T(8,128)S(1)} async-done(((f32[32,64,128]{2,1,0:T(8,128)}), f32[32,64,128]{2,1,0:T(8,128)S(1)}, u32[]{:S(2)}, u32[]{:S(2)}) %all-to-all-start.10) | async-done | bytes 1048608 | tf_op jit(solution)/shard_map/all_to_all | solution.py:926
  488.4 16.3 %all-to-all-done.13.got_ref = f32[32,72,128]{2,1,0:T(8,128)S(1)} async-done(((f32[32,72,128]{2,1,0:T(8,128)}), f32[32,72,128]{2,1,0:T(8,128)S(1)}, u32[]{:S(2)}, u32[]{:S(2)}) %all-to-all-start.13) | async-done | bytes 1179680 | tf_op jit(solution)/shard_map/all_to_all | solution.py:929
  523.7 13.8 %all-to-all-done.11.refs_1_ = f32[32,72,128]{2,1,0:T(8,128)} async-done(((f32[32,72,128]{2,1,0:T(8,128)}), f32[32,72,128]{2,1,0:T(8,128)}, u32[]{:S(2)}, u32[]{:S(2)}) %all-to-all-start.11) | async-done | bytes 1179680 | tf_op jit(solution)/shard_map/all_to_all | solution.py:929
  538.1 18.6 %shard_map.147 = (f32[4,64,2048]{2,1,0:T(8,128)}, f32[4,8,2048]{2,1,0:T(8,128)}, f32[4,64,2048]{2,1,0:T(8,128)}, f32[8,128]{1,0:T(8,128)}, f32[4,64,2048]{2,1,0:...) custom-call(f32[4,4]{1,0:T(4,128)} %refs_0_.7, ...), custom_call_target="tpu_custom_call" | custom-call | tf_op jit(solution)/shard_map/pallas_call | solution.py:607
  567.1 19.6 %all-to-all-done.16 = f32[32,64,128]{2,1,0:T(8,128)S(1)} async-done(((f32[32,64,128]{2,1,0:T(8,128)}), f32[32,64,128]{2,1,0:T(8,128)S(1)}, u32[]{:S(2)}, u32[]{:S(2)}) %all-to-all-start.16) | async-done | bytes 1048608 | tf_op jit(solution)/shard_map/all_to_all | solution.py:926
  603.9 13.6 %all-to-all-done.14 = f32[32,64,128]{2,1,0:T(8,128)S(1)} async-done(((f32[32,64,128]{2,1,0:T(8,128)}), f32[32,64,128]{2,1,0:T(8,128)S(1)}, u32[]{:S(2)}, u32[]{:S(2)}) %all-to-all-start.14) | async-done | bytes 1048608 | tf_op jit(solution)/shard_map/all_to_all | solution.py:926
  623.5 11.7 %shard_map.149 = f32[32,72,128]{2,1,0:T(8,128)} custom-call(f32[2048,128]{1,0:T(8,128)} %bitcast.112, f32[8,128]{1,0:T(8,128)} %broadcast_1_aux_ref.2.aux_ref, bf16[2048,2048]{1,0:T(8,128)(2,1)} %bitcast.97, bf16[2048,2048]{1,0:T(8,128)(2,1)} %back_ref.15, f32[2048,1]{1,0:T(8,128)} %copy.246.along_ref, f32[1,128]{1,0:T(1,128)} %get-tuple-element.105.other_ref), custom_call_target="tpu_custom_call" | custom-call | tf_op jit(solution)/shard_map/pallas_call | solution.py:384
  635.2 16.1 %all-to-all-done.17.got_ref = f32[32,72,128]{2,1,0:T(8,128)S(1)} async-done(((f32[32,72,128]{2,1,0:T(8,128)}), f32[32,72,128]{2,1,0:T(8,128)S(1)}, u32[]{:S(2)}, u32[]{:S(2)}) %all-to-all-start.17) | async-done | bytes 1179680 | tf_op jit(solution)/shard_map/all_to_all | solution.py:929
  671.1 13.1 %all-to-all-done.15.refs_1_ = f32[32,72,128]{2,1,0:T(8,128)} async-done(((f32[32,72,128]{2,1,0:T(8,128)}), f32[32,72,128]{2,1,0:T(8,128)}, u32[]{:S(2)}, u32[]{:S(2)}) %all-to-all-start.15) | async-done | bytes 1179680 | tf_op jit(solution)/shard_map/all_to_all | solution.py:929
  684.8 15.0 %shard_map.152 = (f32[4,64,2048]{2,1,0:T(8,128)}, f32[4,8,2048]{2,1,0:T(8,128)}, f32[4,64,2048]{2,1,0:T(8,128)}, f32[8,128]{1,0:T(8,128)}, f32[4,64,2048]{2,1,0:T(8,128)}, /*index=5*/f32[4,8,2048]{2,1,0:T(8,128)}) custom-call(f32[4,4]{1,0:T(4,128)} %refs_0_.7, f32[32,72,128]{2,1,0:T(8,128)} %all-to-all-done.15.refs_1_, bf16[2048,2048]{1,0:T(8,128)(2,1)} %refs_2_.7, ...), custom_call_target="tpu_custom_call" | custom-call | tf_op jit(solution)/shard_map/pallas_call | solution.py:607
  727.9 24.2 %all-to-all-done.19.own_ref.previous_ref.next_ref = f32[4,4,64,512]{3,2,1,0:T(8,128)S(1)} async-done(((f32[4,4,64,512]{3,2,1,0:T(8,128)}), f32[4,4,64,512]{3,2,1,0:T(8,128)S(1)}, u32[]{:S(2)}, u32[]{:S(2)}) %all-to-all-start.19) | async-done | bytes 2097184 | tf_op jit(solution)/shard_map/all_to_all | solution.py:970
  (214 shorter events, 365.0 us)
Async XLA Ops:
  7.8 30.9 %collective-permute-start = (f32[5,3,4,512]{3,1,2,0:T(4,128)}, f32[5,3,4,512]{3,1,2,0:T(4,128)S(1)}, u32[]{:S(2)}, u32[]{:S(2)}) collective-permute-start(f32[5,3,4,512]{3,1,2,0:T(4,128)} %pad_maximum_fusion), channel_id=1, source_target_pairs={{0,4},{4,8},{8,12},{12,16},{16,20},{20,24},{24,28},{1,5},{5,9},{9,... | collective-permute-start | bytes 368648 | tf_op jit(solution)/shard_map/ppermute | solution.py:754
  11.7 26.7 %collective-permute-start.1 = (f32[5,3,4,512]{3,1,2,0:T(4,128)}, f32[5,3,4,512]{3,1,2,0:T(4,128)S(1)}, u32[]{:S(2)}, u32[]{:S(2)}) collective-permute-start(f32[5,3,4,512]{3,1,2,0:T(4,128)} %pad_maximum_fusion.1), channel_id=1, source_target_pairs={{4,0},{8,4},{12,8},{16,12},{20,16},{24,20},{28,24},{5,1},{9,5},{13... | collective-permute-start | bytes 368648 | tf_op jit(solution)/shard_map/ppermute | solution.py:754
  16.3 71.4 %all-to-all-start = ((f32[4,4,64,512]{3,2,1,0:T(8,128)}), f32[4,4,64,512]{3,2,1,0:T(8,128)}, u32[]{:S(2)}, u32[]{:S(2)}) async-start(f32[4,4,64,512]{3,2,1,0:T(8,128)} %bitcast.108), calls=%async_computation | async-start | bytes 4194304 | tf_op jit(solution)/shard_map/all_to_all | solution.py:898
  87.7 27.3 %all-to-all-start.1 = ((f32[4,4,64,512]{3,2,1,0:T(8,128)}), f32[4,4,64,512]{3,2,1,0:T(8,128)S(1)}, u32[]{:S(2)}, u32[]{:S(2)}) async-start(f32[4,4,64,512]{3,2,1,0:T(8,128)} %get-tuple-element.37), calls=%async_computation.1 | async-start | bytes 4194304 | tf_op jit(solution)/shard_map/all_to_all | solution.py:900
  123.9 30.3 %all-to-all-start.4 = ((f32[32,64,128]{2,1,0:T(8,128)}), f32[32,64,128]{2,1,0:T(8,128)S(1)}, u32[]{:S(2)}, u32[]{:S(2)}) async-start(f32[32,64,128]{2,1,0:T(8,128)} %bitcast.125), calls=%async_computation.4 | async-start | bytes 2097152 | tf_op jit(solution)/shard_map/all_to_all | solution.py:926
  154.3 29.9 %all-to-all-start.2 = ((f32[32,64,128]{2,1,0:T(8,128)}), f32[32,64,128]{2,1,0:T(8,128)S(1)}, u32[]{:S(2)}, u32[]{:S(2)}) async-start(f32[32,64,128]{2,1,0:T(8,128)} %bitcast.118), calls=%async_computation.2 | async-start | bytes 2097152 | tf_op jit(solution)/shard_map/all_to_all | solution.py:926
  184.1 32.6 %all-to-all-start.5 = ((f32[32,72,128]{2,1,0:T(8,128)}), f32[32,72,128]{2,1,0:T(8,128)S(1)}, u32[]{:S(2)}, u32[]{:S(2)}) async-start(f32[32,72,128]{2,1,0:T(8,128)} %shard_map.135), calls=%async_computation.5 | async-start | bytes 2359296 | tf_op jit(solution)/shard_map/all_to_all | solution.py:929
  216.8 32.7 %all-to-all-start.3 = ((f32[32,72,128]{2,1,0:T(8,128)}), f32[32,72,128]{2,1,0:T(8,128)S(1)}, u32[]{:S(2)}, u32[]{:S(2)}) async-start(f32[32,72,128]{2,1,0:T(8,128)} %shard_map.134), calls=%async_computation.3 | async-start | bytes 2359296 | tf_op jit(solution)/shard_map/all_to_all | solution.py:929
  268.0 29.9 %all-to-all-start.8 = ((f32[32,64,128]{2,1,0:T(8,128)}), f32[32,64,128]{2,1,0:T(8,128)S(1)}, u32[]{:S(2)}, u32[]{:S(2)}) async-start(f32[32,64,128]{2,1,0:T(8,128)} %bitcast.124), calls=%async_computation.8 | async-start | bytes 2097152 | tf_op jit(solution)/shard_map/all_to_all | solution.py:926
  297.9 29.9 %all-to-all-start.6 = ((f32[32,64,128]{2,1,0:T(8,128)}), f32[32,64,128]{2,1,0:T(8,128)S(1)}, u32[]{:S(2)}, u32[]{:S(2)}) async-start(f32[32,64,128]{2,1,0:T(8,128)} %bitcast.120), calls=%async_computation.6 | async-start | bytes 2097152 | tf_op jit(solution)/shard_map/all_to_all | solution.py:926
  327.7 32.6 %all-to-all-start.9 = ((f32[32,72,128]{2,1,0:T(8,128)}), f32[32,72,128]{2,1,0:T(8,128)S(1)}, u32[]{:S(2)}, u32[]{:S(2)}) async-start(f32[32,72,128]{2,1,0:T(8,128)} %shard_map.140), calls=%async_computation.9 | async-start | bytes 2359296 | tf_op jit(solution)/shard_map/all_to_all | solution.py:929
  360.4 32.9 %all-to-all-start.7 = ((f32[32,72,128]{2,1,0:T(8,128)}), f32[32,72,128]{2,1,0:T(8,128)S(1)}, u32[]{:S(2)}, u32[]{:S(2)}) async-start(f32[32,72,128]{2,1,0:T(8,128)} %shard_map.139), calls=%async_computation.7 | async-start | bytes 2359296 | tf_op jit(solution)/shard_map/all_to_all | solution.py:929
  412.3 29.9 %all-to-all-start.12 = ((f32[32,64,128]{2,1,0:T(8,128)}), f32[32,64,128]{2,1,0:T(8,128)S(1)}, u32[]{:S(2)}, u32[]{:S(2)}) async-start(f32[32,64,128]{2,1,0:T(8,128)} %bitcast.123), calls=%async_computation.12 | async-start | bytes 2097152 | tf_op jit(solution)/shard_map/all_to_all | solution.py:926
  442.2 29.9 %all-to-all-start.10 = ((f32[32,64,128]{2,1,0:T(8,128)}), f32[32,64,128]{2,1,0:T(8,128)S(1)}, u32[]{:S(2)}, u32[]{:S(2)}) async-start(f32[32,64,128]{2,1,0:T(8,128)} %bitcast.121), calls=%async_computation.10 | async-start | bytes 2097152 | tf_op jit(solution)/shard_map/all_to_all | solution.py:926
  472.1 32.6 %all-to-all-start.13 = ((f32[32,72,128]{2,1,0:T(8,128)}), f32[32,72,128]{2,1,0:T(8,128)S(1)}, u32[]{:S(2)}, u32[]{:S(2)}) async-start(f32[32,72,128]{2,1,0:T(8,128)} %shard_map.145), calls=%async_computation.13 | async-start | bytes 2359296 | tf_op jit(solution)/shard_map/all_to_all | solution.py:929
  504.7 32.8 %all-to-all-start.11 = ((f32[32,72,128]{2,1,0:T(8,128)}), f32[32,72,128]{2,1,0:T(8,128)}, u32[]{:S(2)}, u32[]{:S(2)}) async-start(f32[32,72,128]{2,1,0:T(8,128)} %shard_map.144), calls=%async_computation.11 | async-start | bytes 2359296 | tf_op jit(solution)/shard_map/all_to_all | solution.py:929
  556.7 29.9 %all-to-all-start.16 = ((f32[32,64,128]{2,1,0:T(8,128)}), f32[32,64,128]{2,1,0:T(8,128)S(1)}, u32[]{:S(2)}, u32[]{:S(2)}) async-start(f32[32,64,128]{2,1,0:T(8,128)} %bitcast.122), calls=%async_computation.16 | async-start | bytes 2097152 | tf_op jit(solution)/shard_map/all_to_all | solution.py:926
  587.6 29.9 %all-to-all-start.14 = ((f32[32,64,128]{2,1,0:T(8,128)}), f32[32,64,128]{2,1,0:T(8,128)S(1)}, u32[]{:S(2)}, u32[]{:S(2)}) async-start(f32[32,64,128]{2,1,0:T(8,128)} %bitcast.119), calls=%async_computation.14 | async-start | bytes 2097152 | tf_op jit(solution)/shard_map/all_to_all | solution.py:926
  618.5 32.9 %all-to-all-start.17 = ((f32[32,72,128]{2,1,0:T(8,128)}), f32[32,72,128]{2,1,0:T(8,128)S(1)}, u32[]{:S(2)}, u32[]{:S(2)}) async-start(f32[32,72,128]{2,1,0:T(8,128)} %shard_map.150), calls=%async_computation.17 | async-start | bytes 2359296 | tf_op jit(solution)/shard_map/all_to_all | solution.py:929
  651.4 32.8 %all-to-all-start.15 = ((f32[32,72,128]{2,1,0:T(8,128)}), f32[32,72,128]{2,1,0:T(8,128)}, u32[]{:S(2)}, u32[]{:S(2)}) async-start(f32[32,72,128]{2,1,0:T(8,128)} %shard_map.149), calls=%async_computation.15 | async-start | bytes 2359296 | tf_op jit(solution)/shard_map/all_to_all | solution.py:929
  701.1 10.8 %all-to-all-start.18 = ((f32[32,8,128]{2,1,0:T(8,128)}), f32[32,8,128]{2,1,0:T(8,128)S(1)}, u32[]{:S(2)}, u32[]{:S(2)}) async-start(f32[32,8,128]{2,1,0:T(8,128)} %broadcast_in_dim.114), calls=%async_computation.18 | async-start | bytes 262144 | tf_op jit(solution)/shard_map/all_to_all | solution.py:967
  722.3 29.7 %all-to-all-start.19 = ((f32[4,4,64,512]{3,2,1,0:T(8,128)}), f32[4,4,64,512]{3,2,1,0:T(8,128)S(1)}, u32[]{:S(2)}, u32[]{:S(2)}) async-start(f32[4,4,64,512]{3,2,1,0:T(8,128)} %shard_map.153), calls=%async_computation.19 | async-start | bytes 4194304 | tf_op jit(solution)/shard_map/all_to_all | solution.py:970
  752.1 16.0 %collective-permute-start.4 = (f32[4,1,512]{2,1,0:T(1,128)S(1)}, f32[4,1,512]{2,1,0:T(1,128)S(1)}, u32[]{:S(2)}, u32[]{:S(2)}) collective-permute-start(f32[4,1,512]{2,1,0:T(1,128)S(1)} %get-tuple-element.83), channel_id=1, source_target_pairs={{0,4},{4,8},{8,12},{12,16},{16,20},{20,24},{24,28},{1,5},{5,9},{9,... | collective-permute-start | bytes 24584 | tf_op jit(solution)/shard_map/ppermute | solution.py:754
  754.4 13.7 %collective-permute-start.5 = (f32[4,1,512]{2,1,0:T(1,128)S(1)}, f32[4,1,512]{2,1,0:T(1,128)S(1)}, u32[]{:S(2)}, u32[]{:S(2)}) collective-permute-start(f32[4,1,512]{2,1,0:T(1,128)S(1)} %get-tuple-element.82), channel_id=1, source_target_pairs={{4,0},{8,4},{12,8},{16,12},{20,16},{24,20},{28,24},{5,1},{9,5},{13... | collective-permute-start | bytes 24584 | tf_op jit(solution)/shard_map/ppermute | solution.py:754
  (42 other events, 289.9 us)

commit v5 on v4

--- a/solution.py
+++ b/solution.py
@@ -149,7 +149,7 @@
 
 
 def start_kernel(
-    block, mix_ref, field_ref, basis_ref, kept_ref, out_ref, lines_ref,
+    block, mix_ref, field_ref, basis_ref, kept_ref, out_ref,
     field, basis, lines, sent, semaphores, basis_semaphores, out_semaphores,
 ):
     pieces, planes, rows, span = field_ref.shape
@@ -161,11 +161,8 @@
     kept = pltpu.make_async_copy(field, kept_ref, semaphores.at[pieces])
     kept.start()
     mix_planes(lambda k, i, j: field[k, i, j], mix_ref, lines, rows)
-    mixed = pltpu.make_async_copy(lines, lines_ref, semaphores.at[pieces + 1])
-    mixed.start()
     send_lines(lines, basis, sent, out_ref, block, 0, out_semaphores, stream)
     kept.wait()
-    mixed.wait()
 
 
 def start_lines(field, basis_z, basis_y, columns, chunks):
@@ -177,18 +174,17 @@
     return pl.pallas_call(
         functools.partial(start_kernel, block),
         in_specs=[scalar, anywhere, anywhere],
-        out_specs=[anywhere] * 3,
+        out_specs=[anywhere] * 2,
         out_shape=[
             jax.ShapeDtypeStruct((planes, rows, full), jnp.float32),
             jax.ShapeDtypeStruct(sent, jnp.float32),
-            jax.ShapeDtypeStruct((2 * planes * rows, full), jnp.bfloat16),
         ],
         scratch_shapes=[
             pltpu.VMEM((planes, rows, full), jnp.float32),
             pltpu.VMEM(basis_y.shape, jnp.bfloat16),
             pltpu.VMEM((2 * planes * rows, full), jnp.bfloat16),
             pltpu.VMEM(sent, jnp.float32),
-            pltpu.SemaphoreType.DMA((pieces + 2,)),
+            pltpu.SemaphoreType.DMA((pieces + 1,)),
             pltpu.SemaphoreType.DMA((blocks, 1)),
             pltpu.SemaphoreType.DMA((blocks, 1)),
         ],
@@ -196,35 +192,39 @@
     )(basis_z, field, basis_y)
 
 
-def more_kernel(block, chunk, lines_ref, basis_ref, out_ref, basis, lines, sent, semaphore, basis_semaphores, out_semaphores):
-    given = pltpu.make_async_copy(lines_ref, lines, semaphore)
+def more_kernel(
+    block, chunk, mix_ref, field_ref, basis_ref, out_ref, field, basis, lines, sent, semaphore, basis_semaphores, out_semaphores
+):
+    given = pltpu.make_async_copy(field_ref, field, semaphore)
     given.start()
     stream = column_stream(basis_ref, basis, block, chunk, basis_semaphores.shape[0], basis_semaphores)
     stream.begin()
     given.wait()
+    mix_planes(lambda k, i, j: field[k, i, j], mix_ref, lines, field.shape[1])
     send_lines(lines, basis, sent, out_ref, block, chunk, out_semaphores, stream)
 
 
-def more_lines(lines, basis_y, planes, rows, columns, chunks, chunk):
-    full = lines.shape[1]
+def more_lines(field, basis_z, basis_y, columns, chunks, chunk):
+    planes, rows, full = field.shape
     block = min(256, full // chunks)
     blocks = full // chunks // block
     sent = (planes, full // chunks // columns, rows, columns)
     return pl.pallas_call(
         functools.partial(more_kernel, block, chunk),
-        in_specs=[anywhere, anywhere],
+        in_specs=[scalar, anywhere, anywhere],
         out_specs=anywhere,
         out_shape=jax.ShapeDtypeStruct(sent, jnp.float32),
         scratch_shapes=[
+            pltpu.VMEM(field.shape, jnp.float32),
             pltpu.VMEM(basis_y.shape, jnp.bfloat16),
-            pltpu.VMEM(lines.shape, jnp.bfloat16),
+            pltpu.VMEM((2 * planes * rows, full), jnp.bfloat16),
             pltpu.VMEM(sent, jnp.float32),
             pltpu.SemaphoreType.DMA,
             pltpu.SemaphoreType.DMA((blocks, 1)),
             pltpu.SemaphoreType.DMA((blocks, 1)),
         ],
         compiler_params=params(),
-    )(lines, basis_y)
+    )(basis_z, field, basis_y)
 
 
 def take_lines(got, lines, planes, rows):
@@ -246,29 +246,81 @@
         lines[half + main :, lanes] = low
 
 
-def part_kernel(planes, rows, block, got_ref, basis_ref, out_ref, got, basis, lines, out, given_semaphores, semaphores, out_semaphores):
+def mixed_back(result, mix_ref, k, rows):
+    planes = mix_ref.shape[0]
+    main = planes * rows
+    value = result[:rows] * mix_ref[k, 0]
+    edge = result[main : main + spare] * mix_ref[k, 0]
+    for m in range(1, planes):
+        value = value + result[m * rows : (m + 1) * rows] * mix_ref[k, m]
+        edge = edge + result[main + m * spare : main + (m + 1) * spare] * mix_ref[k, m]
+    return value, edge
+
+
+def part_kernel(stage, rows, block, *refs):
+    refs = list(refs)
+    take = lambda: refs.pop(0)
+    mix_ref, got_ref, basis_ref = take(), take(), take()
+    if stage >= 1:
+        scalars_ref, old_z, old_edge_z = take(), take(), take()
+    if stage >= 2:
+        old_v, old_edge_v = take(), take()
+    out_refs = [take() for _ in range(4 if stage >= 1 else 2)]
+    got, basis, lines = take(), take(), take()
+    outs = [take() for _ in range(4 if stage >= 1 else 2)]
+    given_semaphores, semaphores, out_semaphores = take(), take(), take()
+    z, edge_z = outs[:2]
+    planes = mix_ref.shape[0]
     parts = got.shape[0] // planes
     width = lines.shape[1]
     half = planes * (rows + spare)
     blocks = basis.shape[0] // block
     groups = [slice(m * parts, (m + 1) * parts) for m in range(planes)]
     given = start_all([(got_ref.at[group], got.at[group]) for group in groups], given_semaphores)
-    stream = Stream(
-        lambda n: [(basis_ref.at[piece(n, block), :width], basis.at[piece(n, block)])], blocks, semaphores
-    )
-    sink = Stream(
-        lambda n: [(out.at[:, piece(n, block)], out_ref.at[:, piece(n, block)])], blocks, out_semaphores
-    )
+    fields = []
+    if stage >= 1:
+        v, edge_v = outs[2:]
+        fields += [(old_z, z), (old_edge_z, edge_z)]
+    if stage >= 2:
+        fields += [(old_v, v), (old_edge_v, edge_v)]
+
+    def needed(n):
+        own = piece(n, block)
+        pairs = [(basis_ref.at[own, :width], basis.at[own])]
+        return pairs + [(old.at[:, :, own], target.at[:, :, own]) for old, target in fields]
+
+    def made(n):
+        own = piece(n, block)
+        return [(out.at[:, :, own], out_ref.at[:, :, own]) for out, out_ref in zip(outs, out_refs)]
+
+    stream = Stream(needed, blocks, semaphores)
+    sink = Stream(made, blocks, out_semaphores)
     stream.begin()
     wait_all(given)
     take_lines(got, lines, planes, rows)
 
     def step(n, carry):
         stream.take(n)
+        lanes = piece(n, block)
         result = lax.dot_general(
-            lines[...], basis[piece(n, block), :], (((1,), (1,)), ((), ())), preferred_element_type=jnp.float32
+            lines[...], basis[lanes, :], (((1,), (1,)), ((), ())), preferred_element_type=jnp.float32
         )
-        out[:, piece(n, block)] = result[:half] + result[half:]
+        result = result[:half] + result[half:]
+        if stage >= 1:
+            length = scalars_ref[2:3, 0:1]
+            turn = scalars_ref[3:4, 0:1]
+        for k in range(planes):
+            value, edge = mixed_back(result, mix_ref, k, rows)
+            if stage >= 1:
+                if stage >= 2:
+                    value = value + turn * v[k, :, lanes]
+                    edge = edge + turn * edge_v[k, :, lanes]
+                v[k, :, lanes] = value
+                edge_v[k, :, lanes] = edge
+                value = z[k, :, lanes] - length * value
+                edge = edge_z[k, :, lanes] - length * edge
+            z[k, :, lanes] = value
+            edge_z[k, :, lanes] = edge
         sink.start(n)
         return carry
 
@@ -276,26 +328,42 @@
     sink.end()
 
 
-def part_lines(got, basis_y, planes, rows, chunks):
+def part_lines(stage, got, basis_z, basis_y, rows, chunks, state):
+    planes = basis_z.shape[0]
     full = basis_y.shape[0]
     block = min(256, full)
     half = planes * (rows + spare)
-    return pl.pallas_call(
-        functools.partial(part_kernel, planes, rows, block),
-        in_specs=[anywhere, anywhere],
-        out_specs=anywhere,
-        out_shape=jax.ShapeDtypeStruct((half, full), jnp.float32),
+    field, edge = (planes, rows, full), (planes, spare, full)
+    names = ["z", "edge_z"]
+    given = [basis_z, got, basis_y]
+    specs = [scalar, anywhere, anywhere]
+    if stage >= 1:
+        names += ["v", "edge_v"]
+        given += [state["scalars"], state["z"], state["edge_z"]]
+        specs += [vector, anywhere, anywhere]
+    if stage >= 2:
+        given += [state["v"], state["edge_v"]]
+        specs += [anywhere, anywhere]
+    shapes = [field, edge] * (len(names) // 2)
+    results = pl.pallas_call(
+        functools.partial(part_kernel, stage, rows, block),
+        in_specs=specs,
+        out_specs=[anywhere] * len(names),
+        out_shape=[jax.ShapeDtypeStruct(shape, jnp.float32) for shape in shapes],
         scratch_shapes=[
             pltpu.VMEM(got.shape, jnp.float32),
             pltpu.VMEM((full, full // chunks), jnp.bfloat16),
             pltpu.VMEM((2 * half, full // chunks), jnp.bfloat16),
-            pltpu.VMEM((half, full), jnp.float32),
+        ]
+        + [pltpu.VMEM(shape, jnp.float32) for shape in shapes]
+        + [
             pltpu.SemaphoreType.DMA((planes,)),
-            pltpu.SemaphoreType.DMA((full // block, 1)),
-            pltpu.SemaphoreType.DMA((full // block, 1)),
+            pltpu.SemaphoreType.DMA((full // block, 5)),
+            pltpu.SemaphoreType.DMA((full // block, 4)),
         ],
         compiler_params=params(),
-    )(got, basis_y)
+    )(*given)
+    return dict(zip(names, results))
 
 
 def column_kernel(
@@ -405,24 +473,28 @@
     refs = list(refs)
     take = lambda: refs.pop(0)
     mix_ref, got_ref, basis_ref = take(), take(), take()
-    part_ref = take() if chunks > 1 else None
+    has_z = stage >= 1 or chunks > 1
+    has_v = stage >= 2 or (stage >= 1 and chunks > 1)
     diagonal_ref, low_x, high_x, low_y, high_y = take(), take(), take(), take(), take()
-    residual_ref = take()
-    if stage >= 1:
-        old_z, old_edge_z, scalars_ref = take(), take(), take()
-    if stage >= 2:
+    residual_ref = take() if last else None
+    scalars_ref = take() if stage >= 1 else None
+    if has_z:
+        old_z, old_edge_z = take(), take()
+    if has_v:
         old_v, old_edge_v = take(), take()
-    z_ref, edge_z_ref, y_ref, aux_ref = take(), take(), take(), take()
+    z_ref, edge_z_ref, y_ref = take(), take(), take()
+    aux_ref = take() if last else None
     if stage >= 1:
         v_ref, edge_v_ref = take(), take()
     if not last:
-        out_ref, lines_ref = take(), take()
-    got, basis, diagonal, lines, around, edge_z, image, residual = [take() for _ in range(8)]
+        out_ref = take()
+    got, basis, diagonal, lines, around, edge_z, image = [take() for _ in range(7)]
+    residual = take() if last else None
+    z = take() if has_z else None
     if stage >= 1:
-        z, v, edge_v = take(), take(), take()
+        v, edge_v = take(), take()
     if not last:
         ahead_lines, sent = take(), take()
-    part = take() if chunks > 1 else None
     given_semaphores, semaphores, late_semaphores = take(), take(), take()
     if not last:
         basis_semaphores, out_semaphores = take(), take()
@@ -436,17 +508,15 @@
     given = start_all([(got_ref.at[group], got.at[group]) for group in groups], given_semaphores)
     width = full // chunks
     turned = slice(full - width, full)
-    fields = [(residual_ref, residual)]
-    if stage >= 1:
+    fields = [(residual_ref, residual)] if last else []
+    if has_z:
         fields += [(old_z, z), (old_edge_z, edge_z)]
-    if stage >= 2:
+    if has_v:
         fields += [(old_v, v), (old_edge_v, edge_v)]
 
     def needed(n):
         own = piece(n, block)
         pairs = [(basis_ref.at[own, turned], basis.at[own, turned])]
-        if chunks > 1:
-            pairs.append((part_ref.at[:, own], part.at[:, own]))
         return pairs + [(old.at[:, :, own], target.at[:, :, own]) for old, target in fields]
 
     stream = Stream(needed, blocks, semaphores)
@@ -466,18 +536,19 @@
             lines[...], basis[lanes, turned], (((1,), (1,)), ((), ())), preferred_element_type=jnp.float32
         )
         result = result[:half] + result[half:]
-        if chunks > 1:
-            result = result + part[:, lanes]
         if stage >= 1:
             length = scalars_ref[2:3, 0:1]
             turn = scalars_ref[3:4, 0:1]
         for k in range(planes):
-            value = result[:rows] * mix_ref[k, 0]
-            edge = result[main : main + spare] * mix_ref[k, 0]
-            for m in range(1, planes):
-                value = value + result[m * rows : (m + 1) * rows] * mix_ref[k, m]
-                edge = edge + result[main + m * spare : main + (m + 1) * spare] * mix_ref[k, m]
-            if stage >= 1:
+            value, edge = mixed_back(result, mix_ref, k, rows)
+            if chunks > 1:
+                scale = 1.0 if stage == 0 else -length
+                if stage >= 1:
+                    v[k, :, lanes] = v[k, :, lanes] + value
+                    edge_v[k, :, lanes] = edge_v[k, :, lanes] + edge
+                value = z[k, :, lanes] + scale * value
+                edge = edge_z[k, :, lanes] + scale * edge
+            elif stage >= 1:
                 if stage >= 2:
                     value = value + turn * v[k, :, lanes]
                     edge = edge + turn * edge_v[k, :, lanes]
@@ -486,9 +557,10 @@
                 value = z[k, :, lanes] - length * value
                 edge = edge_z[k, :, lanes] - length * edge
             edge_z[k, :, lanes] = edge
-            shared = fold(residual[k, :, lanes] * value)
-            for start in range(0, rows, 8):
-                carry = carry + shared[start : start + 8]
+            if last:
+                shared = fold(residual[k, :, lanes] * value)
+                for start in range(0, rows, 8):
+                    carry = carry + shared[start : start + 8]
             around[k, spare : spare + rows, lanes] = value
             around[k, spare - 1 : spare, lanes] = edge[0:1]
             around[k, spare + rows : spare + rows + 1, lanes] = edge[1:2]
@@ -526,26 +598,18 @@
         total = total + (low_y[...] * (value - left) - high_y[...] * (right - value))
         total = total + (2.0 * value - before - after)
         image[k, own, :] = total
-        return carry + fold(value * total)
+        return carry + fold(value * total) if last else carry
 
     bend = lax.fori_loop(0, planes * (rows // 8), operate, nothing, unroll=2)
-    aux_ref[...] = jnp.concatenate(
-        [
-            nothing[:2],
-            jnp.sum(product, axis=0, keepdims=True),
-            jnp.sum(bend, axis=0, keepdims=True),
-            nothing[4:],
-        ],
-        axis=0,
-    )
+    if last:
+        product = jnp.sum(product, axis=0, keepdims=True)
+        bend = jnp.sum(bend, axis=0, keepdims=True)
+        aux_ref[...] = jnp.concatenate([nothing[:2], product, bend, nothing[4:]], axis=0)
     image_copy = pltpu.make_async_copy(image, y_ref, late_semaphores.at[1])
     image_copy.start()
     if not last:
         mix_planes(lambda k, i, j: image[k, i, j], mix_ref, ahead_lines, rows)
-        mixed = pltpu.make_async_copy(ahead_lines, lines_ref, late_semaphores.at[6])
-        mixed.start()
         send_lines(ahead_lines, basis, sent, out_ref, block, 0, out_semaphores, ahead)
-        mixed.wait()
     image_copy.wait()
     wait_all(done)
 
@@ -553,23 +617,30 @@
 def turn_lines(stage, last, got, part, operator, basis_z, basis_y, state, chunks):
     planes, rows, full = operator[0].shape
     _, _, columns = got.shape
-    block = min(256, full // chunks)
+    block = min(512, full // chunks)
     blocks = full // block
     field_shape = jax.ShapeDtypeStruct((planes, rows, full), jnp.float32)
     edge_shape = jax.ShapeDtypeStruct((planes, spare, full), jnp.float32)
-    specs = [scalar] + [anywhere] * (4 if chunks > 1 else 3) + [vector] * 4
-    given = [basis_z, got, basis_y] + ([part] if chunks > 1 else []) + list(operator)
-    specs.append(anywhere)
-    given.append(state["residual"])
+    before = part if chunks > 1 else state
+    specs = [scalar] + [anywhere] * 3 + [vector] * 4
+    given = [basis_z, got, basis_y] + list(operator)
+    if last:
+        specs.append(anywhere)
+        given.append(state["residual"])
     if stage >= 1:
-        specs += [anywhere] * 2 + [vector]
-        given += [state["z"], state["edge_z"], state["scalars"]]
-    if stage >= 2:
-        specs += [anywhere] * 2
-        given += [state["v"], state["edge_v"]]
-    names = ["z", "edge_z", "y", "aux"]
-    outs = [anywhere] * 3 + [vector]
-    shapes = [field_shape, edge_shape, field_shape, jax.ShapeDtypeStruct((spare, columns), jnp.float32)]
+        specs.append(vector)
+        given.append(state["scalars"])
+    for name in ("z", "v"):
+        if name in before:
+            specs += [anywhere] * 2
+            given += [before[name], before["edge_" + name]]
+    names = ["z", "edge_z", "y"]
+    outs = [anywhere] * 3
+    shapes = [field_shape, edge_shape, field_shape]
+    if last:
+        names.append("aux")
+        outs.append(vector)
+        shapes.append(jax.ShapeDtypeStruct((spare, columns), jnp.float32))
     if stage >= 1:
         names += ["v", "edge_v"]
         outs += [anywhere, anywhere]
@@ -584,23 +655,23 @@
         pltpu.VMEM((planes, rows + 2 * spare, full), jnp.float32),
         edge,
         field,
-        field,
     ]
+    if last:
+        scratch.append(field)
+    if "z" in before:
+        scratch.append(field)
     if stage >= 1:
-        scratch += [field, field, edge]
+        scratch += [field, edge]
     if not last:
         sent = (planes, full // chunks // columns, rows, columns)
-        mixed = (2 * planes * rows, full)
-        names += ["sent", "lines"]
-        outs += [anywhere] * 2
-        shapes += [jax.ShapeDtypeStruct(sent, jnp.float32), jax.ShapeDtypeStruct(mixed, jnp.bfloat16)]
-        scratch += [pltpu.VMEM(mixed, jnp.bfloat16), pltpu.VMEM(sent, jnp.float32)]
-    if chunks > 1:
-        scratch.append(pltpu.VMEM(part.shape, jnp.float32))
+        names.append("sent")
+        outs.append(anywhere)
+        shapes.append(jax.ShapeDtypeStruct(sent, jnp.float32))
+        scratch += [pltpu.VMEM((2 * planes * rows, full), jnp.bfloat16), pltpu.VMEM(sent, jnp.float32)]
     scratch += [
         pltpu.SemaphoreType.DMA((planes,)),
-        pltpu.SemaphoreType.DMA((blocks, 7)),
-        pltpu.SemaphoreType.DMA((7,)),
+        pltpu.SemaphoreType.DMA((blocks, 6)),
+        pltpu.SemaphoreType.DMA((6,)),
     ]
     if not last:
         scratch += [pltpu.SemaphoreType.DMA((blocks // chunks, 1))] * 2
@@ -759,26 +830,31 @@
     return lax.dynamic_slice_in_dim(padded, start, count + before + after)
 
 
-def add_kernel(numbers_ref, pressure_ref, direction_ref, lifted_ref, out_ref):
-    length = numbers_ref[2:3, 0:1]
-    turn = numbers_ref[3:4, 0:1]
+def lanes_sum(value, columns):
+    return jnp.sum(value.reshape(-1, value.shape[-1] // columns, columns), axis=(0, 1))
+
+
+def add_kernel(numbers_ref, sums_ref, pressure_ref, direction_ref, lifted_ref, out_ref):
+    total = jnp.sum(jnp.sum(sums_ref[...], axis=0), axis=1, keepdims=True)
+    turn = total[2:3] / numbers_ref[0:1, 0:1]
+    length = total[2:3] / (total[3:4] - turn * turn * numbers_ref[1:2, 0:1])
     for k in range(pressure_ref.shape[0]):
         direction = lifted_ref[k] + turn * direction_ref[k]
         out_ref[0, k] = pressure_ref[k] + length * direction
 
 
-def add_step(numbers, pressure, direction, lifted, pieces):
+def add_step(numbers, sums, pressure, direction, lifted, pieces):
     planes, rows, full = pressure.shape
     span = full // pieces
     field = pl.BlockSpec((planes, rows, span), lambda n: (0, 0, n))
     return pl.pallas_call(
         add_kernel,
         grid=(pieces,),
-        in_specs=[vector] + [field] * 3,
+        in_specs=[vector] * 2 + [field] * 3,
         out_specs=pl.BlockSpec((1, planes, rows, span), lambda n: (n, 0, 0, 0)),
         out_shape=jax.ShapeDtypeStruct((pieces, planes, rows, span), jnp.float32),
         compiler_params=params(),
-    )(numbers, pressure, direction, lifted)
+    )(numbers, sums, pressure, direction, lifted)
 
 
 def correct_kernel(
@@ -872,7 +948,10 @@
     reach = 3
 
     def edge_rows(part):
-        return jnp.concatenate([velocity[:, part], weight[None, part], code[None, part]])
+        cut = cut_flags[part]
+        share = share_weight[part] * cut.astype(jnp.float32)
+        target = (cut * (redirect[part] + 1)).astype(jnp.float32)
+        return jnp.concatenate([velocity[:, part], share[None], target[None]])
 
     above, below = neighbours("gx", edge_rows(slice(x_count - reach, None)), edge_rows(slice(0, reach)))
     velocity = velocity.transpose(0, 2, 1, 3)
@@ -916,22 +995,23 @@
         for chunk in range(chunks)
     ]
 
-    def apply(sent, lines, aux):
-        part = sums = None
+    def apply(stage, field, sent, aux, state):
         sents = [sent] + [
-            more_lines(lines, basis_y, planes, rows, columns, chunks, chunk) for chunk in range(1, chunks)
+            more_lines(field, basis_z, basis_y, columns, chunks, chunk) for chunk in range(1, chunks)
         ]
+        gots = []
         for chunk, sent in enumerate(sents):
             sent = sent.reshape(devices, rows, columns)
             got = lax.all_to_all(sent, both, 0, 0, tiled=True).reshape(full_x, columns)
             given = aux if chunk == 0 else jnp.zeros((spare, columns), jnp.float32)
             got = column_lines(got, given, basis_xt, basis_x, along, other[chunk], rows)
-            got = lax.all_to_all(got, both, 0, 0, tiled=True)
-            if chunk == 0:
-                sums = got[:, rows:]
-            if chunk + 1 < chunks:
-                part = part_lines(got, basis_y, planes, rows, chunks)
-        return got, part, sums
+            gots.append(lax.all_to_all(got, both, 0, 0, tiled=True))
+        if stage > 0:
+            state["scalars"] = numbers_of(gots[0][:, rows:], state.get("scalars"))
+        part = None
+        if chunks > 1:
+            part = part_lines(stage, gots[0], basis_z, basis_y, rows, chunks, state)
+        return gots[-1], part
 
     def numbers_of(sums, numbers):
         product = jnp.sum(sums[:, 2])
@@ -943,15 +1023,15 @@
         numbers = jnp.stack([product, bend, product / bend, turn])
         return jnp.broadcast_to(jnp.pad(numbers, (0, 4))[:, None], (8, 128))
 
-    residual, sent, lines = start_lines(source, basis_z, basis_y, columns, chunks)
-    got, part, _ = apply(sent, lines, jnp.zeros((spare, columns), jnp.float32))
-    state = {"residual": residual}
+    residual, sent = start_lines(source, basis_z, basis_y, columns, chunks)
+    state = {}
+    got, part = apply(0, residual, sent, jnp.zeros((spare, columns), jnp.float32), state)
     state |= turn_lines(0, False, got, part, operator, basis_z, basis_y, state, chunks)
-    numbers = None
     for stage in range(1, ITERS):
-        got, part, sums = apply(state["sent"], state["lines"], state["aux"])
-        numbers = numbers_of(sums, numbers)
-        length, turn = numbers[2, 0], numbers[3, 0]
+        partial = [lanes_sum(residual * state["z"], columns), lanes_sum(state["z"] * state["y"], columns)]
+        aux = jnp.pad(jnp.stack(partial), ((2, spare - 4), (0, 0)))
+        got, part = apply(stage, state["y"], state["sent"], aux, state)
+        length, turn = state["scalars"][2, 0], state["scalars"][3, 0]
         if stage == 1:
             direction, image = state["z"], state["y"]
             pressure = length * direction
@@ -959,14 +1039,13 @@
             direction = state["z"] + turn * direction
             image = state["y"] + turn * image
             pressure = pressure + length * direction
-        state["residual"] = state["residual"] - length * image
-        state["scalars"] = numbers
+        residual = residual - length * image
+        state["residual"] = residual
         last = stage + 1 == ITERS
         state |= turn_lines(stage, last, got, part, operator, basis_z, basis_y, state, chunks)
     sums = jnp.broadcast_to(state["aux"][None], (devices, spare, columns))
     sums = lax.all_to_all(sums, both, 0, 0, tiled=True)
-    numbers = numbers_of(sums, numbers)
-    pressure = add_step(numbers, pressure, direction, state["z"], y_parts)
+    pressure = add_step(state["scalars"], sums, pressure, direction, state["z"], y_parts)
     pressure = lax.all_to_all(pressure, "gy", 0, 0, tiled=True)
     above, below = neighbours("gx", pressure[-1, :, -1:], pressure[0, :, :1])
     left, right = neighbours("gy", pressure[..., -1], pressure[..., 0])

time: 792 us -> 778 us (0.982)
  waiting for transfers between devices: 289 us -> 262 us
  other arithmetic: 32 us -> 42 us
    all_to_all x8, waiting for transfers between devices: 128 us -> 107 us  [apply(): got = lax.all_to_all(sent, both, 0, 0, tiled=True).reshape(full_x, columns)]
    pallas_call x9, Pallas kernels: 56.8 us -> 71.5 us  [the longest x4 37.8 us: part_lines(): pl.pallas_call(functools.partial(part_kernel, stage, rows, block), in_spe...]
    reduce_sum x1 -> x8, other arithmetic: 0.67 us -> 12.6 us  [lanes_sum(): jnp.sum(value.reshape(-1, value.shape[-1] // columns, columns), axis=(0, 1))]
    pallas_call x4, Pallas kernels: 68.9 us -> 57.8 us  [turn_lines(): pl.pallas_call(functools.partial(turn_kernel, stage, last, block, chunks)...]
    unnamed x80 -> x70, local copies, waits for them, and re-layouts: 25.2 us -> 29.4 us
  transfers between devices with their start and end apart: 28 -> 28, of which waited for: 21 -> 21; matrix products, arithmetic and copies ran while one was open for 9% -> 11% of each run, Pallas kernels for 23% -> 25%
where the time goes in v5:
time: 778 us; the launch traced here: 766 us
  Pallas kernels  272 us (35%)
  waiting for transfers between devices  262 us (34%)
  starting transfers between devices  118 us (15%)
  local copies, waits for them, and re-layouts  63.8 us (8%)
  other arithmetic  42 us (5%)
  between operations  8.32 us (1%)
    all_to_all x8, waiting for transfers between devices, apply(): gots.append(lax.all_to_all(got, both, 0, 0, tiled=True))  116 us
    all_to_all x8, waiting for transfers between devices, apply(): got = lax.all_to_all(sent, both, 0, 0, tiled=True).reshape(full_x, columns)  107 us
    pallas_call x8, Pallas kernels, column_lines(): pl.pallas_call(functools.partial(column_kernel, rows, block), in_specs=[a...  93.8 us
    pallas_call x4, Pallas kernels, turn_lines(): pl.pallas_call(functools.partial(turn_kernel, stage, last, block, chunks)...  57.8 us
    all_to_all x8, starting transfers between devices, apply(): gots.append(lax.all_to_all(got, both, 0, 0, tiled=True))  38 us
    pallas_call x4, Pallas kernels, part_lines(): pl.pallas_call(functools.partial(part_kernel, stage, rows, block), in_spe...  37.8 us
    all_to_all x8, starting transfers between devices, apply(): got = lax.all_to_all(sent, both, 0, 0, tiled=True).reshape(full_x, columns)  37.5 us
    pallas_call x1, Pallas kernels, first_step(): pl.pallas_call(functools.partial(first_kernel, rows), in_specs=[anywhere]...  31.8 us
  transfers between devices with their start and end apart: 28, of which 21 were waited for; matrix products, arithmetic and copies ran while one was open for 11% of the time, Pallas kernels for 25%

profile of v5, /device:TPU:9, one launch (start us, length us, event | category | flops | bytes accessed | tf_op | source)
XLA Modules:
  0.0 765.7 jit_solution(16177406669709640652)
XLA Ops:
  57.3 31.8 %shard_map.131 = (f32[4,4,64,512]{3,2,1,0:T(8,128)}, f32[3,4,256,512]{3,2,1,0:T(8,128)}) custom-call(f32[3,4,256,512]{3,2,1,0:T(8,128)} %bitcast.117, f32[4,256,512]{2,1,0:T(8,128)} %copy-done.6, f32[4,256,512]{2,1,0:T(8,128)} %get-tuple-element.117.code_ref, f32[5,4,8,512]{3,2,1,0:T(8,128)} %pad.47.above_ref, f32[5,4,8,512]{3,2,1,0:T(8,128)} %pad.48.below_ref, ...), custom_call_target="tpu_custom_call" | custom-call | tf_op jit(solution)/shard_map/pallas_call | solution.py:803
  92.9 12.4 %copy.237 = bf16[2048,2048]{0,1:T(8,128)(2,1)} copy(bf16[2048,2048]{1,0:T(8,128)(2,1)} %back_ref.15) | data formatting | bytes 16777216 | tf_op args[6]
  137.0 18.1 %all-to-all-done.4 = f32[32,64,128]{2,1,0:T(8,128)S(1)} async-done(((f32[32,64,128]{2,1,0:T(8,128)}), f32[32,64,128]{2,1,0:T(8,128)S(1)}, u32[]{:S(2)}, u32[]{:S(2)}) %all-to-all-start.4) | async-done | bytes 1048608 | tf_op jit(solution)/shard_map/all_to_all | solution.py:1005
  189.6 11.7 %shard_map.134 = f32[32,72,128]{2,1,0:T(8,128)} custom-call(f32[2048,128]{1,0:T(8,128)} %bitcast.120, f32[8,128]{1,0:T(8,128)} %broadcast_2_aux_ref.2.aux_ref, bf16[2048,2048]{1,0:T(8,128)(2,1)} %bitcast.105, bf16[2048,2048]{1,0:T(8,128)(2,1)} %back_ref.15, f32[2048,1]{1,0:T(8,128)} %copy.238.along_ref, f32[1,128]{1,0:T(1,128)} %get-tuple-element.126.other_ref), custom_call_target="tpu_custom_call" | custom-call | tf_op jit(solution)/shard_map/pallas_call | solution.py:452
  201.3 16.3 %all-to-all-done.5.refs_1_ = f32[32,72,128]{2,1,0:T(8,128)S(1)} async-done(((f32[32,72,128]{2,1,0:T(8,128)}), f32[32,72,128]{2,1,0:T(8,128)S(1)}, u32[]{:S(2)}, u32[]{:S(2)}) %all-to-all-start.5) | async-done | bytes 1179680 | tf_op jit(solution)/shard_map/all_to_all | solution.py:1008
  236.1 14.2 %all-to-all-done.3.refs_1_ = f32[32,72,128]{2,1,0:T(8,128)S(1)} async-done(((f32[32,72,128]{2,1,0:T(8,128)}), f32[32,72,128]{2,1,0:T(8,128)S(1)}, u32[]{:S(2)}, u32[]{:S(2)}) %all-to-all-start.3) | async-done | bytes 1179680 | tf_op jit(solution)/shard_map/all_to_all | solution.py:1008
  251.3 14.3 %shard_map.137 = (f32[4,64,2048]{2,1,0:T(8,128)}, f32[4,8,2048]{2,1,0:T(8,128)}, f32[4,64,2048]{2,1,0:T(8,128)}, f32[4,8,64,128]{3,2,1,0:T(8,128)}) custom-call(f32[4,4]{1,0:T(4,128)} %refs_0_.15, f32[32,72,128]{2,1,0:T(8,128)} %copy-done.14, bf16[2048,2048]{1,0:T(8,128)(2,1)} %refs_2_.15, f32[4,64,2048]{2,1,0:T(8,128)} %bitcast.112, ...), custom_call_target="tpu_custom_call" | custom-call | tf_op jit(solution)/shard_map/pallas_call | solution.py:678
  277.5 18.1 %all-to-all-done.8 = f32[32,64,128]{2,1,0:T(8,128)S(1)} async-done(((f32[32,64,128]{2,1,0:T(8,128)}), f32[32,64,128]{2,1,0:T(8,128)S(1)}, u32[]{:S(2)}, u32[]{:S(2)}) %all-to-all-start.8) | async-done | bytes 1048608 | tf_op jit(solution)/shard_map/all_to_all | solution.py:1005
  304.6 11.7 %shard_map.140 = f32[32,72,128]{2,1,0:T(8,128)} custom-call(f32[2048,128]{1,0:T(8,128)} %bitcast.126, f32[8,128]{1,0:T(8,128)} %select_maximum_fusion.2.aux_ref, bf16[2048,2048]{1,0:T(8,128)(2,1)} %bitcast.106, bf16[2048,2048]{1,0:T(8,128)(2,1)} %back_ref.15, f32[2048,1]{1,0:T(8,128)} %copy.238.along_ref, f32[1,128]{1,0:T(1,128)} %get-tuple-element.125.other_ref), custom_call_target="tpu_custom_call" | custom-call | tf_op jit(solution)/shard_map/pallas_call | solution.py:452
  332.5 11.8 %shard_map.139 = f32[32,72,128]{2,1,0:T(8,128)} custom-call(f32[2048,128]{1,0:T(8,128)} %bitcast.124, f32[8,128]{1,0:T(8,128)} %broadcast_2_aux_ref.2.aux_ref, bf16[2048,2048]{1,0:T(8,128)(2,1)} %bitcast.107, bf16[2048,2048]{1,0:T(8,128)(2,1)} %back_ref.15, f32[2048,1]{1,0:T(8,128)} %copy.238.along_ref, f32[1,128]{1,0:T(1,128)} %get-tuple-element.126.other_ref), custom_call_target="tpu_custom_call" | custom-call | tf_op jit(solution)/shard_map/pallas_call | solution.py:452
  344.3 16.1 %all-to-all-done.9.refs_1_ = f32[32,72,128]{2,1,0:T(8,128)S(1)} async-done(((f32[32,72,128]{2,1,0:T(8,128)}), f32[32,72,128]{2,1,0:T(8,128)S(1)}, u32[]{:S(2)}, u32[]{:S(2)}) %all-to-all-start.9) | async-done | bytes 1179680 | tf_op jit(solution)/shard_map/all_to_all | solution.py:1008
  378.3 14.9 %all-to-all-done.7.refs_1_ = f32[32,72,128]{2,1,0:T(8,128)} async-done(((f32[32,72,128]{2,1,0:T(8,128)}), f32[32,72,128]{2,1,0:T(8,128)}, u32[]{:S(2)}, u32[]{:S(2)}) %all-to-all-start.7) | async-done | bytes 1179680 | tf_op jit(solution)/shard_map/all_to_all | solution.py:1008
  393.2 15.0 %shard_map.142 = (f32[4,64,2048]{2,1,0:T(8,128)}, f32[4,8,2048]{2,1,0:T(8,128)}, f32[4,64,2048]{2,1,0:T(8,128)}, f32[4,64,2048]{2,1,0:T(8,128)}, f32[4,8,2048]{2,1,0:T(8,128)}, /*index=5*/f32[4,8,64,128]{3,2,1,0:T(8,128)}) custom-call(f32[4,4]{1,0:T(4,128)} %refs_0_.15, f32[32,72,128]{2,1,0:T(8,128)} %all-to-all-done.7.refs_1_, bf16[2048,2048]{1,0:T(8,128)(2,1)} %refs_2_.15, ...), custom_call_target="tpu_custom_call" | custom-call | tf_op jit(solution)/shard_map/pallas_call | solution.py:678
  420.0 18.1 %all-to-all-done.12 = f32[32,64,128]{2,1,0:T(8,128)S(1)} async-done(((f32[32,64,128]{2,1,0:T(8,128)}), f32[32,64,128]{2,1,0:T(8,128)S(1)}, u32[]{:S(2)}, u32[]{:S(2)}) %all-to-all-start.12) | async-done | bytes 1048608 | tf_op jit(solution)/shard_map/all_to_all | solution.py:1005
  449.4 11.8 %shard_map.145 = f32[32,72,128]{2,1,0:T(8,128)} custom-call(f32[2048,128]{1,0:T(8,128)} %bitcast.128, f32[8,128]{1,0:T(8,128)} %select_maximum_fusion.1.aux_ref, bf16[2048,2048]{1,0:T(8,128)(2,1)} %bitcast.108, bf16[2048,2048]{1,0:T(8,128)(2,1)} %back_ref.15, f32[2048,1]{1,0:T(8,128)} %copy.238.along_ref, f32[1,128]{1,0:T(1,128)} %get-tuple-element.125.other_ref), custom_call_target="tpu_custom_call" | custom-call | tf_op jit(solution)/shard_map/pallas_call | solution.py:452
  474.5 11.7 %shard_map.144 = f32[32,72,128]{2,1,0:T(8,128)} custom-call(f32[2048,128]{1,0:T(8,128)} %bitcast.125, f32[8,128]{1,0:T(8,128)} %broadcast_2_aux_ref.2.aux_ref, bf16[2048,2048]{1,0:T(8,128)(2,1)} %bitcast.109, bf16[2048,2048]{1,0:T(8,128)(2,1)} %back_ref.15, f32[2048,1]{1,0:T(8,128)} %copy.238.along_ref, f32[1,128]{1,0:T(1,128)} %get-tuple-element.126.other_ref), custom_call_target="tpu_custom_call" | custom-call | tf_op jit(solution)/shard_map/pallas_call | solution.py:452
  486.3 16.3 %all-to-all-done.13.refs_1_ = f32[32,72,128]{2,1,0:T(8,128)S(1)} async-done(((f32[32,72,128]{2,1,0:T(8,128)}), f32[32,72,128]{2,1,0:T(8,128)S(1)}, u32[]{:S(2)}, u32[]{:S(2)}) %all-to-all-start.13) | async-done | bytes 1179680 | tf_op jit(solution)/shard_map/all_to_all | solution.py:1008
  522.7 12.9 %all-to-all-done.11.refs_1_ = f32[32,72,128]{2,1,0:T(8,128)} async-done(((f32[32,72,128]{2,1,0:T(8,128)}), f32[32,72,128]{2,1,0:T(8,128)}, u32[]{:S(2)}, u32[]{:S(2)}) %all-to-all-start.11) | async-done | bytes 1179680 | tf_op jit(solution)/shard_map/all_to_all | solution.py:1008
  535.5 15.0 %shard_map.147 = (f32[4,64,2048]{2,1,0:T(8,128)}, f32[4,8,2048]{2,1,0:T(8,128)}, f32[4,64,2048]{2,1,0:T(8,128)}, f32[4,64,2048]{2,1,0:T(8,128)}, f32[4,8,2048]{2,1,0:T(8,128)}, /*index=5*/f32[4,8,64,128]{3,2,1,0:T(8,128)}) custom-call(f32[4,4]{1,0:T(4,128)} %refs_0_.15, f32[32,72,128]{2,1,0:T(8,128)} %all-to-all-done.11.refs_1_, ...), custom_call_target="tpu_custom_call" | custom-call | tf_op jit(solution)/shard_map/pallas_call | solution.py:678
  562.3 18.1 %all-to-all-done.14 = f32[32,64,128]{2,1,0:T(8,128)S(1)} async-done(((f32[32,64,128]{2,1,0:T(8,128)}), f32[32,64,128]{2,1,0:T(8,128)S(1)}, u32[]{:S(2)}, u32[]{:S(2)}) %all-to-all-start.14) | async-done | bytes 1048608 | tf_op jit(solution)/shard_map/all_to_all | solution.py:1005
  616.9 11.8 %shard_map.150 = f32[32,72,128]{2,1,0:T(8,128)} custom-call(f32[2048,128]{1,0:T(8,128)} %bitcast.123, f32[8,128]{1,0:T(8,128)} %broadcast_2_aux_ref.2.aux_ref, bf16[2048,2048]{1,0:T(8,128)(2,1)} %bitcast.111, bf16[2048,2048]{1,0:T(8,128)(2,1)} %back_ref.15, f32[2048,1]{1,0:T(8,128)} %copy.238.along_ref, f32[1,128]{1,0:T(1,128)} %get-tuple-element.126.other_ref), custom_call_target="tpu_custom_call" | custom-call | tf_op jit(solution)/shard_map/pallas_call | solution.py:452
  628.6 16.2 %all-to-all-done.15.refs_1_ = f32[32,72,128]{2,1,0:T(8,128)S(1)} async-done(((f32[32,72,128]{2,1,0:T(8,128)}), f32[32,72,128]{2,1,0:T(8,128)S(1)}, u32[]{:S(2)}, u32[]{:S(2)}) %all-to-all-start.15) | async-done | bytes 1179680 | tf_op jit(solution)/shard_map/all_to_all | solution.py:1008
  677.7 13.5 %shard_map.152 = (f32[4,64,2048]{2,1,0:T(8,128)}, f32[4,8,2048]{2,1,0:T(8,128)}, f32[4,64,2048]{2,1,0:T(8,128)}, f32[8,128]{1,0:T(8,128)}, f32[4,64,2048]{2,1,0:T(8,128)}, /*index=5*/f32[4,8,2048]{2,1,0:T(8,128)}) custom-call(f32[4,4]{1,0:T(4,128)} %refs_0_.15, f32[32,72,128]{2,1,0:T(8,128)} %all-to-all-done.17.refs_1_, bf16[2048,2048]{1,0:T(8,128)(2,1)} %refs_2_.15, ...), custom_call_target="tpu_custom_call" | custom-call | tf_op jit(solution)/shard_map/pallas_call | solution.py:678
  714.9 24.2 %all-to-all-done.19.own_ref.previous_ref.next_ref = f32[4,4,64,512]{3,2,1,0:T(8,128)S(1)} async-done(((f32[4,4,64,512]{3,2,1,0:T(8,128)}), f32[4,4,64,512]{3,2,1,0:T(8,128)S(1)}, u32[]{:S(2)}, u32[]{:S(2)}) %all-to-all-start.19) | async-done | bytes 2097184 | tf_op jit(solution)/shard_map/all_to_all | solution.py:1049
  (208 shorter events, 381.5 us)
Async XLA Ops:
  9.0 31.0 %collective-permute-start = (f32[5,3,4,512]{3,1,2,0:T(4,128)}, f32[5,3,4,512]{3,1,2,0:T(4,128)S(1)}, u32[]{:S(2)}, u32[]{:S(2)}) collective-permute-start(f32[5,3,4,512]{3,1,2,0:T(4,128)} %pad_maximum_fusion), channel_id=1, source_target_pairs={{0,4},{4,8},{8,12},{12,16},{16,20},{20,24},{24,28},{1,5},{5,9},{9,... | collective-permute-start | bytes 368648 | tf_op jit(solution)/shard_map/ppermute | solution.py:825
  12.8 26.8 %collective-permute-start.1 = (f32[5,3,4,512]{3,1,2,0:T(4,128)}, f32[5,3,4,512]{3,1,2,0:T(4,128)S(1)}, u32[]{:S(2)}, u32[]{:S(2)}) collective-permute-start(f32[5,3,4,512]{3,1,2,0:T(4,128)} %pad_maximum_fusion.1), channel_id=1, source_target_pairs={{4,0},{8,4},{12,8},{16,12},{20,16},{24,20},{28,24},{5,1},{9,5},{13... | collective-permute-start | bytes 368648 | tf_op jit(solution)/shard_map/ppermute | solution.py:825
  17.4 71.6 %all-to-all-start = ((f32[4,4,64,512]{3,2,1,0:T(8,128)}), f32[4,4,64,512]{3,2,1,0:T(8,128)}, u32[]{:S(2)}, u32[]{:S(2)}) async-start(f32[4,4,64,512]{3,2,1,0:T(8,128)} %bitcast.119), calls=%async_computation | async-start | bytes 4194304 | tf_op jit(solution)/shard_map/all_to_all | solution.py:977
  89.1 27.3 %all-to-all-start.1 = ((f32[4,4,64,512]{3,2,1,0:T(8,128)}), f32[4,4,64,512]{3,2,1,0:T(8,128)S(1)}, u32[]{:S(2)}, u32[]{:S(2)}) async-start(f32[4,4,64,512]{3,2,1,0:T(8,128)} %get-tuple-element.44), calls=%async_computation.1 | async-start | bytes 4194304 | tf_op jit(solution)/shard_map/all_to_all | solution.py:979
  124.7 30.3 %all-to-all-start.4 = ((f32[32,64,128]{2,1,0:T(8,128)}), f32[32,64,128]{2,1,0:T(8,128)S(1)}, u32[]{:S(2)}, u32[]{:S(2)}) async-start(f32[32,64,128]{2,1,0:T(8,128)} %bitcast.135), calls=%async_computation.4 | async-start | bytes 2097152 | tf_op jit(solution)/shard_map/all_to_all | solution.py:1005
  155.1 29.9 %all-to-all-start.2 = ((f32[32,64,128]{2,1,0:T(8,128)}), f32[32,64,128]{2,1,0:T(8,128)S(1)}, u32[]{:S(2)}, u32[]{:S(2)}) async-start(f32[32,64,128]{2,1,0:T(8,128)} %bitcast.122), calls=%async_computation.2 | async-start | bytes 2097152 | tf_op jit(solution)/shard_map/all_to_all | solution.py:1005
  184.9 32.6 %all-to-all-start.5 = ((f32[32,72,128]{2,1,0:T(8,128)}), f32[32,72,128]{2,1,0:T(8,128)S(1)}, u32[]{:S(2)}, u32[]{:S(2)}) async-start(f32[32,72,128]{2,1,0:T(8,128)} %shard_map.135), calls=%async_computation.5 | async-start | bytes 2359296 | tf_op jit(solution)/shard_map/all_to_all | solution.py:1008
  217.6 32.7 %all-to-all-start.3 = ((f32[32,72,128]{2,1,0:T(8,128)}), f32[32,72,128]{2,1,0:T(8,128)S(1)}, u32[]{:S(2)}, u32[]{:S(2)}) async-start(f32[32,72,128]{2,1,0:T(8,128)} %shard_map.134), calls=%async_computation.3 | async-start | bytes 2359296 | tf_op jit(solution)/shard_map/all_to_all | solution.py:1008
  265.6 29.9 %all-to-all-start.8 = ((f32[32,64,128]{2,1,0:T(8,128)}), f32[32,64,128]{2,1,0:T(8,128)S(1)}, u32[]{:S(2)}, u32[]{:S(2)}) async-start(f32[32,64,128]{2,1,0:T(8,128)} %bitcast.134), calls=%async_computation.8 | async-start | bytes 2097152 | tf_op jit(solution)/shard_map/all_to_all | solution.py:1005
  296.5 29.9 %all-to-all-start.6 = ((f32[32,64,128]{2,1,0:T(8,128)}), f32[32,64,128]{2,1,0:T(8,128)S(1)}, u32[]{:S(2)}, u32[]{:S(2)}) async-start(f32[32,64,128]{2,1,0:T(8,128)} %bitcast.129), calls=%async_computation.6 | async-start | bytes 2097152 | tf_op jit(solution)/shard_map/all_to_all | solution.py:1005
  327.4 33.0 %all-to-all-start.9 = ((f32[32,72,128]{2,1,0:T(8,128)}), f32[32,72,128]{2,1,0:T(8,128)S(1)}, u32[]{:S(2)}, u32[]{:S(2)}) async-start(f32[32,72,128]{2,1,0:T(8,128)} %shard_map.140), calls=%async_computation.9 | async-start | bytes 2359296 | tf_op jit(solution)/shard_map/all_to_all | solution.py:1008
  360.4 32.8 %all-to-all-start.7 = ((f32[32,72,128]{2,1,0:T(8,128)}), f32[32,72,128]{2,1,0:T(8,128)}, u32[]{:S(2)}, u32[]{:S(2)}) async-start(f32[32,72,128]{2,1,0:T(8,128)} %shard_map.139), calls=%async_computation.7 | async-start | bytes 2359296 | tf_op jit(solution)/shard_map/all_to_all | solution.py:1008
  408.2 29.9 %all-to-all-start.12 = ((f32[32,64,128]{2,1,0:T(8,128)}), f32[32,64,128]{2,1,0:T(8,128)S(1)}, u32[]{:S(2)}, u32[]{:S(2)}) async-start(f32[32,64,128]{2,1,0:T(8,128)} %bitcast.132), calls=%async_computation.12 | async-start | bytes 2097152 | tf_op jit(solution)/shard_map/all_to_all | solution.py:1005
  439.1 29.9 %all-to-all-start.10 = ((f32[32,64,128]{2,1,0:T(8,128)}), f32[32,64,128]{2,1,0:T(8,128)S(1)}, u32[]{:S(2)}, u32[]{:S(2)}) async-start(f32[32,64,128]{2,1,0:T(8,128)} %bitcast.131), calls=%async_computation.10 | async-start | bytes 2097152 | tf_op jit(solution)/shard_map/all_to_all | solution.py:1005
  469.9 32.6 %all-to-all-start.13 = ((f32[32,72,128]{2,1,0:T(8,128)}), f32[32,72,128]{2,1,0:T(8,128)S(1)}, u32[]{:S(2)}, u32[]{:S(2)}) async-start(f32[32,72,128]{2,1,0:T(8,128)} %shard_map.145), calls=%async_computation.13 | async-start | bytes 2359296 | tf_op jit(solution)/shard_map/all_to_all | solution.py:1008
  502.6 32.9 %all-to-all-start.11 = ((f32[32,72,128]{2,1,0:T(8,128)}), f32[32,72,128]{2,1,0:T(8,128)}, u32[]{:S(2)}, u32[]{:S(2)}) async-start(f32[32,72,128]{2,1,0:T(8,128)} %shard_map.144), calls=%async_computation.11 | async-start | bytes 2359296 | tf_op jit(solution)/shard_map/all_to_all | solution.py:1008
  550.5 29.9 %all-to-all-start.14 = ((f32[32,64,128]{2,1,0:T(8,128)}), f32[32,64,128]{2,1,0:T(8,128)S(1)}, u32[]{:S(2)}, u32[]{:S(2)}) async-start(f32[32,64,128]{2,1,0:T(8,128)} %bitcast.133), calls=%async_computation.14 | async-start | bytes 2097152 | tf_op jit(solution)/shard_map/all_to_all | solution.py:1005
  581.4 29.9 %all-to-all-start.16 = ((f32[32,64,128]{2,1,0:T(8,128)}), f32[32,64,128]{2,1,0:T(8,128)S(1)}, u32[]{:S(2)}, u32[]{:S(2)}) async-start(f32[32,64,128]{2,1,0:T(8,128)} %bitcast.130), calls=%async_computation.16 | async-start | bytes 2097152 | tf_op jit(solution)/shard_map/all_to_all | solution.py:1005
  612.3 32.6 %all-to-all-start.15 = ((f32[32,72,128]{2,1,0:T(8,128)}), f32[32,72,128]{2,1,0:T(8,128)S(1)}, u32[]{:S(2)}, u32[]{:S(2)}) async-start(f32[32,72,128]{2,1,0:T(8,128)} %shard_map.148), calls=%async_computation.15 | async-start | bytes 2359296 | tf_op jit(solution)/shard_map/all_to_all | solution.py:1008
  644.9 32.8 %all-to-all-start.17 = ((f32[32,72,128]{2,1,0:T(8,128)}), f32[32,72,128]{2,1,0:T(8,128)}, u32[]{:S(2)}, u32[]{:S(2)}) async-start(f32[32,72,128]{2,1,0:T(8,128)} %shard_map.150), calls=%async_computation.17 | async-start | bytes 2359296 | tf_op jit(solution)/shard_map/all_to_all | solution.py:1008
  692.5 11.0 %all-to-all-start.18 = ((f32[32,8,128]{2,1,0:T(8,128)}), f32[32,8,128]{2,1,0:T(8,128)S(1)}, u32[]{:S(2)}, u32[]{:S(2)}) async-start(f32[32,8,128]{2,1,0:T(8,128)} %broadcast_in_dim.108), calls=%async_computation.18 | async-start | bytes 262144 | tf_op jit(solution)/shard_map/all_to_all | solution.py:1047
  709.3 29.7 %all-to-all-start.19 = ((f32[4,4,64,512]{3,2,1,0:T(8,128)}), f32[4,4,64,512]{3,2,1,0:T(8,128)S(1)}, u32[]{:S(2)}, u32[]{:S(2)}) async-start(f32[4,4,64,512]{3,2,1,0:T(8,128)} %shard_map.153), calls=%async_computation.19 | async-start | bytes 4194304 | tf_op jit(solution)/shard_map/all_to_all | solution.py:1049
  739.1 16.0 %collective-permute-start.4 = (f32[4,1,512]{2,1,0:T(1,128)S(1)}, f32[4,1,512]{2,1,0:T(1,128)S(1)}, u32[]{:S(2)}, u32[]{:S(2)}) collective-permute-start(f32[4,1,512]{2,1,0:T(1,128)S(1)} %get-tuple-element.108), channel_id=1, source_target_pairs={{0,4},{4,8},{8,12},{12,16},{16,20},{20,24},{24,28},{1,5},{5,9},{9,... | collective-permute-start | bytes 24584 | tf_op jit(solution)/shard_map/ppermute | solution.py:825
  741.4 13.7 %collective-permute-start.5 = (f32[4,1,512]{2,1,0:T(1,128)S(1)}, f32[4,1,512]{2,1,0:T(1,128)S(1)}, u32[]{:S(2)}, u32[]{:S(2)}) collective-permute-start(f32[4,1,512]{2,1,0:T(1,128)S(1)} %get-tuple-element.107), channel_id=1, source_target_pairs={{4,0},{8,4},{12,8},{16,12},{20,16},{24,20},{28,24},{5,1},{9,5},{13... | collective-permute-start | bytes 24584 | tf_op jit(solution)/shard_map/ppermute | solution.py:825
  (37 other events, 270.1 us)

commit v6 on v5

--- a/solution.py
+++ b/solution.py
@@ -15,7 +15,6 @@
 cut_shift = 0.45
 both = ("gx", "gy")
 spare = 8
-vmem_bytes = 56 * 1024 * 1024
 
 
 def halves(value):
@@ -24,8 +23,8 @@
     return high, low
 
 
-def params():
-    return pltpu.CompilerParams(vmem_limit_bytes=vmem_bytes)
+def params(mebibytes):
+    return pltpu.CompilerParams(vmem_limit_bytes=mebibytes * 1024 * 1024)
 
 
 def mix_planes(read, mix_ref, lines, rows):
@@ -106,6 +105,10 @@
 def wait_all(copies):
     for copy in copies:
         copy.wait()
+
+
+def far(*values):
+    return [pltpu.with_memory_space_constraint(value, pltpu.HBM) for value in values]
 
 
 def piece(index, size):
@@ -173,11 +176,11 @@
     sent = (planes, full // chunks // columns, rows, columns)
     return pl.pallas_call(
         functools.partial(start_kernel, block),
-        in_specs=[scalar, anywhere, anywhere],
+        in_specs=[scalar, vector, anywhere],
         out_specs=[anywhere] * 2,
         out_shape=[
-            jax.ShapeDtypeStruct((planes, rows, full), jnp.float32),
-            jax.ShapeDtypeStruct(sent, jnp.float32),
+            pltpu.HBM((planes, rows, full), jnp.float32),
+            pltpu.HBM(sent, jnp.float32),
         ],
         scratch_shapes=[
             pltpu.VMEM((planes, rows, full), jnp.float32),
@@ -188,8 +191,8 @@
             pltpu.SemaphoreType.DMA((blocks, 1)),
             pltpu.SemaphoreType.DMA((blocks, 1)),
         ],
-        compiler_params=params(),
-    )(basis_z, field, basis_y)
+        compiler_params=params(24),
+    )(basis_z, field, *far(basis_y))
 
 
 def more_kernel(
@@ -213,7 +216,7 @@
         functools.partial(more_kernel, block, chunk),
         in_specs=[scalar, anywhere, anywhere],
         out_specs=anywhere,
-        out_shape=jax.ShapeDtypeStruct(sent, jnp.float32),
+        out_shape=pltpu.HBM(sent, jnp.float32),
         scratch_shapes=[
             pltpu.VMEM(field.shape, jnp.float32),
             pltpu.VMEM(basis_y.shape, jnp.bfloat16),
@@ -223,8 +226,8 @@
             pltpu.SemaphoreType.DMA((blocks, 1)),
             pltpu.SemaphoreType.DMA((blocks, 1)),
         ],
-        compiler_params=params(),
-    )(basis_z, field, basis_y)
+        compiler_params=params(24),
+    )(basis_z, *far(field, basis_y))
 
 
 def take_lines(got, lines, planes, rows):
@@ -335,21 +338,21 @@
     half = planes * (rows + spare)
     field, edge = (planes, rows, full), (planes, spare, full)
     names = ["z", "edge_z"]
-    given = [basis_z, got, basis_y]
-    specs = [scalar, anywhere, anywhere]
+    given = [basis_z, got, *far(basis_y)]
+    specs = [scalar, vector, anywhere]
     if stage >= 1:
         names += ["v", "edge_v"]
-        given += [state["scalars"], state["z"], state["edge_z"]]
+        given += [state["scalars"], *far(state["z"], state["edge_z"])]
         specs += [vector, anywhere, anywhere]
     if stage >= 2:
-        given += [state["v"], state["edge_v"]]
+        given += far(state["v"], state["edge_v"])
         specs += [anywhere, anywhere]
     shapes = [field, edge] * (len(names) // 2)
     results = pl.pallas_call(
         functools.partial(part_kernel, stage, rows, block),
         in_specs=specs,
         out_specs=[anywhere] * len(names),
-        out_shape=[jax.ShapeDtypeStruct(shape, jnp.float32) for shape in shapes],
+        out_shape=[pltpu.HBM(shape, jnp.float32) for shape in shapes],
         scratch_shapes=[
             pltpu.VMEM(got.shape, jnp.float32),
             pltpu.VMEM((full, full // chunks), jnp.bfloat16),
@@ -361,7 +364,7 @@
             pltpu.SemaphoreType.DMA((full // block, 5)),
             pltpu.SemaphoreType.DMA((full // block, 4)),
         ],
-        compiler_params=params(),
+        compiler_params=params(28),
     )(*given)
     return dict(zip(names, results))
 
@@ -451,9 +454,9 @@
     devices = full // rows
     return pl.pallas_call(
         functools.partial(column_kernel, rows, block),
-        in_specs=[anywhere, vector, anywhere, anywhere, vector, vector],
+        in_specs=[vector, vector, anywhere, anywhere, vector, vector],
         out_specs=anywhere,
-        out_shape=jax.ShapeDtypeStruct((devices, rows + spare, columns), jnp.float32),
+        out_shape=pltpu.HBM((devices, rows + spare, columns), jnp.float32),
         scratch_shapes=[
             pltpu.VMEM((full, columns), jnp.float32),
             pltpu.VMEM((full, full), jnp.bfloat16),
@@ -465,8 +468,8 @@
             pltpu.SemaphoreType.DMA((2, full // block, 1)),
             pltpu.SemaphoreType.DMA((full // block, 1)),
         ],
-        compiler_params=params(),
-    )(field, aux, basis_xt, basis_x, along, other)
+        compiler_params=params(28),
+    )(field, aux, *far(basis_xt, basis_x), along, other)
 
 
 def turn_kernel(stage, last, block, chunks, *refs):
@@ -619,21 +622,21 @@
     _, _, columns = got.shape
     block = min(512, full // chunks)
     blocks = full // block
-    field_shape = jax.ShapeDtypeStruct((planes, rows, full), jnp.float32)
-    edge_shape = jax.ShapeDtypeStruct((planes, spare, full), jnp.float32)
+    field_shape = pltpu.HBM((planes, rows, full), jnp.float32)
+    edge_shape = pltpu.HBM((planes, spare, full), jnp.float32)
     before = part if chunks > 1 else state
-    specs = [scalar] + [anywhere] * 3 + [vector] * 4
-    given = [basis_z, got, basis_y] + list(operator)
+    specs = [scalar, vector] + [anywhere] * 2 + [vector] * 4
+    given = [basis_z, got, *far(basis_y, operator[0])] + list(operator[1:])
     if last:
         specs.append(anywhere)
-        given.append(state["residual"])
+        given += far(state["residual"])
     if stage >= 1:
         specs.append(vector)
         given.append(state["scalars"])
     for name in ("z", "v"):
         if name in before:
             specs += [anywhere] * 2
-            given += [before[name], before["edge_" + name]]
+            given += far(before[name], before["edge_" + name])
     names = ["z", "edge_z", "y"]
     outs = [anywhere] * 3
     shapes = [field_shape, edge_shape, field_shape]
@@ -666,7 +669,7 @@
         sent = (planes, full // chunks // columns, rows, columns)
         names.append("sent")
         outs.append(anywhere)
-        shapes.append(jax.ShapeDtypeStruct(sent, jnp.float32))
+        shapes.append(pltpu.HBM(sent, jnp.float32))
         scratch += [pltpu.VMEM((2 * planes * rows, full), jnp.bfloat16), pltpu.VMEM(sent, jnp.float32)]
     scratch += [
         pltpu.SemaphoreType.DMA((planes,)),
@@ -681,37 +684,34 @@
         out_specs=outs,
         out_shape=shapes,
         scratch_shapes=scratch,
-        compiler_params=params(),
+        compiler_params=params(40),
     )(*given)
     return dict(zip(names, results))
 
 
 def first_kernel(
     rows, velocity_ref, weight_ref, code_ref, above_ref, below_ref, side_ref, half_x_ref, half_y_ref,
-    source_ref, predicted_ref, fields, moved, kept, semaphores,
+    source_ref, predicted_ref, fields, moved, kept, semaphores, late_semaphores,
 ):
     planes, count, span = weight_ref.shape
     wide = half_y_ref.shape[1]
     pad = 16
-    copies = []
+    middle = count // 16 * 8
+    early, late = [], []
     for channel in range(5):
         if channel < 3:
             main = velocity_ref.at[channel]
         else:
             main = weight_ref if channel == 3 else code_ref
         target = fields.at[channel]
-        copies.append((main, target.at[:, pad : pad + count, :span]))
-        copies.append((above_ref.at[channel], target.at[:, pad - 8 : pad, :span]))
-        copies.append((below_ref.at[channel], target.at[:, pad + count : pad + count + 8, :span]))
-        copies.append((side_ref.at[channel], target.at[:, :, span:]))
-    copies = [
-        pltpu.make_async_copy(given, target, semaphores.at[index])
-        for index, (given, target) in enumerate(copies)
-    ]
-    for copy in copies:
-        copy.start()
-    for copy in copies:
-        copy.wait()
+        early.append((main.at[:, :middle], target.at[:, pad : pad + middle, :span]))
+        early.append((above_ref.at[channel], target.at[:, pad - 8 : pad, :span]))
+        early.append((below_ref.at[channel], target.at[:, pad + count : pad + count + 8, :span]))
+        early.append((side_ref.at[channel], target.at[:, :, span:]))
+        late.append((main.at[:, middle:], target.at[:, pad + middle : pad + count, :span]))
+    early = start_all(early, semaphores)
+    late = start_all(late, late_semaphores)
+    wait_all(early)
     tiles = count // 8 + 2
     half_y = half_y_ref[...]
 
@@ -719,8 +719,9 @@
         return pltpu.roll(value, wide - 1, 1) - pltpu.roll(value, 1, 1)
 
     def advance(index, carry):
-        k = index // tiles
-        start = pl.multiple_of(8 + (index - k * tiles) * 8, 8)
+        tile = index // planes
+        k = index - tile * planes
+        start = pl.multiple_of(8 + tile * 8, 8)
         window = pl.ds(pl.multiple_of(start - 8, 8), 24)
         own = pl.ds(start, 8)
         before = jnp.where(k == 0, planes - 1, k - 1)
@@ -743,7 +744,10 @@
             kept[c, k, own, :] = total - share
         return carry
 
-    lax.fori_loop(0, planes * tiles, advance, 0, unroll=4)
+    safe = planes * (middle // 8)
+    lax.fori_loop(0, safe, advance, 0, unroll=4)
+    wait_all(late)
+    lax.fori_loop(safe, planes * tiles, advance, 0, unroll=4)
 
     def settle(index, carry):
         k = index // tiles
@@ -769,6 +773,9 @@
         return carry
 
     lax.fori_loop(0, planes * tiles, settle, 0, unroll=4)
+    done = start_all(
+        [(kept.at[c, :, pad : pad + count, :span], predicted_ref.at[c]) for c in range(3)], late_semaphores
+    )
     inner = count // 8
     group = rows // 8
 
@@ -788,13 +795,10 @@
         target = tile // group
         spot = pl.multiple_of((tile - target * group) * 8, 8)
         source_ref[target, k, pl.ds(spot, 8), :] = -total[:, :span]
-        out = pl.ds(pl.multiple_of(tile * 8, 8), 8)
-        predicted_ref[0, k, out, :] = first[8:16, :span]
-        predicted_ref[1, k, out, :] = second[:, :span]
-        predicted_ref[2, k, out, :] = kept[2, k, own, :span]
         return carry
 
     lax.fori_loop(0, planes * inner, collect, 0, unroll=8)
+    wait_all(done)
 
 
 def first_step(velocity, weight, code, above, below, side, half_x, half_y, rows):
@@ -803,7 +807,7 @@
     return pl.pallas_call(
         functools.partial(first_kernel, rows),
         in_specs=[anywhere] * 6 + [vector] * 2,
-        out_specs=[vector] * 2,
+        out_specs=[vector, anywhere],
         out_shape=[
             jax.ShapeDtypeStruct((count // rows, planes, rows, span), jnp.float32),
             jax.ShapeDtypeStruct((3, planes, count, span), jnp.float32),
@@ -813,9 +817,10 @@
             pltpu.VMEM((3, planes, tall, wide), jnp.float32),
             pltpu.VMEM((3, planes, tall, wide), jnp.float32),
             pltpu.SemaphoreType.DMA((20,)),
+            pltpu.SemaphoreType.DMA((5,)),
         ],
-        compiler_params=params(),
-    )(velocity, weight, code, above, below, side, half_x, half_y)
+        compiler_params=params(48),
+    )(*far(velocity, weight, code, above, below, side), half_x, half_y)
 
 
 def neighbours(axis, last, leading):
@@ -852,8 +857,8 @@
         grid=(pieces,),
         in_specs=[vector] * 2 + [field] * 3,
         out_specs=pl.BlockSpec((1, planes, rows, span), lambda n: (n, 0, 0, 0)),
-        out_shape=jax.ShapeDtypeStruct((pieces, planes, rows, span), jnp.float32),
-        compiler_params=params(),
+        out_shape=pltpu.HBM((pieces, planes, rows, span), jnp.float32),
+        compiler_params=params(20),
     )(numbers, sums, pressure, direction, lifted)
 
 
@@ -908,7 +913,7 @@
             jax.ShapeDtypeStruct((3, count, planes, span), jnp.float32),
             jax.ShapeDtypeStruct((count, planes, span), jnp.float32),
         ],
-        compiler_params=params(),
+        compiler_params=params(28),
     )(predicted, pressure, pressure, pressure, above, below, left, right, half_x, half_y)
 
 
@@ -965,8 +970,11 @@
         return jnp.concatenate([above[..., part], middle, below[..., part]], axis=2).swapaxes(2, 3)
 
     left, right = neighbours("gy", edge_columns(slice(y_count - reach, None)), edge_columns(slice(0, reach)))
-    side = jnp.concatenate([right, jnp.zeros((5, planes, 128 - 2 * reach, x_count + 2 * reach), jnp.float32), left], axis=2)
-    side = jnp.pad(side.swapaxes(2, 3), ((0, 0), (0, 0), (16 - reach, 16 - reach), (0, 0)))
+    left, right = [
+        jnp.pad(part, ((0, 0), (0, 0), (0, 0), (16 - reach, 16 - reach))) for part in (left, right)
+    ]
+    side = jnp.concatenate([right, jnp.zeros((5, planes, 128 - 2 * reach, x_count + 32), jnp.float32), left], axis=2)
+    side = side.swapaxes(2, 3)
     above = jnp.pad(above, ((0, 0), (0, 0), (8 - reach, 0), (0, 0)))
     below = jnp.pad(below, ((0, 0), (0, 0), (0, 8 - reach), (0, 0)))
     half_x = 0.5 * extended_1(inverse_dx, x_index * x_count, x_count, 16, 16)[:, None]

time: 778 us -> 753 us (0.968)
  Pallas kernels: 272 us -> 237 us
  waiting for transfers between devices: 262 us -> 286 us
  local copies, waits for them, and re-layouts: 63.8 us -> 52.1 us
    pallas_call x8, Pallas kernels: 93.8 us -> 81 us  [column_lines(): pl.pallas_call(functools.partial(column_kernel, rows, block), in_specs=[v...]
    all_to_all x8, waiting for transfers between devices: 116 us -> 129 us  [apply(): gots.append(lax.all_to_all(got, both, 0, 0, tiled=True))]
    all_to_all x8, waiting for transfers between devices: 107 us -> 116 us  [apply(): got = lax.all_to_all(sent, both, 0, 0, tiled=True).reshape(full_x, columns)]
    unnamed x70 -> x44, local copies, waits for them, and re-layouts: 29.4 us -> 27.2 us
  transfers between devices with their start and end apart: 28 -> 28, of which waited for: 21 -> 20; matrix products, arithmetic and copies ran while one was open for 11% -> 10% of each run, Pallas kernels for 25% -> 23%
where the time goes in v6:
time: 753 us; the launch traced here: 743 us
  waiting for transfers between devices  286 us (38%)
  Pallas kernels  237 us (31%)
  starting transfers between devices  118 us (16%)
  local copies, waits for them, and re-layouts  52.1 us (7%)
  other arithmetic  41.6 us (6%)
  between operations  9.03 us (1%)
    all_to_all x8, waiting for transfers between devices, apply(): gots.append(lax.all_to_all(got, both, 0, 0, tiled=True))  129 us
    all_to_all x8, waiting for transfers between devices, apply(): got = lax.all_to_all(sent, both, 0, 0, tiled=True).reshape(full_x, columns)  116 us
    pallas_call x8, Pallas kernels, column_lines(): pl.pallas_call(functools.partial(column_kernel, rows, block), in_specs=[v...  81 us
    pallas_call x4, Pallas kernels, turn_lines(): pl.pallas_call(functools.partial(turn_kernel, stage, last, block, chunks)...  52.4 us
    all_to_all x8, starting transfers between devices, apply(): got = lax.all_to_all(sent, both, 0, 0, tiled=True).reshape(full_x, columns)  38.1 us
    all_to_all x8, starting transfers between devices, apply(): gots.append(lax.all_to_all(got, both, 0, 0, tiled=True))  37.7 us
    pallas_call x4, Pallas kernels, part_lines(): pl.pallas_call(functools.partial(part_kernel, stage, rows, block), in_spe...  35.7 us
    pallas_call x4, Pallas kernels, more_lines(): pl.pallas_call(functools.partial(more_kernel, block, chunk), in_specs=[sc...  28.1 us
  transfers between devices with their start and end apart: 28, of which 20 were waited for; matrix products, arithmetic and copies ran while one was open for 10% of the time, Pallas kernels for 23%

profile of v6, /device:TPU:9, one launch (start us, length us, event | category | flops | bytes accessed | tf_op | source)
XLA Modules:
  0.0 743.5 jit_solution(9270113888010454205)
XLA Ops:
  57.4 25.3 %shard_map.131 = (f32[4,4,64,512]{3,2,1,0:T(8,128)S(1)}, f32[3,4,256,512]{3,2,1,0:T(8,128)}) custom-call(f32[3,4,256,512]{3,2,1,0:T(8,128)} %bitcast.134, f32[4,256,512]{2,1,0:T(8,128)} %copy-done.10, f32[4,256,512]{2,1,0:T(8,128)} %get-tuple-element.117.code_ref, f32[5,4,8,512]{3,2,1,0:T(8,128)} %pad.50.above_ref, f32[5,4,8,512]{3,2,1,0:T(8,128)} %pad.51.below_ref, ...), custom_call_target="tpu_custom_call" | custom-call | tf_op jit(solution)/shard_map/pallas_call | solution.py:807
  87.7 12.3 %copy.237 = bf16[2048,2048]{0,1:T(8,128)(2,1)} copy(bf16[2048,2048]{1,0:T(8,128)(2,1)} %back_ref.15) | data formatting | bytes 16777216 | tf_op args[6]
  100.0 11.9 %all-to-all-done.1.field_ref = f32[4,4,64,512]{3,2,1,0:T(8,128)S(1)} async-done(((f32[4,4,64,512]{3,2,1,0:T(8,128)}), f32[4,4,64,512]{3,2,1,0:T(8,128)S(1)}, u32[]{:S(2)}, u32[]{:S(2)}) %all-to-all-start.1) | async-done | bytes 2097184 | tf_op jit(solution)/shard_map/all_to_all | solution.py:987
  131.2 18.2 %all-to-all-done.4 = f32[32,64,128]{2,1,0:T(8,128)S(1)} async-done(((f32[32,64,128]{2,1,0:T(8,128)}), f32[32,64,128]{2,1,0:T(8,128)S(1)}, u32[]{:S(2)}, u32[]{:S(2)}) %all-to-all-start.4) | async-done | bytes 1048608 | tf_op jit(solution)/shard_map/all_to_all | solution.py:1013
  166.6 12.7 %all-to-all-done.2 = f32[32,64,128]{2,1,0:T(8,128)S(1)} async-done(((f32[32,64,128]{2,1,0:T(8,128)}), f32[32,64,128]{2,1,0:T(8,128)S(1)}, u32[]{:S(2)}, u32[]{:S(2)}) %all-to-all-start.2) | async-done | bytes 1048608 | tf_op jit(solution)/shard_map/all_to_all | solution.py:1013
  183.9 10.1 %shard_map.134 = f32[32,72,128]{2,1,0:T(8,128)} custom-call(f32[2048,128]{1,0:T(8,128)S(1)} %bitcast.104, f32[8,128]{1,0:T(8,128)S(1)} %broadcast_2_aux_ref.2.aux_ref, bf16[2048,2048]{1,0:T(8,128)(2,1)} %bitcast.122, bf16[2048,2048]{1,0:T(8,128)(2,1)} %back_ref.15, f32[2048,1]{1,0:T(8,128)S(1)} %copy.238.along_ref, f32[1,128]{1,0:T(1,128)S(1)} %get-tuple-element.126.other_ref), custom_call_target="tpu_custom_call" | custom-call | tf_op jit(solution)/shard_map/pallas_call | solution.py:455
  194.1 17.9 %all-to-all-done.5.refs_1_ = f32[32,72,128]{2,1,0:T(8,128)S(1)} async-done(((f32[32,72,128]{2,1,0:T(8,128)}), f32[32,72,128]{2,1,0:T(8,128)S(1)}, u32[]{:S(2)}, u32[]{:S(2)}) %all-to-all-start.5) | async-done | bytes 1179680 | tf_op jit(solution)/shard_map/all_to_all | solution.py:1016
  228.4 16.4 %all-to-all-done.3.refs_1_ = f32[32,72,128]{2,1,0:T(8,128)S(1)} async-done(((f32[32,72,128]{2,1,0:T(8,128)}), f32[32,72,128]{2,1,0:T(8,128)S(1)}, u32[]{:S(2)}, u32[]{:S(2)}) %all-to-all-start.3) | async-done | bytes 1179680 | tf_op jit(solution)/shard_map/all_to_all | solution.py:1016
  244.8 13.3 %shard_map.137 = (f32[4,64,2048]{2,1,0:T(8,128)}, f32[4,8,2048]{2,1,0:T(8,128)}, f32[4,64,2048]{2,1,0:T(8,128)}, f32[4,8,64,128]{3,2,1,0:T(8,128)}) custom-call(f32[4,4]{1,0:T(4,128)S(1)} %copy-done.4, f32[32,72,128]{2,1,0:T(8,128)S(1)} %all-to-all-done.3.refs_1_, bf16[2048,2048]{1,0:T(8,128)(2,1)} %refs_2_.15, f32[4,64,2048]{2,1,0:T(8,128)} %bitcast.129, ...), custom_call_target="tpu_custom_call" | custom-call | tf_op jit(solution)/shard_map/pallas_call | solution.py:681
  269.8 18.2 %all-to-all-done.8 = f32[32,64,128]{2,1,0:T(8,128)S(1)} async-done(((f32[32,64,128]{2,1,0:T(8,128)}), f32[32,64,128]{2,1,0:T(8,128)S(1)}, u32[]{:S(2)}, u32[]{:S(2)}) %all-to-all-start.8) | async-done | bytes 1048608 | tf_op jit(solution)/shard_map/all_to_all | solution.py:1013
  306.2 11.6 %all-to-all-done.6 = f32[32,64,128]{2,1,0:T(8,128)S(1)} async-done(((f32[32,64,128]{2,1,0:T(8,128)}), f32[32,64,128]{2,1,0:T(8,128)S(1)}, u32[]{:S(2)}, u32[]{:S(2)}) %all-to-all-start.6) | async-done | bytes 1048608 | tf_op jit(solution)/shard_map/all_to_all | solution.py:1013
  332.6 17.9 %all-to-all-done.9.refs_1_ = f32[32,72,128]{2,1,0:T(8,128)S(1)} async-done(((f32[32,72,128]{2,1,0:T(8,128)}), f32[32,72,128]{2,1,0:T(8,128)S(1)}, u32[]{:S(2)}, u32[]{:S(2)}) %all-to-all-start.9) | async-done | bytes 1179680 | tf_op jit(solution)/shard_map/all_to_all | solution.py:1016
  367.2 16.0 %all-to-all-done.7.refs_1_ = f32[32,72,128]{2,1,0:T(8,128)S(1)} async-done(((f32[32,72,128]{2,1,0:T(8,128)}), f32[32,72,128]{2,1,0:T(8,128)S(1)}, u32[]{:S(2)}, u32[]{:S(2)}) %all-to-all-start.7) | async-done | bytes 1179680 | tf_op jit(solution)/shard_map/all_to_all | solution.py:1016
  383.1 13.8 %shard_map.142 = (f32[4,64,2048]{2,1,0:T(8,128)}, f32[4,8,2048]{2,1,0:T(8,128)}, f32[4,64,2048]{2,1,0:T(8,128)}, f32[4,64,2048]{2,1,0:T(8,128)}, f32[4,8,2048]{2,1,0:T(8,128)}, /*index=5*/f32[4,8,64,128]{3,2,1,0:T(8,128)}) custom-call(f32[4,4]{1,0:T(4,128)S(1)} %copy-done.4, f32[32,72,128]{2,1,0:T(8,128)S(1)} %all-to-all-done.7.refs_1_, ...), custom_call_target="tpu_custom_call" | custom-call | tf_op jit(solution)/shard_map/pallas_call | solution.py:681
  408.6 18.2 %all-to-all-done.12 = f32[32,64,128]{2,1,0:T(8,128)S(1)} async-done(((f32[32,64,128]{2,1,0:T(8,128)}), f32[32,64,128]{2,1,0:T(8,128)S(1)}, u32[]{:S(2)}, u32[]{:S(2)}) %all-to-all-start.12) | async-done | bytes 1048608 | tf_op jit(solution)/shard_map/all_to_all | solution.py:1013
  471.4 17.9 %all-to-all-done.13.refs_1_ = f32[32,72,128]{2,1,0:T(8,128)S(1)} async-done(((f32[32,72,128]{2,1,0:T(8,128)}), f32[32,72,128]{2,1,0:T(8,128)S(1)}, u32[]{:S(2)}, u32[]{:S(2)}) %all-to-all-start.13) | async-done | bytes 1179680 | tf_op jit(solution)/shard_map/all_to_all | solution.py:1016
  507.6 14.3 %all-to-all-done.11.refs_1_ = f32[32,72,128]{2,1,0:T(8,128)S(1)} async-done(((f32[32,72,128]{2,1,0:T(8,128)}), f32[32,72,128]{2,1,0:T(8,128)S(1)}, u32[]{:S(2)}, u32[]{:S(2)}) %all-to-all-start.11) | async-done | bytes 1179680 | tf_op jit(solution)/shard_map/all_to_all | solution.py:1016
  522.0 13.8 %shard_map.147 = (f32[4,64,2048]{2,1,0:T(8,128)}, f32[4,8,2048]{2,1,0:T(8,128)}, f32[4,64,2048]{2,1,0:T(8,128)}, f32[4,64,2048]{2,1,0:T(8,128)}, f32[4,8,2048]{2,1,0:T(8,128)}, /*index=5*/f32[4,8,64,128]{3,2,1,0:T(8,128)}) custom-call(f32[4,4]{1,0:T(4,128)S(1)} %copy-done.4, f32[32,72,128]{2,1,0:T(8,128)S(1)} %all-to-all-done.11.refs_1_, ...), custom_call_target="tpu_custom_call" | custom-call | tf_op jit(solution)/shard_map/pallas_call | solution.py:681
  547.5 18.2 %all-to-all-done.14 = f32[32,64,128]{2,1,0:T(8,128)S(1)} async-done(((f32[32,64,128]{2,1,0:T(8,128)}), f32[32,64,128]{2,1,0:T(8,128)S(1)}, u32[]{:S(2)}, u32[]{:S(2)}) %all-to-all-start.14) | async-done | bytes 1048608 | tf_op jit(solution)/shard_map/all_to_all | solution.py:1013
  610.7 17.8 %all-to-all-done.15.refs_1_ = f32[32,72,128]{2,1,0:T(8,128)S(1)} async-done(((f32[32,72,128]{2,1,0:T(8,128)}), f32[32,72,128]{2,1,0:T(8,128)S(1)}, u32[]{:S(2)}, u32[]{:S(2)}) %all-to-all-start.15) | async-done | bytes 1179680 | tf_op jit(solution)/shard_map/all_to_all | solution.py:1016
  637.2 10.4 %shard_map.151 = (f32[4,64,2048]{2,1,0:T(8,128)}, f32[4,8,2048]{2,1,0:T(8,128)}, f32[4,64,2048]{2,1,0:T(8,128)}, f32[4,8,2048]{2,1,0:T(8,128)}) custom-call(f32[4,4]{1,0:T(4,128)S(1)} %copy-done.4, f32[32,72,128]{2,1,0:T(8,128)S(1)} %all-to-all-done.15.refs_1_, bf16[2048,2048]{1,0:T(8,128)(2,1)} %refs_2_.15, ...), custom_call_target="tpu_custom_call" | custom-call | tf_op jit(solution)/shard_map/pallas_call | solution.py:351
  649.9 11.2 %all-to-all-done.17.refs_1_ = f32[32,72,128]{2,1,0:T(8,128)S(1)} async-done(((f32[32,72,128]{2,1,0:T(8,128)}), f32[32,72,128]{2,1,0:T(8,128)S(1)}, u32[]{:S(2)}, u32[]{:S(2)}) %all-to-all-start.17) | async-done | bytes 1179680 | tf_op jit(solution)/shard_map/all_to_all | solution.py:1016
  661.1 11.6 %shard_map.152 = (f32[4,64,2048]{2,1,0:T(8,128)}, f32[4,8,2048]{2,1,0:T(8,128)}, f32[4,64,2048]{2,1,0:T(8,128)}, f32[8,128]{1,0:T(8,128)S(1)}, f32[4,64,2048]{2,1,0:T(8,128)}, /*index=5*/f32[4,8,2048]{2,1,0:T(8,128)}) custom-call(f32[4,4]{1,0:T(4,128)S(1)} %copy-done.4, f32[32,72,128]{2,1,0:T(8,128)S(1)} %all-to-all-done.17.refs_1_, ...), custom_call_target="tpu_custom_call" | custom-call | tf_op jit(solution)/shard_map/pallas_call | solution.py:681
  695.0 24.8 %all-to-all-done.19.own_ref.previous_ref.next_ref = f32[4,4,64,512]{3,2,1,0:T(8,128)S(1)} async-done(((f32[4,4,64,512]{3,2,1,0:T(8,128)}), f32[4,4,64,512]{3,2,1,0:T(8,128)S(1)}, u32[]{:S(2)}, u32[]{:S(2)}) %all-to-all-start.19) | async-done | bytes 2097184 | tf_op jit(solution)/shard_map/all_to_all | solution.py:1057
  (181 shorter events, 360.8 us)
Async XLA Ops:
  9.0 31.1 %collective-permute-start = (f32[5,3,4,512]{3,1,2,0:T(4,128)}, f32[5,3,4,512]{3,1,2,0:T(4,128)S(1)}, u32[]{:S(2)}, u32[]{:S(2)}) collective-permute-start(f32[5,3,4,512]{3,1,2,0:T(4,128)} %pad_maximum_fusion), channel_id=1, source_target_pairs={{0,4},{4,8},{8,12},{12,16},{16,20},{20,24},{24,28},{1,5},{5,9},{9,... | collective-permute-start | bytes 368648 | tf_op jit(solution)/shard_map/ppermute | solution.py:830
  12.9 26.2 %collective-permute-start.1 = (f32[5,3,4,512]{3,1,2,0:T(4,128)}, f32[5,3,4,512]{3,1,2,0:T(4,128)}, u32[]{:S(2)}, u32[]{:S(2)}) collective-permute-start(f32[5,3,4,512]{3,1,2,0:T(4,128)} %pad_maximum_fusion.1), channel_id=1, source_target_pairs={{4,0},{8,4},{12,8},{16,12},{20,16},{24,20},{28,24},{5,1},{9,5},{13... | collective-permute-start | bytes 368648 | tf_op jit(solution)/shard_map/ppermute | solution.py:830
  17.5 66.6 %all-to-all-start = ((f32[4,4,64,512]{3,2,1,0:T(8,128)}), f32[4,4,64,512]{3,2,1,0:T(8,128)}, u32[]{:S(2)}, u32[]{:S(2)}) async-start(f32[4,4,64,512]{3,2,1,0:T(8,128)} %bitcast.136), calls=%async_computation | async-start | bytes 4194304 | tf_op jit(solution)/shard_map/all_to_all | solution.py:985
  84.1 27.9 %all-to-all-start.1 = ((f32[4,4,64,512]{3,2,1,0:T(8,128)}), f32[4,4,64,512]{3,2,1,0:T(8,128)S(1)}, u32[]{:S(2)}, u32[]{:S(2)}) async-start(f32[4,4,64,512]{3,2,1,0:T(8,128)} %copy-done.2), calls=%async_computation.1 | async-start | bytes 4194304 | tf_op jit(solution)/shard_map/all_to_all | solution.py:987
  118.5 31.0 %all-to-all-start.4 = ((f32[32,64,128]{2,1,0:T(8,128)}), f32[32,64,128]{2,1,0:T(8,128)S(1)}, u32[]{:S(2)}, u32[]{:S(2)}) async-start(f32[32,64,128]{2,1,0:T(8,128)} %bitcast.144), calls=%async_computation.4 | async-start | bytes 2097152 | tf_op jit(solution)/shard_map/all_to_all | solution.py:1013
  149.4 29.9 %all-to-all-start.2 = ((f32[32,64,128]{2,1,0:T(8,128)}), f32[32,64,128]{2,1,0:T(8,128)S(1)}, u32[]{:S(2)}, u32[]{:S(2)}) async-start(f32[32,64,128]{2,1,0:T(8,128)} %bitcast.137), calls=%async_computation.2 | async-start | bytes 2097152 | tf_op jit(solution)/shard_map/all_to_all | solution.py:1013
  179.3 32.6 %all-to-all-start.5 = ((f32[32,72,128]{2,1,0:T(8,128)}), f32[32,72,128]{2,1,0:T(8,128)S(1)}, u32[]{:S(2)}, u32[]{:S(2)}) async-start(f32[32,72,128]{2,1,0:T(8,128)} %shard_map.135), calls=%async_computation.5 | async-start | bytes 2359296 | tf_op jit(solution)/shard_map/all_to_all | solution.py:1016
  211.9 32.8 %all-to-all-start.3 = ((f32[32,72,128]{2,1,0:T(8,128)}), f32[32,72,128]{2,1,0:T(8,128)S(1)}, u32[]{:S(2)}, u32[]{:S(2)}) async-start(f32[32,72,128]{2,1,0:T(8,128)} %shard_map.134), calls=%async_computation.3 | async-start | bytes 2359296 | tf_op jit(solution)/shard_map/all_to_all | solution.py:1016
  258.0 29.9 %all-to-all-start.8 = ((f32[32,64,128]{2,1,0:T(8,128)}), f32[32,64,128]{2,1,0:T(8,128)S(1)}, u32[]{:S(2)}, u32[]{:S(2)}) async-start(f32[32,64,128]{2,1,0:T(8,128)} %bitcast.143), calls=%async_computation.8 | async-start | bytes 2097152 | tf_op jit(solution)/shard_map/all_to_all | solution.py:1013
  288.0 29.9 %all-to-all-start.6 = ((f32[32,64,128]{2,1,0:T(8,128)}), f32[32,64,128]{2,1,0:T(8,128)S(1)}, u32[]{:S(2)}, u32[]{:S(2)}) async-start(f32[32,64,128]{2,1,0:T(8,128)} %bitcast.138), calls=%async_computation.6 | async-start | bytes 2097152 | tf_op jit(solution)/shard_map/all_to_all | solution.py:1013
  317.8 32.6 %all-to-all-start.9 = ((f32[32,72,128]{2,1,0:T(8,128)}), f32[32,72,128]{2,1,0:T(8,128)S(1)}, u32[]{:S(2)}, u32[]{:S(2)}) async-start(f32[32,72,128]{2,1,0:T(8,128)} %shard_map.140), calls=%async_computation.9 | async-start | bytes 2359296 | tf_op jit(solution)/shard_map/all_to_all | solution.py:1016
  350.5 32.7 %all-to-all-start.7 = ((f32[32,72,128]{2,1,0:T(8,128)}), f32[32,72,128]{2,1,0:T(8,128)S(1)}, u32[]{:S(2)}, u32[]{:S(2)}) async-start(f32[32,72,128]{2,1,0:T(8,128)} %shard_map.139), calls=%async_computation.7 | async-start | bytes 2359296 | tf_op jit(solution)/shard_map/all_to_all | solution.py:1016
  396.9 29.9 %all-to-all-start.12 = ((f32[32,64,128]{2,1,0:T(8,128)}), f32[32,64,128]{2,1,0:T(8,128)S(1)}, u32[]{:S(2)}, u32[]{:S(2)}) async-start(f32[32,64,128]{2,1,0:T(8,128)} %bitcast.141), calls=%async_computation.12 | async-start | bytes 2097152 | tf_op jit(solution)/shard_map/all_to_all | solution.py:1013
  426.8 29.9 %all-to-all-start.10 = ((f32[32,64,128]{2,1,0:T(8,128)}), f32[32,64,128]{2,1,0:T(8,128)S(1)}, u32[]{:S(2)}, u32[]{:S(2)}) async-start(f32[32,64,128]{2,1,0:T(8,128)} %bitcast.140), calls=%async_computation.10 | async-start | bytes 2097152 | tf_op jit(solution)/shard_map/all_to_all | solution.py:1013
  456.7 32.6 %all-to-all-start.13 = ((f32[32,72,128]{2,1,0:T(8,128)}), f32[32,72,128]{2,1,0:T(8,128)S(1)}, u32[]{:S(2)}, u32[]{:S(2)}) async-start(f32[32,72,128]{2,1,0:T(8,128)} %shard_map.145), calls=%async_computation.13 | async-start | bytes 2359296 | tf_op jit(solution)/shard_map/all_to_all | solution.py:1016
  489.3 32.7 %all-to-all-start.11 = ((f32[32,72,128]{2,1,0:T(8,128)}), f32[32,72,128]{2,1,0:T(8,128)S(1)}, u32[]{:S(2)}, u32[]{:S(2)}) async-start(f32[32,72,128]{2,1,0:T(8,128)} %shard_map.144), calls=%async_computation.11 | async-start | bytes 2359296 | tf_op jit(solution)/shard_map/all_to_all | solution.py:1016
  535.8 29.9 %all-to-all-start.14 = ((f32[32,64,128]{2,1,0:T(8,128)}), f32[32,64,128]{2,1,0:T(8,128)S(1)}, u32[]{:S(2)}, u32[]{:S(2)}) async-start(f32[32,64,128]{2,1,0:T(8,128)} %bitcast.142), calls=%async_computation.14 | async-start | bytes 2097152 | tf_op jit(solution)/shard_map/all_to_all | solution.py:1013
  565.7 29.9 %all-to-all-start.16 = ((f32[32,64,128]{2,1,0:T(8,128)}), f32[32,64,128]{2,1,0:T(8,128)S(1)}, u32[]{:S(2)}, u32[]{:S(2)}) async-start(f32[32,64,128]{2,1,0:T(8,128)} %bitcast.139), calls=%async_computation.16 | async-start | bytes 2097152 | tf_op jit(solution)/shard_map/all_to_all | solution.py:1013
  595.5 32.9 %all-to-all-start.15 = ((f32[32,72,128]{2,1,0:T(8,128)}), f32[32,72,128]{2,1,0:T(8,128)S(1)}, u32[]{:S(2)}, u32[]{:S(2)}) async-start(f32[32,72,128]{2,1,0:T(8,128)} %shard_map.148), calls=%async_computation.15 | async-start | bytes 2359296 | tf_op jit(solution)/shard_map/all_to_all | solution.py:1016
  628.4 32.7 %all-to-all-start.17 = ((f32[32,72,128]{2,1,0:T(8,128)}), f32[32,72,128]{2,1,0:T(8,128)S(1)}, u32[]{:S(2)}, u32[]{:S(2)}) async-start(f32[32,72,128]{2,1,0:T(8,128)} %shard_map.150), calls=%async_computation.17 | async-start | bytes 2359296 | tf_op jit(solution)/shard_map/all_to_all | solution.py:1016
  673.4 10.8 %all-to-all-start.18 = ((f32[32,8,128]{2,1,0:T(8,128)}), f32[32,8,128]{2,1,0:T(8,128)S(1)}, u32[]{:S(2)}, u32[]{:S(2)}) async-start(f32[32,8,128]{2,1,0:T(8,128)} %broadcast_in_dim.108), calls=%async_computation.18 | async-start | bytes 262144 | tf_op jit(solution)/shard_map/all_to_all | solution.py:1055
  690.0 29.7 %all-to-all-start.19 = ((f32[4,4,64,512]{3,2,1,0:T(8,128)}), f32[4,4,64,512]{3,2,1,0:T(8,128)S(1)}, u32[]{:S(2)}, u32[]{:S(2)}) async-start(f32[4,4,64,512]{3,2,1,0:T(8,128)} %shard_map.153), calls=%async_computation.19 | async-start | bytes 4194304 | tf_op jit(solution)/shard_map/all_to_all | solution.py:1057
  719.8 15.2 %collective-permute-start.4 = (f32[4,1,512]{2,1,0:T(1,128)S(1)}, f32[4,1,512]{2,1,0:T(1,128)S(1)}, u32[]{:S(2)}, u32[]{:S(2)}) collective-permute-start(f32[4,1,512]{2,1,0:T(1,128)S(1)} %get-tuple-element.108), channel_id=1, source_target_pairs={{0,4},{4,8},{8,12},{12,16},{16,20},{20,24},{24,28},{1,5},{5,9},{9,... | collective-permute-start | bytes 24584 | tf_op jit(solution)/shard_map/ppermute | solution.py:830
  722.1 12.9 %collective-permute-start.5 = (f32[4,1,512]{2,1,0:T(1,128)S(1)}, f32[4,1,512]{2,1,0:T(1,128)S(1)}, u32[]{:S(2)}, u32[]{:S(2)}) collective-permute-start(f32[4,1,512]{2,1,0:T(1,128)S(1)} %get-tuple-element.107), channel_id=1, source_target_pairs={{4,0},{8,4},{12,8},{16,12},{20,16},{24,20},{28,24},{5,1},{9,5},{13... | collective-permute-start | bytes 24584 | tf_op jit(solution)/shard_map/ppermute | solution.py:830
  (24 other events, 200.6 us)

commit v7 on v6

--- a/solution.py
+++ b/solution.py
@@ -231,7 +231,7 @@
 
 
 def take_lines(got, lines, planes, rows):
-    devices, _, columns = got.shape
+    devices, _, _, columns = got.shape
     parts = devices // planes
     half = planes * (rows + spare)
     main = planes * rows
@@ -240,10 +240,11 @@
         lanes = slice(part * columns, (part + 1) * columns)
         edges = []
         for m in range(planes):
-            high, low = halves(got[m * parts + part, :rows, :])
+            high, low = halves(got[m * parts + part, : rows // 4].reshape(rows, columns))
             lines[m * rows : (m + 1) * rows, lanes] = high
             lines[half + m * rows : half + (m + 1) * rows, lanes] = low
-            edges.append(jnp.where(edge_rows, got[m * parts + part, rows:, :], 0.0))
+            edge = got[m * parts + part, rows // 4]
+            edges.append(jnp.where(edge_rows, jnp.concatenate([edge, edge], axis=0), 0.0))
         high, low = halves(jnp.concatenate(edges, axis=0))
         lines[main:half, lanes] = high
         lines[half + main :, lanes] = low
@@ -427,20 +428,21 @@
         result = jnp.dot(back[piece(n, block), :], spectral[...], preferred_element_type=jnp.float32)
         result = result[:, :columns] + result[:, columns:]
         for part in range(group):
-            buffer[n * group + part, :rows, :] = result[part * rows : (part + 1) * rows]
+            own = result[part * rows : (part + 1) * rows]
+            buffer[n * group + part, : rows // 4] = own.reshape(rows // 4, 4, columns)
         return carry
 
     lax.fori_loop(0, blocks, reverse, 0)
-    rest = aux_ref[2:, :]
+    rest = aux_ref[2:4, :]
 
     def close(n, carry):
         for part in range(group):
             own = n * group + part
-            above = buffer[jnp.maximum(own - 1, 0), rows - 1 : rows, :]
+            above = buffer[jnp.maximum(own - 1, 0), rows // 4 - 1, 3:4, :]
             above = jnp.where(own > 0, above, 0.0)
-            below = buffer[jnp.minimum(own + 1, devices - 1), 0:1, :]
+            below = buffer[jnp.minimum(own + 1, devices - 1), 0, 0:1, :]
             below = jnp.where(own + 1 < devices, below, 0.0)
-            buffer[own, rows:, :] = jnp.concatenate([above, below, rest], axis=0)
+            buffer[own, rows // 4] = jnp.concatenate([above, below, rest], axis=0)
         out.start(n)
         return carry
 
@@ -456,14 +458,14 @@
         functools.partial(column_kernel, rows, block),
         in_specs=[vector, vector, anywhere, anywhere, vector, vector],
         out_specs=anywhere,
-        out_shape=pltpu.HBM((devices, rows + spare, columns), jnp.float32),
+        out_shape=pltpu.HBM((devices, rows // 4 + 1, 4, columns), jnp.float32),
         scratch_shapes=[
             pltpu.VMEM((full, columns), jnp.float32),
             pltpu.VMEM((full, full), jnp.bfloat16),
             pltpu.VMEM((full, full), jnp.bfloat16),
             pltpu.VMEM((full, 2 * columns), jnp.bfloat16),
             pltpu.VMEM((full, 2 * columns), jnp.bfloat16),
-            pltpu.VMEM((devices, rows + spare, columns), jnp.float32),
+            pltpu.VMEM((devices, rows // 4 + 1, 4, columns), jnp.float32),
             pltpu.SemaphoreType.DMA((full // block, 1)),
             pltpu.SemaphoreType.DMA((2, full // block, 1)),
             pltpu.SemaphoreType.DMA((full // block, 1)),
@@ -502,7 +504,7 @@
     if not last:
         basis_semaphores, out_semaphores = take(), take()
     planes, rows, full = diagonal.shape
-    devices, _, columns = got.shape
+    devices, _, _, columns = got.shape
     parts = devices // planes
     half = planes * (rows + spare)
     main = planes * rows
@@ -619,7 +621,7 @@
 
 def turn_lines(stage, last, got, part, operator, basis_z, basis_y, state, chunks):
     planes, rows, full = operator[0].shape
-    _, _, columns = got.shape
+    columns = got.shape[-1]
     block = min(512, full // chunks)
     blocks = full // block
     field_shape = pltpu.HBM((planes, rows, full), jnp.float32)
@@ -1015,7 +1017,7 @@
             got = column_lines(got, given, basis_xt, basis_x, along, other[chunk], rows)
             gots.append(lax.all_to_all(got, both, 0, 0, tiled=True))
         if stage > 0:
-            state["scalars"] = numbers_of(gots[0][:, rows:], state.get("scalars"))
+            state["scalars"] = numbers_of(gots[0][:, rows // 4], state.get("scalars"))
         part = None
         if chunks > 1:
             part = part_lines(stage, gots[0], basis_z, basis_y, rows, chunks, state)

time: 753 us -> 742 us (0.985)
  waiting for transfers between devices: 286 us -> 275 us
    all_to_all x8, waiting for transfers between devices: 129 us -> 119 us  [apply(): gots.append(lax.all_to_all(got, both, 0, 0, tiled=True))]
where the time goes in v7:
time: 742 us; the launch traced here: 732 us
  waiting for transfers between devices  275 us (37%)
  Pallas kernels  236 us (32%)
  starting transfers between devices  118 us (16%)
  local copies, waits for them, and re-layouts  52.2 us (7%)
  other arithmetic  41.6 us (6%)
  between operations  9.05 us (1%)
    all_to_all x8, waiting for transfers between devices, apply(): gots.append(lax.all_to_all(got, both, 0, 0, tiled=True))  119 us
    all_to_all x8, waiting for transfers between devices, apply(): got = lax.all_to_all(sent, both, 0, 0, tiled=True).reshape(full_x, columns)  116 us
    pallas_call x8, Pallas kernels, column_lines(): pl.pallas_call(functools.partial(column_kernel, rows, block), in_specs=[v...  80.8 us
    pallas_call x4, Pallas kernels, turn_lines(): pl.pallas_call(functools.partial(turn_kernel, stage, last, block, chunks)...  52 us
    all_to_all x8, starting transfers between devices, apply(): got = lax.all_to_all(sent, both, 0, 0, tiled=True).reshape(full_x, columns)  38.7 us
    all_to_all x8, starting transfers between devices, apply(): gots.append(lax.all_to_all(got, both, 0, 0, tiled=True))  37.2 us
    pallas_call x4, Pallas kernels, part_lines(): pl.pallas_call(functools.partial(part_kernel, stage, rows, block), in_spe...  35.5 us
    pallas_call x4, Pallas kernels, more_lines(): pl.pallas_call(functools.partial(more_kernel, block, chunk), in_specs=[sc...  28.1 us
  transfers between devices with their start and end apart: 28, of which 20 were waited for; matrix products, arithmetic and copies ran while one was open for 10% of the time, Pallas kernels for 23%

profile of v7, /device:TPU:9, one launch (start us, length us, event | category | flops | bytes accessed | tf_op | source)
XLA Modules:
  0.0 732.0 jit_solution(1607613039123854594)
XLA Ops:
  57.4 25.3 %shard_map.131 = (f32[4,4,64,512]{3,2,1,0:T(8,128)S(1)}, f32[3,4,256,512]{3,2,1,0:T(8,128)}) custom-call(f32[3,4,256,512]{3,2,1,0:T(8,128)} %bitcast.140, f32[4,256,512]{2,1,0:T(8,128)} %copy-done.10, f32[4,256,512]{2,1,0:T(8,128)} %get-tuple-element.117.code_ref, f32[5,4,8,512]{3,2,1,0:T(8,128)} %pad.50.above_ref, f32[5,4,8,512]{3,2,1,0:T(8,128)} %pad.51.below_ref, ...), custom_call_target="tpu_custom_call" | custom-call | tf_op jit(solution)/shard_map/pallas_call | solution.py:809
  87.7 12.3 %copy.237 = bf16[2048,2048]{0,1:T(8,128)(2,1)} copy(bf16[2048,2048]{1,0:T(8,128)(2,1)} %back_ref.15) | data formatting | bytes 16777216 | tf_op args[6]
  100.0 11.9 %all-to-all-done.1.field_ref = f32[4,4,64,512]{3,2,1,0:T(8,128)S(1)} async-done(((f32[4,4,64,512]{3,2,1,0:T(8,128)}), f32[4,4,64,512]{3,2,1,0:T(8,128)S(1)}, u32[]{:S(2)}, u32[]{:S(2)}) %all-to-all-start.1) | async-done | bytes 2097184 | tf_op jit(solution)/shard_map/all_to_all | solution.py:989
  131.2 18.2 %all-to-all-done.4 = f32[32,64,128]{2,1,0:T(8,128)S(1)} async-done(((f32[32,64,128]{2,1,0:T(8,128)}), f32[32,64,128]{2,1,0:T(8,128)S(1)}, u32[]{:S(2)}, u32[]{:S(2)}) %all-to-all-start.4) | async-done | bytes 1048608 | tf_op jit(solution)/shard_map/all_to_all | solution.py:1015
  166.6 12.7 %all-to-all-done.2 = f32[32,64,128]{2,1,0:T(8,128)S(1)} async-done(((f32[32,64,128]{2,1,0:T(8,128)}), f32[32,64,128]{2,1,0:T(8,128)S(1)}, u32[]{:S(2)}, u32[]{:S(2)}) %all-to-all-start.2) | async-done | bytes 1048608 | tf_op jit(solution)/shard_map/all_to_all | solution.py:1015
  183.9 10.1 %shard_map.134 = f32[32,17,4,128]{3,2,1,0:T(4,128)} custom-call(f32[2048,128]{1,0:T(8,128)S(1)} %bitcast.110, f32[8,128]{1,0:T(8,128)S(1)} %broadcast_2_aux_ref.2.aux_ref, bf16[2048,2048]{1,0:T(8,128)(2,1)} %bitcast.128, bf16[2048,2048]{1,0:T(8,128)(2,1)} %back_ref.15, f32[2048,1]{1,0:T(8,128)S(1)} %copy.238.along_ref, f32[1,128]{1,0:T(1,128)S(1)} %get-tuple-element.126.other_ref), custom_call_target="tpu_custom_call" | custom-call | tf_op jit(solution)/shard_map/pallas_call | solution.py:457
  194.1 16.5 %all-to-all-done.5.refs_1_ = f32[32,17,4,128]{3,2,1,0:T(4,128)S(1)} async-done(((f32[32,17,4,128]{3,2,1,0:T(4,128)}), f32[32,17,4,128]{3,2,1,0:T(4,128)S(1)}, u32[]{:S(2)}, u32[]{:S(2)}) %all-to-all-start.5) | async-done | bytes 1114144 | tf_op jit(solution)/shard_map/all_to_all | solution.py:1018
  226.9 15.1 %all-to-all-done.3.refs_1_ = f32[32,17,4,128]{3,2,1,0:T(4,128)S(1)} async-done(((f32[32,17,4,128]{3,2,1,0:T(4,128)}), f32[32,17,4,128]{3,2,1,0:T(4,128)S(1)}, u32[]{:S(2)}, u32[]{:S(2)}) %all-to-all-start.3) | async-done | bytes 1114144 | tf_op jit(solution)/shard_map/all_to_all | solution.py:1018
  242.0 13.2 %shard_map.137 = (f32[4,64,2048]{2,1,0:T(8,128)}, f32[4,8,2048]{2,1,0:T(8,128)}, f32[4,64,2048]{2,1,0:T(8,128)}, f32[4,8,64,128]{3,2,1,0:T(8,128)}) custom-call(f32[4,4]{1,0:T(4,128)S(1)} %copy-done.4, f32[32,17,4,128]{3,2,1,0:T(4,128)S(1)} %all-to-all-done.3.refs_1_, bf16[2048,2048]{1,0:T(8,128)(2,1)} %refs_2_.15, f32[4,64,2048]{2,1,0:T(8,128)} %bitcast.135, ...), custom_call_target="tpu_custom_call" | custom-call | tf_op jit(solution)/shard_map/pallas_call | solution.py:683
  266.9 18.2 %all-to-all-done.8 = f32[32,64,128]{2,1,0:T(8,128)S(1)} async-done(((f32[32,64,128]{2,1,0:T(8,128)}), f32[32,64,128]{2,1,0:T(8,128)S(1)}, u32[]{:S(2)}, u32[]{:S(2)}) %all-to-all-start.8) | async-done | bytes 1048608 | tf_op jit(solution)/shard_map/all_to_all | solution.py:1015
  303.3 11.7 %all-to-all-done.6 = f32[32,64,128]{2,1,0:T(8,128)S(1)} async-done(((f32[32,64,128]{2,1,0:T(8,128)}), f32[32,64,128]{2,1,0:T(8,128)S(1)}, u32[]{:S(2)}, u32[]{:S(2)}) %all-to-all-start.6) | async-done | bytes 1048608 | tf_op jit(solution)/shard_map/all_to_all | solution.py:1015
  319.5 10.1 %shard_map.139 = f32[32,17,4,128]{3,2,1,0:T(4,128)} custom-call(f32[2048,128]{1,0:T(8,128)S(1)} %bitcast.113, f32[8,128]{1,0:T(8,128)S(1)} %broadcast_2_aux_ref.2.aux_ref, bf16[2048,2048]{1,0:T(8,128)(2,1)} %bitcast.130, bf16[2048,2048]{1,0:T(8,128)(2,1)} %back_ref.15, f32[2048,1]{1,0:T(8,128)S(1)} %copy.238.along_ref, f32[1,128]{1,0:T(1,128)S(1)} %get-tuple-element.126.other_ref), custom_call_target="tpu_custom_call" | custom-call | tf_op jit(solution)/shard_map/pallas_call | solution.py:457
  329.7 16.5 %all-to-all-done.9.refs_1_ = f32[32,17,4,128]{3,2,1,0:T(4,128)S(1)} async-done(((f32[32,17,4,128]{3,2,1,0:T(4,128)}), f32[32,17,4,128]{3,2,1,0:T(4,128)S(1)}, u32[]{:S(2)}, u32[]{:S(2)}) %all-to-all-start.9) | async-done | bytes 1114144 | tf_op jit(solution)/shard_map/all_to_all | solution.py:1018
  362.8 14.6 %all-to-all-done.7.refs_1_ = f32[32,17,4,128]{3,2,1,0:T(4,128)S(1)} async-done(((f32[32,17,4,128]{3,2,1,0:T(4,128)}), f32[32,17,4,128]{3,2,1,0:T(4,128)S(1)}, u32[]{:S(2)}, u32[]{:S(2)}) %all-to-all-start.7) | async-done | bytes 1114144 | tf_op jit(solution)/shard_map/all_to_all | solution.py:1018
  377.4 13.7 %shard_map.142 = (f32[4,64,2048]{2,1,0:T(8,128)}, f32[4,8,2048]{2,1,0:T(8,128)}, f32[4,64,2048]{2,1,0:T(8,128)}, f32[4,64,2048]{2,1,0:T(8,128)}, f32[4,8,2048]{2,1,0:T(8,128)}, /*index=5*/f32[4,8,64,128]{3,2,1,0:T(8,128)}) custom-call(f32[4,4]{1,0:T(4,128)S(1)} %copy-done.4, f32[32,17,4,128]{3,2,1,0:T(4,128)S(1)} %all-to-all-done.7.refs_1_, ...), custom_call_target="tpu_custom_call" | custom-call | tf_op jit(solution)/shard_map/pallas_call | solution.py:683
  403.1 18.1 %all-to-all-done.12 = f32[32,64,128]{2,1,0:T(8,128)S(1)} async-done(((f32[32,64,128]{2,1,0:T(8,128)}), f32[32,64,128]{2,1,0:T(8,128)S(1)}, u32[]{:S(2)}, u32[]{:S(2)}) %all-to-all-start.12) | async-done | bytes 1048608 | tf_op jit(solution)/shard_map/all_to_all | solution.py:1015
  465.8 16.5 %all-to-all-done.13.refs_1_ = f32[32,17,4,128]{3,2,1,0:T(4,128)S(1)} async-done(((f32[32,17,4,128]{3,2,1,0:T(4,128)}), f32[32,17,4,128]{3,2,1,0:T(4,128)S(1)}, u32[]{:S(2)}, u32[]{:S(2)}) %all-to-all-start.13) | async-done | bytes 1114144 | tf_op jit(solution)/shard_map/all_to_all | solution.py:1018
  500.6 13.0 %all-to-all-done.11.refs_1_ = f32[32,17,4,128]{3,2,1,0:T(4,128)S(1)} async-done(((f32[32,17,4,128]{3,2,1,0:T(4,128)}), f32[32,17,4,128]{3,2,1,0:T(4,128)S(1)}, u32[]{:S(2)}, u32[]{:S(2)}) %all-to-all-start.11) | async-done | bytes 1114144 | tf_op jit(solution)/shard_map/all_to_all | solution.py:1018
  513.6 13.7 %shard_map.147 = (f32[4,64,2048]{2,1,0:T(8,128)}, f32[4,8,2048]{2,1,0:T(8,128)}, f32[4,64,2048]{2,1,0:T(8,128)}, f32[4,64,2048]{2,1,0:T(8,128)}, f32[4,8,2048]{2,1,0:T(8,128)}, /*index=5*/f32[4,8,64,128]{3,2,1,0:T(8,128)}) custom-call(f32[4,4]{1,0:T(4,128)S(1)} %copy-done.4, f32[32,17,4,128]{3,2,1,0:T(4,128)S(1)} %all-to-all-done.11.refs_1_, ...), custom_call_target="tpu_custom_call" | custom-call | tf_op jit(solution)/shard_map/pallas_call | solution.py:683
  539.0 18.2 %all-to-all-done.14 = f32[32,64,128]{2,1,0:T(8,128)S(1)} async-done(((f32[32,64,128]{2,1,0:T(8,128)}), f32[32,64,128]{2,1,0:T(8,128)S(1)}, u32[]{:S(2)}, u32[]{:S(2)}) %all-to-all-start.14) | async-done | bytes 1048608 | tf_op jit(solution)/shard_map/all_to_all | solution.py:1015
  602.0 16.5 %all-to-all-done.15.refs_1_ = f32[32,17,4,128]{3,2,1,0:T(4,128)S(1)} async-done(((f32[32,17,4,128]{3,2,1,0:T(4,128)}), f32[32,17,4,128]{3,2,1,0:T(4,128)S(1)}, u32[]{:S(2)}, u32[]{:S(2)}) %all-to-all-start.15) | async-done | bytes 1114144 | tf_op jit(solution)/shard_map/all_to_all | solution.py:1018
  627.3 10.4 %shard_map.151 = (f32[4,64,2048]{2,1,0:T(8,128)}, f32[4,8,2048]{2,1,0:T(8,128)}, f32[4,64,2048]{2,1,0:T(8,128)}, f32[4,8,2048]{2,1,0:T(8,128)}) custom-call(f32[4,4]{1,0:T(4,128)S(1)} %copy-done.4, f32[32,17,4,128]{3,2,1,0:T(4,128)S(1)} %all-to-all-done.15.refs_1_, bf16[2048,2048]{1,0:T(8,128)(2,1)} %refs_2_.15, ...), custom_call_target="tpu_custom_call" | custom-call | tf_op jit(solution)/shard_map/pallas_call | solution.py:352
  649.8 11.5 %shard_map.152 = (f32[4,64,2048]{2,1,0:T(8,128)}, f32[4,8,2048]{2,1,0:T(8,128)}, f32[4,64,2048]{2,1,0:T(8,128)}, f32[8,128]{1,0:T(8,128)S(1)}, f32[4,64,2048]{2,1,0:T(8,128)}, /*index=5*/f32[4,8,2048]{2,1,0:T(8,128)}) custom-call(f32[4,4]{1,0:T(4,128)S(1)} %copy-done.4, f32[32,17,4,128]{3,2,1,0:T(4,128)S(1)} %all-to-all-done.17.refs_1_, ...), custom_call_target="tpu_custom_call" | custom-call | tf_op jit(solution)/shard_map/pallas_call | solution.py:683
  683.6 24.8 %all-to-all-done.19.own_ref.previous_ref.next_ref = f32[4,4,64,512]{3,2,1,0:T(8,128)S(1)} async-done(((f32[4,4,64,512]{3,2,1,0:T(8,128)}), f32[4,4,64,512]{3,2,1,0:T(8,128)S(1)}, u32[]{:S(2)}, u32[]{:S(2)}) %all-to-all-start.19) | async-done | bytes 2097184 | tf_op jit(solution)/shard_map/all_to_all | solution.py:1059
  (184 shorter events, 360.2 us)
Async XLA Ops:
  9.0 31.1 %collective-permute-start = (f32[5,3,4,512]{3,1,2,0:T(4,128)}, f32[5,3,4,512]{3,1,2,0:T(4,128)S(1)}, u32[]{:S(2)}, u32[]{:S(2)}) collective-permute-start(f32[5,3,4,512]{3,1,2,0:T(4,128)} %pad_maximum_fusion), channel_id=1, source_target_pairs={{0,4},{4,8},{8,12},{12,16},{16,20},{20,24},{24,28},{1,5},{5,9},{9,... | collective-permute-start | bytes 368648 | tf_op jit(solution)/shard_map/ppermute | solution.py:832
  12.9 26.2 %collective-permute-start.1 = (f32[5,3,4,512]{3,1,2,0:T(4,128)}, f32[5,3,4,512]{3,1,2,0:T(4,128)}, u32[]{:S(2)}, u32[]{:S(2)}) collective-permute-start(f32[5,3,4,512]{3,1,2,0:T(4,128)} %pad_maximum_fusion.1), channel_id=1, source_target_pairs={{4,0},{8,4},{12,8},{16,12},{20,16},{24,20},{28,24},{5,1},{9,5},{13... | collective-permute-start | bytes 368648 | tf_op jit(solution)/shard_map/ppermute | solution.py:832
  17.5 66.6 %all-to-all-start = ((f32[4,4,64,512]{3,2,1,0:T(8,128)}), f32[4,4,64,512]{3,2,1,0:T(8,128)}, u32[]{:S(2)}, u32[]{:S(2)}) async-start(f32[4,4,64,512]{3,2,1,0:T(8,128)} %bitcast.142), calls=%async_computation | async-start | bytes 4194304 | tf_op jit(solution)/shard_map/all_to_all | solution.py:987
  84.1 27.9 %all-to-all-start.1 = ((f32[4,4,64,512]{3,2,1,0:T(8,128)}), f32[4,4,64,512]{3,2,1,0:T(8,128)S(1)}, u32[]{:S(2)}, u32[]{:S(2)}) async-start(f32[4,4,64,512]{3,2,1,0:T(8,128)} %copy-done.2), calls=%async_computation.1 | async-start | bytes 4194304 | tf_op jit(solution)/shard_map/all_to_all | solution.py:989
  118.5 31.0 %all-to-all-start.4 = ((f32[32,64,128]{2,1,0:T(8,128)}), f32[32,64,128]{2,1,0:T(8,128)S(1)}, u32[]{:S(2)}, u32[]{:S(2)}) async-start(f32[32,64,128]{2,1,0:T(8,128)} %bitcast.150), calls=%async_computation.4 | async-start | bytes 2097152 | tf_op jit(solution)/shard_map/all_to_all | solution.py:1015
  149.4 29.9 %all-to-all-start.2 = ((f32[32,64,128]{2,1,0:T(8,128)}), f32[32,64,128]{2,1,0:T(8,128)S(1)}, u32[]{:S(2)}, u32[]{:S(2)}) async-start(f32[32,64,128]{2,1,0:T(8,128)} %bitcast.143), calls=%async_computation.2 | async-start | bytes 2097152 | tf_op jit(solution)/shard_map/all_to_all | solution.py:1015
  179.3 31.2 %all-to-all-start.5 = ((f32[32,17,4,128]{3,2,1,0:T(4,128)}), f32[32,17,4,128]{3,2,1,0:T(4,128)S(1)}, u32[]{:S(2)}, u32[]{:S(2)}) async-start(f32[32,17,4,128]{3,2,1,0:T(4,128)} %shard_map.135), calls=%async_computation.5 | async-start | bytes 2228224 | tf_op jit(solution)/shard_map/all_to_all | solution.py:1018
  210.6 31.4 %all-to-all-start.3 = ((f32[32,17,4,128]{3,2,1,0:T(4,128)}), f32[32,17,4,128]{3,2,1,0:T(4,128)S(1)}, u32[]{:S(2)}, u32[]{:S(2)}) async-start(f32[32,17,4,128]{3,2,1,0:T(4,128)} %shard_map.134), calls=%async_computation.3 | async-start | bytes 2228224 | tf_op jit(solution)/shard_map/all_to_all | solution.py:1018
  255.2 29.9 %all-to-all-start.8 = ((f32[32,64,128]{2,1,0:T(8,128)}), f32[32,64,128]{2,1,0:T(8,128)S(1)}, u32[]{:S(2)}, u32[]{:S(2)}) async-start(f32[32,64,128]{2,1,0:T(8,128)} %bitcast.149), calls=%async_computation.8 | async-start | bytes 2097152 | tf_op jit(solution)/shard_map/all_to_all | solution.py:1015
  285.1 29.9 %all-to-all-start.6 = ((f32[32,64,128]{2,1,0:T(8,128)}), f32[32,64,128]{2,1,0:T(8,128)S(1)}, u32[]{:S(2)}, u32[]{:S(2)}) async-start(f32[32,64,128]{2,1,0:T(8,128)} %bitcast.144), calls=%async_computation.6 | async-start | bytes 2097152 | tf_op jit(solution)/shard_map/all_to_all | solution.py:1015
  314.9 31.2 %all-to-all-start.9 = ((f32[32,17,4,128]{3,2,1,0:T(4,128)}), f32[32,17,4,128]{3,2,1,0:T(4,128)S(1)}, u32[]{:S(2)}, u32[]{:S(2)}) async-start(f32[32,17,4,128]{3,2,1,0:T(4,128)} %shard_map.140), calls=%async_computation.9 | async-start | bytes 2228224 | tf_op jit(solution)/shard_map/all_to_all | solution.py:1018
  346.2 31.3 %all-to-all-start.7 = ((f32[32,17,4,128]{3,2,1,0:T(4,128)}), f32[32,17,4,128]{3,2,1,0:T(4,128)S(1)}, u32[]{:S(2)}, u32[]{:S(2)}) async-start(f32[32,17,4,128]{3,2,1,0:T(4,128)} %shard_map.139), calls=%async_computation.7 | async-start | bytes 2228224 | tf_op jit(solution)/shard_map/all_to_all | solution.py:1018
  391.1 30.1 %all-to-all-start.12 = ((f32[32,64,128]{2,1,0:T(8,128)}), f32[32,64,128]{2,1,0:T(8,128)S(1)}, u32[]{:S(2)}, u32[]{:S(2)}) async-start(f32[32,64,128]{2,1,0:T(8,128)} %bitcast.147), calls=%async_computation.12 | async-start | bytes 2097152 | tf_op jit(solution)/shard_map/all_to_all | solution.py:1015
  421.2 29.9 %all-to-all-start.10 = ((f32[32,64,128]{2,1,0:T(8,128)}), f32[32,64,128]{2,1,0:T(8,128)S(1)}, u32[]{:S(2)}, u32[]{:S(2)}) async-start(f32[32,64,128]{2,1,0:T(8,128)} %bitcast.146), calls=%async_computation.10 | async-start | bytes 2097152 | tf_op jit(solution)/shard_map/all_to_all | solution.py:1015
  451.1 31.2 %all-to-all-start.13 = ((f32[32,17,4,128]{3,2,1,0:T(4,128)}), f32[32,17,4,128]{3,2,1,0:T(4,128)S(1)}, u32[]{:S(2)}, u32[]{:S(2)}) async-start(f32[32,17,4,128]{3,2,1,0:T(4,128)} %shard_map.145), calls=%async_computation.13 | async-start | bytes 2228224 | tf_op jit(solution)/shard_map/all_to_all | solution.py:1018
  482.3 31.3 %all-to-all-start.11 = ((f32[32,17,4,128]{3,2,1,0:T(4,128)}), f32[32,17,4,128]{3,2,1,0:T(4,128)S(1)}, u32[]{:S(2)}, u32[]{:S(2)}) async-start(f32[32,17,4,128]{3,2,1,0:T(4,128)} %shard_map.144), calls=%async_computation.11 | async-start | bytes 2228224 | tf_op jit(solution)/shard_map/all_to_all | solution.py:1018
  527.3 29.9 %all-to-all-start.14 = ((f32[32,64,128]{2,1,0:T(8,128)}), f32[32,64,128]{2,1,0:T(8,128)S(1)}, u32[]{:S(2)}, u32[]{:S(2)}) async-start(f32[32,64,128]{2,1,0:T(8,128)} %bitcast.148), calls=%async_computation.14 | async-start | bytes 2097152 | tf_op jit(solution)/shard_map/all_to_all | solution.py:1015
  557.2 30.1 %all-to-all-start.16 = ((f32[32,64,128]{2,1,0:T(8,128)}), f32[32,64,128]{2,1,0:T(8,128)S(1)}, u32[]{:S(2)}, u32[]{:S(2)}) async-start(f32[32,64,128]{2,1,0:T(8,128)} %bitcast.145), calls=%async_computation.16 | async-start | bytes 2097152 | tf_op jit(solution)/shard_map/all_to_all | solution.py:1015
  587.3 31.2 %all-to-all-start.15 = ((f32[32,17,4,128]{3,2,1,0:T(4,128)}), f32[32,17,4,128]{3,2,1,0:T(4,128)S(1)}, u32[]{:S(2)}, u32[]{:S(2)}) async-start(f32[32,17,4,128]{3,2,1,0:T(4,128)} %shard_map.148), calls=%async_computation.15 | async-start | bytes 2228224 | tf_op jit(solution)/shard_map/all_to_all | solution.py:1018
  618.5 31.3 %all-to-all-start.17 = ((f32[32,17,4,128]{3,2,1,0:T(4,128)}), f32[32,17,4,128]{3,2,1,0:T(4,128)S(1)}, u32[]{:S(2)}, u32[]{:S(2)}) async-start(f32[32,17,4,128]{3,2,1,0:T(4,128)} %shard_map.150), calls=%async_computation.17 | async-start | bytes 2228224 | tf_op jit(solution)/shard_map/all_to_all | solution.py:1018
  662.0 10.8 %all-to-all-start.18 = ((f32[32,8,128]{2,1,0:T(8,128)}), f32[32,8,128]{2,1,0:T(8,128)S(1)}, u32[]{:S(2)}, u32[]{:S(2)}) async-start(f32[32,8,128]{2,1,0:T(8,128)} %broadcast_in_dim.108), calls=%async_computation.18 | async-start | bytes 262144 | tf_op jit(solution)/shard_map/all_to_all | solution.py:1057
  678.6 29.7 %all-to-all-start.19 = ((f32[4,4,64,512]{3,2,1,0:T(8,128)}), f32[4,4,64,512]{3,2,1,0:T(8,128)S(1)}, u32[]{:S(2)}, u32[]{:S(2)}) async-start(f32[4,4,64,512]{3,2,1,0:T(8,128)} %shard_map.153), calls=%async_computation.19 | async-start | bytes 4194304 | tf_op jit(solution)/shard_map/all_to_all | solution.py:1059
  708.4 15.2 %collective-permute-start.4 = (f32[4,1,512]{2,1,0:T(1,128)S(1)}, f32[4,1,512]{2,1,0:T(1,128)S(1)}, u32[]{:S(2)}, u32[]{:S(2)}) collective-permute-start(f32[4,1,512]{2,1,0:T(1,128)S(1)} %get-tuple-element.108), channel_id=1, source_target_pairs={{0,4},{4,8},{8,12},{12,16},{16,20},{20,24},{24,28},{1,5},{5,9},{9,... | collective-permute-start | bytes 24584 | tf_op jit(solution)/shard_map/ppermute | solution.py:832
  710.7 12.9 %collective-permute-start.5 = (f32[4,1,512]{2,1,0:T(1,128)S(1)}, f32[4,1,512]{2,1,0:T(1,128)S(1)}, u32[]{:S(2)}, u32[]{:S(2)}) collective-permute-start(f32[4,1,512]{2,1,0:T(1,128)S(1)} %get-tuple-element.107), channel_id=1, source_target_pairs={{4,0},{8,4},{12,8},{16,12},{20,16},{24,20},{28,24},{5,1},{9,5},{13... | collective-permute-start | bytes 24584 | tf_op jit(solution)/shard_map/ppermute | solution.py:832
  (24 other events, 200.6 us)

commit v8 on v7

--- a/solution.py
+++ b/solution.py
@@ -747,9 +747,9 @@
         return carry
 
     safe = planes * (middle // 8)
-    lax.fori_loop(0, safe, advance, 0, unroll=4)
+    lax.fori_loop(0, safe, advance, 0, unroll=8)
     wait_all(late)
-    lax.fori_loop(safe, planes * tiles, advance, 0, unroll=4)
+    lax.fori_loop(safe, planes * tiles, advance, 0, unroll=8)
 
     def settle(index, carry):
         k = index // tiles
@@ -774,7 +774,7 @@
             kept[c, k, own, :] = result
         return carry
 
-    lax.fori_loop(0, planes * tiles, settle, 0, unroll=4)
+    lax.fori_loop(0, planes * tiles, settle, 0, unroll=8)
     done = start_all(
         [(kept.at[c, :, pad : pad + count, :span], predicted_ref.at[c]) for c in range(3)], late_semaphores
     )
@@ -861,7 +861,7 @@
         out_specs=pl.BlockSpec((1, planes, rows, span), lambda n: (n, 0, 0, 0)),
         out_shape=pltpu.HBM((pieces, planes, rows, span), jnp.float32),
         compiler_params=params(20),
-    )(numbers, sums, pressure, direction, lifted)
+    )(numbers, sums, *far(pressure, direction, lifted))
 
 
 def correct_kernel(

time: 742 us -> 741 us (level)
    unnamed x44 -> x40, local copies, waits for them, and re-layouts: 27.2 us -> 24 us
where the time goes in v8:
time: 741 us; the launch traced here: 731 us
  waiting for transfers between devices  274 us (37%)
  Pallas kernels  238 us (32%)
  starting transfers between devices  118 us (16%)
  local copies, waits for them, and re-layouts  49 us (7%)
  other arithmetic  42.4 us (6%)
  between operations  8.86 us (1%)
    all_to_all x8, waiting for transfers between devices, apply(): gots.append(lax.all_to_all(got, both, 0, 0, tiled=True))  119 us
    all_to_all x8, waiting for transfers between devices, apply(): got = lax.all_to_all(sent, both, 0, 0, tiled=True).reshape(full_x, columns)  116 us
    pallas_call x8, Pallas kernels, column_lines(): pl.pallas_call(functools.partial(column_kernel, rows, block), in_specs=[v...  80.8 us
    pallas_call x4, Pallas kernels, turn_lines(): pl.pallas_call(functools.partial(turn_kernel, stage, last, block, chunks)...  52 us
    all_to_all x8, starting transfers between devices, apply(): got = lax.all_to_all(sent, both, 0, 0, tiled=True).reshape(full_x, columns)  38.7 us
    all_to_all x8, starting transfers between devices, apply(): gots.append(lax.all_to_all(got, both, 0, 0, tiled=True))  37.2 us
    pallas_call x4, Pallas kernels, part_lines(): pl.pallas_call(functools.partial(part_kernel, stage, rows, block), in_spe...  35.5 us
    pallas_call x4, Pallas kernels, more_lines(): pl.pallas_call(functools.partial(more_kernel, block, chunk), in_specs=[sc...  28 us
  transfers between devices with their start and end apart: 28, of which 20 were waited for; matrix products, arithmetic and copies ran while one was open for 10% of the time, Pallas kernels for 23%

profile of v8, /device:TPU:9, one launch (start us, length us, event | category | flops | bytes accessed | tf_op | source)
XLA Modules:
  0.0 731.1 jit_solution(11664009198453763052)
XLA Ops:
  57.5 25.2 %shard_map.131 = (f32[4,4,64,512]{3,2,1,0:T(8,128)S(1)}, f32[3,4,256,512]{3,2,1,0:T(8,128)}) custom-call(f32[3,4,256,512]{3,2,1,0:T(8,128)} %bitcast.140, f32[4,256,512]{2,1,0:T(8,128)} %copy-done.8, f32[4,256,512]{2,1,0:T(8,128)} %get-tuple-element.117.code_ref, f32[5,4,8,512]{3,2,1,0:T(8,128)} %pad.50.above_ref, f32[5,4,8,512]{3,2,1,0:T(8,128)} %pad.51.below_ref, ...), custom_call_target="tpu_custom_call" | custom-call | tf_op jit(solution)/shard_map/pallas_call | solution.py:809
  87.6 12.3 %copy.237 = bf16[2048,2048]{0,1:T(8,128)(2,1)} copy(bf16[2048,2048]{1,0:T(8,128)(2,1)} %back_ref.15) | data formatting | bytes 16777216 | tf_op args[6]
  100.0 11.9 %all-to-all-done.1.field_ref = f32[4,4,64,512]{3,2,1,0:T(8,128)S(1)} async-done(((f32[4,4,64,512]{3,2,1,0:T(8,128)}), f32[4,4,64,512]{3,2,1,0:T(8,128)S(1)}, u32[]{:S(2)}, u32[]{:S(2)}) %all-to-all-start.1) | async-done | bytes 2097184 | tf_op jit(solution)/shard_map/all_to_all | solution.py:989
  131.1 18.2 %all-to-all-done.4 = f32[32,64,128]{2,1,0:T(8,128)S(1)} async-done(((f32[32,64,128]{2,1,0:T(8,128)}), f32[32,64,128]{2,1,0:T(8,128)S(1)}, u32[]{:S(2)}, u32[]{:S(2)}) %all-to-all-start.4) | async-done | bytes 1048608 | tf_op jit(solution)/shard_map/all_to_all | solution.py:1015
  166.5 12.7 %all-to-all-done.2 = f32[32,64,128]{2,1,0:T(8,128)S(1)} async-done(((f32[32,64,128]{2,1,0:T(8,128)}), f32[32,64,128]{2,1,0:T(8,128)S(1)}, u32[]{:S(2)}, u32[]{:S(2)}) %all-to-all-start.2) | async-done | bytes 1048608 | tf_op jit(solution)/shard_map/all_to_all | solution.py:1015
  193.9 16.5 %all-to-all-done.5.refs_1_ = f32[32,17,4,128]{3,2,1,0:T(4,128)S(1)} async-done(((f32[32,17,4,128]{3,2,1,0:T(4,128)}), f32[32,17,4,128]{3,2,1,0:T(4,128)S(1)}, u32[]{:S(2)}, u32[]{:S(2)}) %all-to-all-start.5) | async-done | bytes 1114144 | tf_op jit(solution)/shard_map/all_to_all | solution.py:1018
  226.8 15.1 %all-to-all-done.3.refs_1_ = f32[32,17,4,128]{3,2,1,0:T(4,128)S(1)} async-done(((f32[32,17,4,128]{3,2,1,0:T(4,128)}), f32[32,17,4,128]{3,2,1,0:T(4,128)S(1)}, u32[]{:S(2)}, u32[]{:S(2)}) %all-to-all-start.3) | async-done | bytes 1114144 | tf_op jit(solution)/shard_map/all_to_all | solution.py:1018
  241.9 13.1 %shard_map.137 = (f32[4,64,2048]{2,1,0:T(8,128)}, f32[4,8,2048]{2,1,0:T(8,128)}, f32[4,64,2048]{2,1,0:T(8,128)}, f32[4,8,64,128]{3,2,1,0:T(8,128)}) custom-call(f32[4,4]{1,0:T(4,128)S(1)} %copy-done.2, f32[32,17,4,128]{3,2,1,0:T(4,128)S(1)} %all-to-all-done.3.refs_1_, bf16[2048,2048]{1,0:T(8,128)(2,1)} %refs_2_.15, f32[4,64,2048]{2,1,0:T(8,128)} %bitcast.135, ...), custom_call_target="tpu_custom_call" | custom-call | tf_op jit(solution)/shard_map/pallas_call | solution.py:683
  266.7 18.2 %all-to-all-done.8 = f32[32,64,128]{2,1,0:T(8,128)S(1)} async-done(((f32[32,64,128]{2,1,0:T(8,128)}), f32[32,64,128]{2,1,0:T(8,128)S(1)}, u32[]{:S(2)}, u32[]{:S(2)}) %all-to-all-start.8) | async-done | bytes 1048608 | tf_op jit(solution)/shard_map/all_to_all | solution.py:1015
  293.0 10.1 %shard_map.140 = f32[32,17,4,128]{3,2,1,0:T(4,128)} custom-call(f32[2048,128]{1,0:T(8,128)S(1)} %bitcast.115, f32[8,128]{1,0:T(8,128)S(1)} %select_maximum_fusion.4.aux_ref, bf16[2048,2048]{1,0:T(8,128)(2,1)} %bitcast.129, bf16[2048,2048]{1,0:T(8,128)(2,1)} %back_ref.15, f32[2048,1]{1,0:T(8,128)S(1)} %copy.238.along_ref, ...), custom_call_target="tpu_custom_call" | custom-call | tf_op jit(solution)/shard_map/pallas_call | solution.py:457
  303.1 11.7 %all-to-all-done.6 = f32[32,64,128]{2,1,0:T(8,128)S(1)} async-done(((f32[32,64,128]{2,1,0:T(8,128)}), f32[32,64,128]{2,1,0:T(8,128)S(1)}, u32[]{:S(2)}, u32[]{:S(2)}) %all-to-all-start.6) | async-done | bytes 1048608 | tf_op jit(solution)/shard_map/all_to_all | solution.py:1015
  319.4 10.1 %shard_map.139 = f32[32,17,4,128]{3,2,1,0:T(4,128)} custom-call(f32[2048,128]{1,0:T(8,128)S(1)} %bitcast.113, f32[8,128]{1,0:T(8,128)S(1)} %broadcast_2_aux_ref.2.aux_ref, bf16[2048,2048]{1,0:T(8,128)(2,1)} %bitcast.130, bf16[2048,2048]{1,0:T(8,128)(2,1)} %back_ref.15, f32[2048,1]{1,0:T(8,128)S(1)} %copy.238.along_ref, f32[1,128]{1,0:T(1,128)S(1)} %get-tuple-element.126.other_ref), custom_call_target="tpu_custom_call" | custom-call | tf_op jit(solution)/shard_map/pallas_call | solution.py:457
  329.5 16.5 %all-to-all-done.9.refs_1_ = f32[32,17,4,128]{3,2,1,0:T(4,128)S(1)} async-done(((f32[32,17,4,128]{3,2,1,0:T(4,128)}), f32[32,17,4,128]{3,2,1,0:T(4,128)S(1)}, u32[]{:S(2)}, u32[]{:S(2)}) %all-to-all-start.9) | async-done | bytes 1114144 | tf_op jit(solution)/shard_map/all_to_all | solution.py:1018
  362.6 14.7 %all-to-all-done.7.refs_1_ = f32[32,17,4,128]{3,2,1,0:T(4,128)S(1)} async-done(((f32[32,17,4,128]{3,2,1,0:T(4,128)}), f32[32,17,4,128]{3,2,1,0:T(4,128)S(1)}, u32[]{:S(2)}, u32[]{:S(2)}) %all-to-all-start.7) | async-done | bytes 1114144 | tf_op jit(solution)/shard_map/all_to_all | solution.py:1018
  377.3 13.7 %shard_map.142 = (f32[4,64,2048]{2,1,0:T(8,128)}, f32[4,8,2048]{2,1,0:T(8,128)}, f32[4,64,2048]{2,1,0:T(8,128)}, f32[4,64,2048]{2,1,0:T(8,128)}, f32[4,8,2048]{2,1,0:T(8,128)}, /*index=5*/f32[4,8,64,128]{3,2,1,0:T(8,128)}) custom-call(f32[4,4]{1,0:T(4,128)S(1)} %copy-done.2, f32[32,17,4,128]{3,2,1,0:T(4,128)S(1)} %all-to-all-done.7.refs_1_, ...), custom_call_target="tpu_custom_call" | custom-call | tf_op jit(solution)/shard_map/pallas_call | solution.py:683
  403.0 18.1 %all-to-all-done.12 = f32[32,64,128]{2,1,0:T(8,128)S(1)} async-done(((f32[32,64,128]{2,1,0:T(8,128)}), f32[32,64,128]{2,1,0:T(8,128)S(1)}, u32[]{:S(2)}, u32[]{:S(2)}) %all-to-all-start.12) | async-done | bytes 1048608 | tf_op jit(solution)/shard_map/all_to_all | solution.py:1015
  465.7 16.5 %all-to-all-done.13.refs_1_ = f32[32,17,4,128]{3,2,1,0:T(4,128)S(1)} async-done(((f32[32,17,4,128]{3,2,1,0:T(4,128)}), f32[32,17,4,128]{3,2,1,0:T(4,128)S(1)}, u32[]{:S(2)}, u32[]{:S(2)}) %all-to-all-start.13) | async-done | bytes 1114144 | tf_op jit(solution)/shard_map/all_to_all | solution.py:1018
  500.4 13.0 %all-to-all-done.11.refs_1_ = f32[32,17,4,128]{3,2,1,0:T(4,128)S(1)} async-done(((f32[32,17,4,128]{3,2,1,0:T(4,128)}), f32[32,17,4,128]{3,2,1,0:T(4,128)S(1)}, u32[]{:S(2)}, u32[]{:S(2)}) %all-to-all-start.11) | async-done | bytes 1114144 | tf_op jit(solution)/shard_map/all_to_all | solution.py:1018
  513.5 13.7 %shard_map.147 = (f32[4,64,2048]{2,1,0:T(8,128)}, f32[4,8,2048]{2,1,0:T(8,128)}, f32[4,64,2048]{2,1,0:T(8,128)}, f32[4,64,2048]{2,1,0:T(8,128)}, f32[4,8,2048]{2,1,0:T(8,128)}, /*index=5*/f32[4,8,64,128]{3,2,1,0:T(8,128)}) custom-call(f32[4,4]{1,0:T(4,128)S(1)} %copy-done.2, f32[32,17,4,128]{3,2,1,0:T(4,128)S(1)} %all-to-all-done.11.refs_1_, ...), custom_call_target="tpu_custom_call" | custom-call | tf_op jit(solution)/shard_map/pallas_call | solution.py:683
  538.8 18.2 %all-to-all-done.14 = f32[32,64,128]{2,1,0:T(8,128)S(1)} async-done(((f32[32,64,128]{2,1,0:T(8,128)}), f32[32,64,128]{2,1,0:T(8,128)S(1)}, u32[]{:S(2)}, u32[]{:S(2)}) %all-to-all-start.14) | async-done | bytes 1048608 | tf_op jit(solution)/shard_map/all_to_all | solution.py:1015
  601.8 16.5 %all-to-all-done.15.refs_1_ = f32[32,17,4,128]{3,2,1,0:T(4,128)S(1)} async-done(((f32[32,17,4,128]{3,2,1,0:T(4,128)}), f32[32,17,4,128]{3,2,1,0:T(4,128)S(1)}, u32[]{:S(2)}, u32[]{:S(2)}) %all-to-all-start.15) | async-done | bytes 1114144 | tf_op jit(solution)/shard_map/all_to_all | solution.py:1018
  627.1 10.4 %shard_map.151 = (f32[4,64,2048]{2,1,0:T(8,128)}, f32[4,8,2048]{2,1,0:T(8,128)}, f32[4,64,2048]{2,1,0:T(8,128)}, f32[4,8,2048]{2,1,0:T(8,128)}) custom-call(f32[4,4]{1,0:T(4,128)S(1)} %copy-done.2, f32[32,17,4,128]{3,2,1,0:T(4,128)S(1)} %all-to-all-done.15.refs_1_, bf16[2048,2048]{1,0:T(8,128)(2,1)} %refs_2_.15, ...), custom_call_target="tpu_custom_call" | custom-call | tf_op jit(solution)/shard_map/pallas_call | solution.py:352
  649.7 11.5 %shard_map.152 = (f32[4,64,2048]{2,1,0:T(8,128)}, f32[4,8,2048]{2,1,0:T(8,128)}, f32[4,64,2048]{2,1,0:T(8,128)}, f32[8,128]{1,0:T(8,128)S(1)}, f32[4,64,2048]{2,1,0:T(8,128)}, /*index=5*/f32[4,8,2048]{2,1,0:T(8,128)}) custom-call(f32[4,4]{1,0:T(4,128)S(1)} %copy-done.2, f32[32,17,4,128]{3,2,1,0:T(4,128)S(1)} %all-to-all-done.17.refs_1_, ...), custom_call_target="tpu_custom_call" | custom-call | tf_op jit(solution)/shard_map/pallas_call | solution.py:683
  682.6 24.8 %all-to-all-done.19.own_ref.previous_ref.next_ref = f32[4,4,64,512]{3,2,1,0:T(8,128)S(1)} async-done(((f32[4,4,64,512]{3,2,1,0:T(8,128)}), f32[4,4,64,512]{3,2,1,0:T(8,128)S(1)}, u32[]{:S(2)}, u32[]{:S(2)}) %all-to-all-start.19) | async-done | bytes 2097184 | tf_op jit(solution)/shard_map/all_to_all | solution.py:1059
  (180 shorter events, 359.3 us)
Async XLA Ops:
  9.0 31.2 %collective-permute-start = (f32[5,3,4,512]{3,1,2,0:T(4,128)}, f32[5,3,4,512]{3,1,2,0:T(4,128)S(1)}, u32[]{:S(2)}, u32[]{:S(2)}) collective-permute-start(f32[5,3,4,512]{3,1,2,0:T(4,128)} %pad_maximum_fusion), channel_id=1, source_target_pairs={{0,4},{4,8},{8,12},{12,16},{16,20},{20,24},{24,28},{1,5},{5,9},{9,... | collective-permute-start | bytes 368648 | tf_op jit(solution)/shard_map/ppermute | solution.py:832
  12.9 26.2 %collective-permute-start.1 = (f32[5,3,4,512]{3,1,2,0:T(4,128)}, f32[5,3,4,512]{3,1,2,0:T(4,128)}, u32[]{:S(2)}, u32[]{:S(2)}) collective-permute-start(f32[5,3,4,512]{3,1,2,0:T(4,128)} %pad_maximum_fusion.1), channel_id=1, source_target_pairs={{4,0},{8,4},{12,8},{16,12},{20,16},{24,20},{28,24},{5,1},{9,5},{13... | collective-permute-start | bytes 368648 | tf_op jit(solution)/shard_map/ppermute | solution.py:832
  17.5 66.5 %all-to-all-start = ((f32[4,4,64,512]{3,2,1,0:T(8,128)}), f32[4,4,64,512]{3,2,1,0:T(8,128)}, u32[]{:S(2)}, u32[]{:S(2)}) async-start(f32[4,4,64,512]{3,2,1,0:T(8,128)} %bitcast.142), calls=%async_computation | async-start | bytes 4194304 | tf_op jit(solution)/shard_map/all_to_all | solution.py:987
  84.0 27.9 %all-to-all-start.1 = ((f32[4,4,64,512]{3,2,1,0:T(8,128)}), f32[4,4,64,512]{3,2,1,0:T(8,128)S(1)}, u32[]{:S(2)}, u32[]{:S(2)}) async-start(f32[4,4,64,512]{3,2,1,0:T(8,128)} %copy-done.1), calls=%async_computation.1 | async-start | bytes 4194304 | tf_op jit(solution)/shard_map/all_to_all | solution.py:989
  118.4 31.0 %all-to-all-start.4 = ((f32[32,64,128]{2,1,0:T(8,128)}), f32[32,64,128]{2,1,0:T(8,128)S(1)}, u32[]{:S(2)}, u32[]{:S(2)}) async-start(f32[32,64,128]{2,1,0:T(8,128)} %bitcast.150), calls=%async_computation.4 | async-start | bytes 2097152 | tf_op jit(solution)/shard_map/all_to_all | solution.py:1015
  149.4 29.9 %all-to-all-start.2 = ((f32[32,64,128]{2,1,0:T(8,128)}), f32[32,64,128]{2,1,0:T(8,128)S(1)}, u32[]{:S(2)}, u32[]{:S(2)}) async-start(f32[32,64,128]{2,1,0:T(8,128)} %bitcast.143), calls=%async_computation.2 | async-start | bytes 2097152 | tf_op jit(solution)/shard_map/all_to_all | solution.py:1015
  179.2 31.2 %all-to-all-start.5 = ((f32[32,17,4,128]{3,2,1,0:T(4,128)}), f32[32,17,4,128]{3,2,1,0:T(4,128)S(1)}, u32[]{:S(2)}, u32[]{:S(2)}) async-start(f32[32,17,4,128]{3,2,1,0:T(4,128)} %shard_map.135), calls=%async_computation.5 | async-start | bytes 2228224 | tf_op jit(solution)/shard_map/all_to_all | solution.py:1018
  210.5 31.4 %all-to-all-start.3 = ((f32[32,17,4,128]{3,2,1,0:T(4,128)}), f32[32,17,4,128]{3,2,1,0:T(4,128)S(1)}, u32[]{:S(2)}, u32[]{:S(2)}) async-start(f32[32,17,4,128]{3,2,1,0:T(4,128)} %shard_map.134), calls=%async_computation.3 | async-start | bytes 2228224 | tf_op jit(solution)/shard_map/all_to_all | solution.py:1018
  255.0 29.9 %all-to-all-start.8 = ((f32[32,64,128]{2,1,0:T(8,128)}), f32[32,64,128]{2,1,0:T(8,128)S(1)}, u32[]{:S(2)}, u32[]{:S(2)}) async-start(f32[32,64,128]{2,1,0:T(8,128)} %bitcast.149), calls=%async_computation.8 | async-start | bytes 2097152 | tf_op jit(solution)/shard_map/all_to_all | solution.py:1015
  284.9 29.9 %all-to-all-start.6 = ((f32[32,64,128]{2,1,0:T(8,128)}), f32[32,64,128]{2,1,0:T(8,128)S(1)}, u32[]{:S(2)}, u32[]{:S(2)}) async-start(f32[32,64,128]{2,1,0:T(8,128)} %bitcast.144), calls=%async_computation.6 | async-start | bytes 2097152 | tf_op jit(solution)/shard_map/all_to_all | solution.py:1015
  314.8 31.2 %all-to-all-start.9 = ((f32[32,17,4,128]{3,2,1,0:T(4,128)}), f32[32,17,4,128]{3,2,1,0:T(4,128)S(1)}, u32[]{:S(2)}, u32[]{:S(2)}) async-start(f32[32,17,4,128]{3,2,1,0:T(4,128)} %shard_map.140), calls=%async_computation.9 | async-start | bytes 2228224 | tf_op jit(solution)/shard_map/all_to_all | solution.py:1018
  346.1 31.3 %all-to-all-start.7 = ((f32[32,17,4,128]{3,2,1,0:T(4,128)}), f32[32,17,4,128]{3,2,1,0:T(4,128)S(1)}, u32[]{:S(2)}, u32[]{:S(2)}) async-start(f32[32,17,4,128]{3,2,1,0:T(4,128)} %shard_map.139), calls=%async_computation.7 | async-start | bytes 2228224 | tf_op jit(solution)/shard_map/all_to_all | solution.py:1018
  391.0 30.1 %all-to-all-start.12 = ((f32[32,64,128]{2,1,0:T(8,128)}), f32[32,64,128]{2,1,0:T(8,128)S(1)}, u32[]{:S(2)}, u32[]{:S(2)}) async-start(f32[32,64,128]{2,1,0:T(8,128)} %bitcast.147), calls=%async_computation.12 | async-start | bytes 2097152 | tf_op jit(solution)/shard_map/all_to_all | solution.py:1015
  421.1 29.9 %all-to-all-start.10 = ((f32[32,64,128]{2,1,0:T(8,128)}), f32[32,64,128]{2,1,0:T(8,128)S(1)}, u32[]{:S(2)}, u32[]{:S(2)}) async-start(f32[32,64,128]{2,1,0:T(8,128)} %bitcast.146), calls=%async_computation.10 | async-start | bytes 2097152 | tf_op jit(solution)/shard_map/all_to_all | solution.py:1015
  450.9 31.2 %all-to-all-start.13 = ((f32[32,17,4,128]{3,2,1,0:T(4,128)}), f32[32,17,4,128]{3,2,1,0:T(4,128)S(1)}, u32[]{:S(2)}, u32[]{:S(2)}) async-start(f32[32,17,4,128]{3,2,1,0:T(4,128)} %shard_map.145), calls=%async_computation.13 | async-start | bytes 2228224 | tf_op jit(solution)/shard_map/all_to_all | solution.py:1018
  482.2 31.3 %all-to-all-start.11 = ((f32[32,17,4,128]{3,2,1,0:T(4,128)}), f32[32,17,4,128]{3,2,1,0:T(4,128)S(1)}, u32[]{:S(2)}, u32[]{:S(2)}) async-start(f32[32,17,4,128]{3,2,1,0:T(4,128)} %shard_map.144), calls=%async_computation.11 | async-start | bytes 2228224 | tf_op jit(solution)/shard_map/all_to_all | solution.py:1018
  527.1 29.9 %all-to-all-start.14 = ((f32[32,64,128]{2,1,0:T(8,128)}), f32[32,64,128]{2,1,0:T(8,128)S(1)}, u32[]{:S(2)}, u32[]{:S(2)}) async-start(f32[32,64,128]{2,1,0:T(8,128)} %bitcast.148), calls=%async_computation.14 | async-start | bytes 2097152 | tf_op jit(solution)/shard_map/all_to_all | solution.py:1015
  557.0 30.1 %all-to-all-start.16 = ((f32[32,64,128]{2,1,0:T(8,128)}), f32[32,64,128]{2,1,0:T(8,128)S(1)}, u32[]{:S(2)}, u32[]{:S(2)}) async-start(f32[32,64,128]{2,1,0:T(8,128)} %bitcast.145), calls=%async_computation.16 | async-start | bytes 2097152 | tf_op jit(solution)/shard_map/all_to_all | solution.py:1015
  587.1 31.2 %all-to-all-start.15 = ((f32[32,17,4,128]{3,2,1,0:T(4,128)}), f32[32,17,4,128]{3,2,1,0:T(4,128)S(1)}, u32[]{:S(2)}, u32[]{:S(2)}) async-start(f32[32,17,4,128]{3,2,1,0:T(4,128)} %shard_map.148), calls=%async_computation.15 | async-start | bytes 2228224 | tf_op jit(solution)/shard_map/all_to_all | solution.py:1018
  618.4 31.3 %all-to-all-start.17 = ((f32[32,17,4,128]{3,2,1,0:T(4,128)}), f32[32,17,4,128]{3,2,1,0:T(4,128)S(1)}, u32[]{:S(2)}, u32[]{:S(2)}) async-start(f32[32,17,4,128]{3,2,1,0:T(4,128)} %shard_map.150), calls=%async_computation.17 | async-start | bytes 2228224 | tf_op jit(solution)/shard_map/all_to_all | solution.py:1018
  661.9 10.8 %all-to-all-start.18 = ((f32[32,8,128]{2,1,0:T(8,128)}), f32[32,8,128]{2,1,0:T(8,128)S(1)}, u32[]{:S(2)}, u32[]{:S(2)}) async-start(f32[32,8,128]{2,1,0:T(8,128)} %broadcast_in_dim.108), calls=%async_computation.18 | async-start | bytes 262144 | tf_op jit(solution)/shard_map/all_to_all | solution.py:1057
  677.6 29.7 %all-to-all-start.19 = ((f32[4,4,64,512]{3,2,1,0:T(8,128)}), f32[4,4,64,512]{3,2,1,0:T(8,128)S(1)}, u32[]{:S(2)}, u32[]{:S(2)}) async-start(f32[4,4,64,512]{3,2,1,0:T(8,128)} %shard_map.153), calls=%async_computation.19 | async-start | bytes 4194304 | tf_op jit(solution)/shard_map/all_to_all | solution.py:1059
  707.4 15.2 %collective-permute-start.4 = (f32[4,1,512]{2,1,0:T(1,128)S(1)}, f32[4,1,512]{2,1,0:T(1,128)S(1)}, u32[]{:S(2)}, u32[]{:S(2)}) collective-permute-start(f32[4,1,512]{2,1,0:T(1,128)S(1)} %get-tuple-element.108), channel_id=1, source_target_pairs={{0,4},{4,8},{8,12},{12,16},{16,20},{20,24},{24,28},{1,5},{5,9},{9,... | collective-permute-start | bytes 24584 | tf_op jit(solution)/shard_map/ppermute | solution.py:832
  709.7 12.9 %collective-permute-start.5 = (f32[4,1,512]{2,1,0:T(1,128)S(1)}, f32[4,1,512]{2,1,0:T(1,128)S(1)}, u32[]{:S(2)}, u32[]{:S(2)}) collective-permute-start(f32[4,1,512]{2,1,0:T(1,128)S(1)} %get-tuple-element.107), channel_id=1, source_target_pairs={{4,0},{8,4},{12,8},{16,12},{20,16},{24,20},{28,24},{5,1},{9,5},{13... | collective-permute-start | bytes 24584 | tf_op jit(solution)/shard_map/ppermute | solution.py:832
  (22 other events, 197.5 us)
